TPU v7x, 32 devices: a whole 2x2x4 slice. The times are simulated.
32 devices in a mesh: dp: 16 (over z, y, x), tensor: 2 (over core).
Axes of the slice: x: 2, y: 2, z: 4, core: 2. Of those that a mesh axis runs over, the one named last changes fastest.
Arguments:
- layer_input: bfloat16 [8192, 2048], P(('dp', 'tensor')), may hold values from -6 to 6
- upstream: bfloat16 [8192, 2048], P(('dp', 'tensor')), may hold values from -6 to 6
- doc_lengths: int32 [16, 6], P('dp'), may hold values from 1 to 448, 512 in all within a row
- token_valid: int32 [16, 512], P('dp'), may hold values 0 or 1
- query_weight: float32 [2048, 2048], P('dp', 'tensor'), may hold values from -0.125 to 0.125
- query_moment: float32 [2048, 2048], P('dp', 'tensor'), may hold values from -224 to 224
- query_second: float32 [2048, 2048], P('dp', 'tensor'), may hold values from 1310.72 to 5242.88
- query_shadow: float32 [2048, 2048], P('dp', 'tensor'), may hold values from -0.125 to 0.125
- keyval_weight: float32 [2048, 2, 256], P('dp', None, 'tensor'), may hold values from -0.125 to 0.125
- keyval_moment: float32 [2048, 2, 256], P('dp', None, 'tensor'), may hold values from -512 to 512
- keyval_second: float32 [2048, 2, 256], P('dp', None, 'tensor'), may hold values from 8192 to 32768
- keyval_shadow: float32 [2048, 2, 256], P('dp', None, 'tensor'), may hold values from -0.125 to 0.125
- mixing_weight: float32 [2048, 2048], P(('tensor', 'dp')), may hold values from -0.5 to 0.5
- mixing_moment: float32 [2048, 2048], P(('tensor', 'dp')), may hold values from -160 to 160
- mixing_second: float32 [2048, 2048], P(('tensor', 'dp')), may hold values from 737.28 to 2949.12
- mixing_shadow: float32 [2048, 2048], P(('tensor', 'dp')), may hold values from -0.5 to 0.5
- expand_weight: float32 [2048, 2, 5632], P('dp', None, 'tensor'), may hold values from -0.125 to 0.125
- expand_moment: float32 [2048, 2, 5632], P('dp', None, 'tensor'), may hold values from -224 to 224
- expand_second: float32 [2048, 2, 5632], P('dp', None, 'tensor'), may hold values from 1310.72 to 5242.88
- expand_shadow: float32 [2048, 2, 5632], P('dp', None, 'tensor'), may hold values from -0.125 to 0.125
- contract_weight: float32 [5632, 2048], P(('tensor', 'dp')), may hold values from -0.078125 to 0.078125
- contract_moment: float32 [5632, 2048], P(('tensor', 'dp')), may hold values from -256 to 256
- contract_second: float32 [5632, 2048], P(('tensor', 'dp')), may hold values from 2048 to 8192
- contract_shadow: float32 [5632, 2048], P(('tensor', 'dp')), may hold values from -0.078125 to 0.078125
- norms_weight: float32 [2, 2048], P(None, ('dp', 'tensor')), may hold values from 0.5 to 1.5
- norms_moment: float32 [2, 2048], P(None, ('dp', 'tensor')), may hold values from -256 to 256
- norms_second: float32 [2, 2048], P(None, ('dp', 'tensor')), may hold values from 2048 to 8192
- norms_shadow: float32 [2, 2048], P(None, ('dp', 'tensor')), may hold values from 0.5 to 1.5
Outputs:
- layer_output: bfloat16 [8192, 2048], P(('dp', 'tensor'))
- input_grad: float32 [8192, 2048], P(('dp', 'tensor'))
- query_master: float32 [2048, 2048], P('dp', 'tensor')
- query_momentum: float32 [2048, 2048], P('dp', 'tensor')
- query_variance: float32 [2048, 2048], P('dp', 'tensor')
- query_average: float32 [2048, 2048], P('dp', 'tensor')
- keyval_master: float32 [2048, 2, 256], P('dp', None, 'tensor')
- keyval_momentum: float32 [2048, 2, 256], P('dp', None, 'tensor')
- keyval_variance: float32 [2048, 2, 256], P('dp', None, 'tensor')
- keyval_average: float32 [2048, 2, 256], P('dp', None, 'tensor')
- mixing_master: float32 [2048, 2048], P(('tensor', 'dp'))
- mixing_momentum: float32 [2048, 2048], P(('tensor', 'dp'))
- mixing_variance: float32 [2048, 2048], P(('tensor', 'dp'))
- mixing_average: float32 [2048, 2048], P(('tensor', 'dp'))
- expand_master: float32 [2048, 2, 5632], P('dp', None, 'tensor')
- expand_momentum: float32 [2048, 2, 5632], P('dp', None, 'tensor')
- expand_variance: float32 [2048, 2, 5632], P('dp', None, 'tensor')
- expand_average: float32 [2048, 2, 5632], P('dp', None, 'tensor')
- contract_master: float32 [5632, 2048], P(('tensor', 'dp'))
- contract_momentum: float32 [5632, 2048], P(('tensor', 'dp'))
- contract_variance: float32 [5632, 2048], P(('tensor', 'dp'))
- contract_average: float32 [5632, 2048], P(('tensor', 'dp'))
- norms_master: float32 [2, 2048], P(None, ('dp', 'tensor'))
- norms_momentum: float32 [2, 2048], P(None, ('dp', 'tensor'))
- norms_variance: float32 [2, 2048], P(None, ('dp', 'tensor'))
- norms_average: float32 [2, 2048], P(None, ('dp', 'tensor'))
Inputs may be any that keep to these rules, and one draw needn't show every extreme that they name: `doc_lengths`: each row sums to 512; its longest document has exactly 448 tokens.
All inputs are finite; a program needn't handle non-finite values. No bound on the sum of `token_valid` on one device may be relied on, other than what follows from the above.
Results may differ from a plain program's by a relative error of at most 0.015.
Values may be sent and summed in bfloat16 or wider, within the bound.
No kernel may reach another device: no remote copies, remote signals or barrier semaphores. Data moves between devices by JAX's collectives and lax.ppermute only.
A program may use at most 320 MiB of HBM per device.

v0:
```python
import jax
import jax.numpy as jnp
from jax import lax
from jax.sharding import PartitionSpec as P

HEAD_DIM = 64
STEP = 5


NORM_EPS = 1e-05
NEG_FILL = -1e30
ROPE_BASE = 10000.0
BETA_ONE = 0.5
BETA_TWO = 0.5
ADAM_EPS = 1e-08
WEIGHT_DECAY = 0.1
MATRIX_RATE = 0.02
GAIN_RATE = 0.2
EMA_KEEP = 0.9
GAIN_KEEP = 0.5
CONTRACT_LAST = (((1,), (1,)), ((), ()))
CONTRACT_FIRST = (((0,), (0,)), ((), ()))


def normalize(field_rows, gain_row):
    factor = lax.rsqrt(jnp.mean(field_rows * field_rows, axis=-1, keepdims=True) + NORM_EPS)
    return field_rows * factor * gain_row


def rotate(field, cosine_table, sine_table):
    half_dim = field.shape[-1] // 2
    first_half = field[..., :half_dim]
    second_half = field[..., half_dim:]
    return jnp.concatenate(
        [
            first_half * cosine_table - second_half * sine_table,
            second_half * cosine_table + first_half * sine_table,
        ],
        axis=-1,
    )


def layout(lengths, valid_keys):
    group_len = valid_keys.shape[0]
    places = jnp.arange(group_len, dtype=jnp.int32)
    doc_ends = jnp.cumsum(lengths)
    doc_starts = doc_ends - lengths
    segment = jnp.sum((doc_ends[None, :] <= places[:, None]).astype(jnp.int32), axis=1)
    owned_doc = segment[:, None] == jnp.arange(lengths.shape[0], dtype=jnp.int32)[None, :]
    position = places - jnp.sum(jnp.where(owned_doc, doc_starts[None, :], 0), axis=1)
    allowed = (
        (segment[:, None] == segment[None, :])
        & (places[None, :] <= places[:, None])
        & ((valid_keys[None, :] == 1) | (places[:, None] == places[None, :]))
    )
    return (position, allowed)


def rope_tables(position, head_size):
    half_dim = head_size // 2
    inverse = ROPE_BASE ** (-(2.0 * jnp.arange(half_dim, dtype=jnp.float32)) / head_size)
    angles = position.astype(jnp.float32)[:, None] * inverse[None, :]
    return (jnp.cos(angles)[:, None, :], jnp.sin(angles)[:, None, :])


def adamw(grad_value, weight, moment, second, shadow, step_rate, decay_rate, keep_rate):
    moment_new = BETA_ONE * moment + (1.0 - BETA_ONE) * grad_value
    second_new = BETA_TWO * second + (1.0 - BETA_TWO) * grad_value * grad_value
    moment_hat = moment_new / (1.0 - BETA_ONE**STEP)
    second_hat = second_new / (1.0 - BETA_TWO**STEP)
    weight_new = weight - step_rate * (
        moment_hat / (jnp.sqrt(second_hat) + ADAM_EPS) + decay_rate * weight
    )
    shadow_new = keep_rate * shadow + (1.0 - keep_rate) * weight_new
    return (weight_new, moment_new, second_new, shadow_new)


def gather_rows(row_block):
    return lax.all_gather(row_block, "tensor", axis=0, tiled=True)


def scatter_rows(row_block):
    return lax.psum_scatter(row_block, "tensor", scatter_dimension=0, tiled=True)


def per_device(
    layer_input,
    upstream,
    doc_lengths,
    token_valid,
    query_weight,
    query_moment,
    query_second,
    query_shadow,
    keyval_weight,
    keyval_moment,
    keyval_second,
    keyval_shadow,
    mixing_weight,
    mixing_moment,
    mixing_second,
    mixing_shadow,
    expand_weight,
    expand_moment,
    expand_second,
    expand_shadow,
    contract_weight,
    contract_moment,
    contract_second,
    contract_shadow,
    norms_weight,
    norms_moment,
    norms_second,
    norms_shadow,
):
    bf_type = jnp.bfloat16
    fl_type = jnp.float32
    query_low, keyval_low, mixing_low, expand_low, contract_low = (
        lax.all_gather(query_weight.astype(bf_type), "dp", axis=0, tiled=True),
        lax.all_gather(keyval_weight.astype(bf_type), "dp", axis=0, tiled=True),
        lax.all_gather(mixing_weight.astype(bf_type), "dp", axis=0, tiled=True),
        lax.all_gather(expand_weight.astype(bf_type), "dp", axis=0, tiled=True),
        lax.all_gather(contract_weight.astype(bf_type), "dp", axis=0, tiled=True),
    )
    gain_rows = lax.all_gather(norms_weight, ("dp", "tensor"), axis=1, tiled=True)
    input_rows = layer_input.astype(fl_type)
    position, allowed = layout(doc_lengths[0], token_valid[0])
    cosine_table, sine_table = rope_tables(position, HEAD_DIM)
    group_len = position.shape[0]
    head_count = query_low.shape[1] // HEAD_DIM
    kv_count = keyval_low.shape[2] // HEAD_DIM
    group_ratio = head_count // kv_count
    factor = HEAD_DIM ** (-0.5)
    normed = normalize(input_rows, gain_rows[0]).astype(bf_type)
    normed_all = gather_rows(normed)
    query_pre = jnp.dot(normed_all, query_low, preferred_element_type=fl_type).reshape(
        group_len, head_count, HEAD_DIM
    )
    keyval_pre = jnp.einsum("gd,dsc->gsc", normed_all, keyval_low, preferred_element_type=fl_type)
    queries = rotate(query_pre, cosine_table, sine_table).astype(bf_type)
    keys = rotate(
        keyval_pre[:, 0].reshape(group_len, kv_count, HEAD_DIM), cosine_table, sine_table
    ).astype(bf_type)
    values = keyval_pre[:, 1].reshape(group_len, kv_count, HEAD_DIM).astype(bf_type)

    def head_scores(kv_index):
        query_block = queries[:, kv_index * group_ratio : (kv_index + 1) * group_ratio]
        raw_scores = (
            jnp.einsum(
                "gre,ke->rgk", query_block, keys[:, kv_index], preferred_element_type=fl_type
            )
            * factor
        )
        return (query_block, jnp.where(allowed[None], raw_scores, NEG_FILL))

    mixed_parts = []
    log_totals = []
    for kv_index in range(kv_count):
        query_block, masked = head_scores(kv_index)
        largest = jnp.max(masked, axis=-1, keepdims=True)
        exp_scores = jnp.exp(masked - largest)
        totals = jnp.sum(exp_scores, axis=-1, keepdims=True)
        soft_probs = (exp_scores / totals).astype(bf_type)
        log_totals.append(largest + jnp.log(totals))
        mixed_parts.append(
            jnp.einsum(
                "rgk,ke->gre", soft_probs, values[:, kv_index], preferred_element_type=fl_type
            )
        )
    mixed = (
        jnp.concatenate(mixed_parts, axis=1)
        .reshape(group_len, head_count * HEAD_DIM)
        .astype(bf_type)
    )
    attended = scatter_rows(jnp.dot(mixed, mixing_low, preferred_element_type=fl_type))
    middle = input_rows + attended
    normed_two = normalize(middle, gain_rows[1]).astype(bf_type)
    normed_two_all = gather_rows(normed_two)
    gate_up = jnp.einsum("gd,dsf->gsf", normed_two_all, expand_low, preferred_element_type=fl_type)
    gate_sig = jax.nn.sigmoid(gate_up[:, 0])
    gate_act = gate_up[:, 0] * gate_sig
    hidden = (gate_act * gate_up[:, 1]).astype(bf_type)
    branch = scatter_rows(jnp.dot(hidden, contract_low, preferred_element_type=fl_type))
    layer_output = (middle + branch).astype(bf_type)
    out_grad = upstream.astype(fl_type)
    out_grad_all = gather_rows(upstream)
    hidden_grad = lax.dot_general(
        out_grad_all, contract_low, CONTRACT_LAST, preferred_element_type=fl_type
    )
    gate_grad = hidden_grad * gate_up[:, 1] * gate_sig * (1.0 + gate_up[:, 0] * (1.0 - gate_sig))
    up_grad = hidden_grad * gate_act
    gate_up_grad = jnp.stack([gate_grad, up_grad], axis=1).astype(bf_type)
    contract_full = lax.dot_general(
        hidden, out_grad_all, CONTRACT_FIRST, preferred_element_type=fl_type
    )
    expand_full = jnp.einsum(
        "gd,gsf->dsf", normed_two_all, gate_up_grad, preferred_element_type=fl_type
    )
    normed_two_grad = scatter_rows(
        jnp.einsum("gsf,dsf->gd", gate_up_grad, expand_low, preferred_element_type=fl_type)
    )
    middle_pull = jax.vjp(normalize, middle, gain_rows[1])[1]
    middle_part, gain_two_grad = middle_pull(normed_two_grad)
    middle_grad = out_grad + middle_part
    attended_all = gather_rows(middle_grad.astype(bf_type))
    mixing_full = lax.dot_general(
        mixed, attended_all, CONTRACT_FIRST, preferred_element_type=fl_type
    )
    mixed_grad = (
        lax.dot_general(attended_all, mixing_low, CONTRACT_LAST, preferred_element_type=fl_type)
        .astype(bf_type)
        .reshape(group_len, head_count, HEAD_DIM)
    )
    query_grads = []
    key_grads = []
    value_grads = []
    for kv_index in range(kv_count):
        query_block, masked = head_scores(kv_index)
        soft_exact = jnp.exp(masked - log_totals[kv_index])
        out_block = mixed_grad[:, kv_index * group_ratio : (kv_index + 1) * group_ratio]
        prob_grad = jnp.einsum(
            "gre,ke->rgk", out_block, values[:, kv_index], preferred_element_type=fl_type
        )
        inner_sum = jnp.sum(prob_grad * soft_exact, axis=-1, keepdims=True)
        score_grad = (soft_exact * (prob_grad - inner_sum)).astype(bf_type)
        query_grads.append(
            jnp.einsum("rgk,ke->gre", score_grad, keys[:, kv_index], preferred_element_type=fl_type)
            * factor
        )
        key_grads.append(
            jnp.einsum("rgk,gre->ke", score_grad, query_block, preferred_element_type=fl_type)
            * factor
        )
        value_grads.append(
            jnp.einsum(
                "rgk,gre->ke", soft_exact.astype(bf_type), out_block, preferred_element_type=fl_type
            )
        )
    query_back = (
        rotate(jnp.concatenate(query_grads, axis=1), cosine_table, -sine_table)
        .astype(bf_type)
        .reshape(group_len, head_count * HEAD_DIM)
    )
    key_back = rotate(jnp.stack(key_grads, axis=1), cosine_table, -sine_table).reshape(
        group_len, kv_count * HEAD_DIM
    )
    value_back = jnp.stack(value_grads, axis=1).reshape(group_len, kv_count * HEAD_DIM)
    keyval_back = jnp.stack([key_back, value_back], axis=1).astype(bf_type)
    query_full = lax.dot_general(
        normed_all, query_back, CONTRACT_FIRST, preferred_element_type=fl_type
    )
    keyval_full = jnp.einsum("gd,gsc->dsc", normed_all, keyval_back, preferred_element_type=fl_type)
    query_grad, keyval_grad, mixing_grad, expand_grad, contract_grad = (
        lax.psum_scatter(query_full, "dp", scatter_dimension=0, tiled=True),
        lax.psum_scatter(keyval_full, "dp", scatter_dimension=0, tiled=True),
        lax.psum_scatter(mixing_full, "dp", scatter_dimension=0, tiled=True),
        lax.psum_scatter(expand_full, "dp", scatter_dimension=0, tiled=True),
        lax.psum_scatter(contract_full, "dp", scatter_dimension=0, tiled=True),
    )
    normed_grad = scatter_rows(
        lax.dot_general(query_back, query_low, CONTRACT_LAST, preferred_element_type=fl_type)
        + jnp.einsum("gsc,dsc->gd", keyval_back, keyval_low, preferred_element_type=fl_type)
    )
    rows_pull = jax.vjp(normalize, input_rows, gain_rows[0])[1]
    rows_part, gain_one_grad = rows_pull(normed_grad)
    input_grad = middle_grad + rows_part
    gain_sums = lax.psum_scatter(
        jnp.stack([gain_one_grad, gain_two_grad]), ("dp", "tensor"), scatter_dimension=1, tiled=True
    )
    query_master, query_momentum, query_variance, query_average = adamw(
        query_grad,
        query_weight,
        query_moment,
        query_second,
        query_shadow,
        MATRIX_RATE,
        WEIGHT_DECAY,
        EMA_KEEP,
    )
    keyval_master, keyval_momentum, keyval_variance, keyval_average = adamw(
        keyval_grad,
        keyval_weight,
        keyval_moment,
        keyval_second,
        keyval_shadow,
        MATRIX_RATE,
        WEIGHT_DECAY,
        EMA_KEEP,
    )
    mixing_master, mixing_momentum, mixing_variance, mixing_average = adamw(
        mixing_grad,
        mixing_weight,
        mixing_moment,
        mixing_second,
        mixing_shadow,
        MATRIX_RATE,
        WEIGHT_DECAY,
        EMA_KEEP,
    )
    expand_master, expand_momentum, expand_variance, expand_average = adamw(
        expand_grad,
        expand_weight,
        expand_moment,
        expand_second,
        expand_shadow,
        MATRIX_RATE,
        WEIGHT_DECAY,
        EMA_KEEP,
    )
    contract_master, contract_momentum, contract_variance, contract_average = adamw(
        contract_grad,
        contract_weight,
        contract_moment,
        contract_second,
        contract_shadow,
        MATRIX_RATE,
        WEIGHT_DECAY,
        EMA_KEEP,
    )
    norms_master, norms_momentum, norms_variance, norms_average = adamw(
        gain_sums, norms_weight, norms_moment, norms_second, norms_shadow, GAIN_RATE, 0.0, GAIN_KEEP
    )
    return (
        layer_output,
        input_grad,
        query_master,
        query_momentum,
        query_variance,
        query_average,
        keyval_master,
        keyval_momentum,
        keyval_variance,
        keyval_average,
        mixing_master,
        mixing_momentum,
        mixing_variance,
        mixing_average,
        expand_master,
        expand_momentum,
        expand_variance,
        expand_average,
        contract_master,
        contract_momentum,
        contract_variance,
        contract_average,
        norms_master,
        norms_momentum,
        norms_variance,
        norms_average,
    )


def solution(mesh):
    in_specs = (
        P(("dp", "tensor"), None),
        P(("dp", "tensor"), None),
        P("dp", None),
        P("dp", None),
        P("dp", "tensor"),
        P("dp", "tensor"),
        P("dp", "tensor"),
        P("dp", "tensor"),
        P("dp", None, "tensor"),
        P("dp", None, "tensor"),
        P("dp", None, "tensor"),
        P("dp", None, "tensor"),
        P(("tensor", "dp"), None),
        P(("tensor", "dp"), None),
        P(("tensor", "dp"), None),
        P(("tensor", "dp"), None),
        P("dp", None, "tensor"),
        P("dp", None, "tensor"),
        P("dp", None, "tensor"),
        P("dp", None, "tensor"),
        P(("tensor", "dp"), None),
        P(("tensor", "dp"), None),
        P(("tensor", "dp"), None),
        P(("tensor", "dp"), None),
        P(None, ("dp", "tensor")),
        P(None, ("dp", "tensor")),
        P(None, ("dp", "tensor")),
        P(None, ("dp", "tensor")),
    )
    out_specs = (
        P(("dp", "tensor"), None),
        P(("dp", "tensor"), None),
        P("dp", "tensor"),
        P("dp", "tensor"),
        P("dp", "tensor"),
        P("dp", "tensor"),
        P("dp", None, "tensor"),
        P("dp", None, "tensor"),
        P("dp", None, "tensor"),
        P("dp", None, "tensor"),
        P(("tensor", "dp"), None),
        P(("tensor", "dp"), None),
        P(("tensor", "dp"), None),
        P(("tensor", "dp"), None),
        P("dp", None, "tensor"),
        P("dp", None, "tensor"),
        P("dp", None, "tensor"),
        P("dp", None, "tensor"),
        P(("tensor", "dp"), None),
        P(("tensor", "dp"), None),
        P(("tensor", "dp"), None),
        P(("tensor", "dp"), None),
        P(None, ("dp", "tensor")),
        P(None, ("dp", "tensor")),
        P(None, ("dp", "tensor")),
        P(None, ("dp", "tensor")),
    )
    return jax.shard_map(
        per_device, mesh=mesh, in_specs=in_specs, out_specs=out_specs, check_vma=False
    )
```

profile of v0, /device:TPU:0, one launch (start us, length us, event | category | flops | bytes accessed | tf_op | source)
XLA Modules:
  0.0 2857.5 jit_solution(3818868732070125591)
XLA Ops:
  7.3 1.7 copy.164
  9.1 43.6 %all-gather = f32[32,64,2]{1,2,0:T(2,128)S(1)} all-gather(f32[1,64,2]{1,2,0:T(2,128)} %bitcast.219), channel_id=1, replica_groups=mesh['dp'=16,'tensor'=2] {'dp','tensor'}, dimensions={0}, use_global_device_ids=true | all-gather | bytes 16896 | tf_op jit(solution)/shard_map/all_gather | solution.py:125
  54.9 2.5 fusion.28
  60.7 5.0 all-gather.13.cloned.1.call-done
  65.7 12.0 all-gather.11.cloned.1.call-done
  77.7 2.8 fusion.115
  80.6 77.8 %all-gather.15.cloned.1.call-done = bf16[2048,1024]{1,0:T(8,128)(2,1)} async-done(((bf16[128,1024]{1,0:T(8,128)(2,1)}), bf16[2048,1024]{1,0:T(8,128)(2,1)}) %all-gather.15.cloned.1.call-update) | async-done | bytes 4194320 | tf_op jit(solution)/shard_map/all_gather | solution.py:119
  158.3 4.6 fusion.116
  169.0 1.6 fusion.45
  170.8 1.6 fusion.44
  172.4 8.6 pad_maximum_fusion.6
  181.0 55.2 %all-gather.17.cloned.1.call-done = bf16[1024,2048]{1,0:T(8,128)(2,1)} async-done(((bf16[64,2048]{1,0:T(8,128)(2,1)}), bf16[1024,2048]{1,0:T(8,128)(2,1)}) %all-gather.17.cloned.1.call-update) | async-done | bytes 4194320 | tf_op jit(solution)/shard_map/all_gather | solution.py:121
  236.3 6.5 fusion.117
  242.9 10.7 reduce-scatter.13.cloned.1.call-done
  253.6 1.9 multiply_reduce_fusion.2
  256.9 3.1 copy.236
  260.8 2.3 convert_element_type.98
  263.1 5.7 all-gather.19.cloned.1.call-done
  268.8 256.2 %all-gather.21.cloned.1.call-done = bf16[2048,2,2816]{2,0,1:T(8,128)(2,1)} async-done(((bf16[128,2,2816]{2,0,1:T(8,128)(2,1)}), bf16[2048,2,2816]{2,0,1:T(8,128)(2,1)}) %all-gather.21.cloned.1.call-update) | async-done | bytes 23068688 | tf_op jit(solution)/shard_map/all_gather | solution.py:122
  525.1 19.6 fusion.37
  544.6 137.9 %all-gather.23.cloned.1.call-done = bf16[2816,2048]{1,0:T(8,128)(2,1)} async-done(((bf16[176,2048]{1,0:T(8,128)(2,1)}), bf16[2816,2048]{1,0:T(8,128)(2,1)}) %all-gather.23.cloned.1.call-update) | async-done | bytes 11534352 | tf_op jit(solution)/shard_map/all_gather | solution.py:123
  682.5 16.5 fusion.25
  699.0 19.9 fusion.21
  719.0 10.3 reduce-scatter.17.cloned.1.call-done
  729.3 2.3 multiply_reduce_fusion
  731.8 1.7 fusion.105
  734.4 11.3 all-gather.27.cloned.1.call-done
  745.6 6.2 convolution_convert_fusion
  751.8 2.7 copy.169
  754.4 5.0 fusion.65
  759.5 8.4 fusion
  767.9 4.6 fusion.2
  772.5 2.0 fusion.53
  774.6 1.8 fusion.40
  777.8 1.6 fusion.3
  779.4 2.7 fusion.5
  782.2 2.0 fusion.55
  784.2 1.8 fusion.41
  789.0 2.5 subtract_convert_fusion
  792.1 2.4 fusion.119
  794.5 2.7 bitcast_add_fusion
  797.3 3.7 fusion.34
  801.0 11.4 fusion.118
  813.0 2.3 fusion.29
  816.8 7.6 fusion.120
  824.8 7.7 fusion.121
  832.6 13.2 fusion.122
  845.8 24.0 fusion.19
  869.9 25.4 reduce-scatter.23.cloned.1.call-done
  899.6 7.2 reduce-scatter.15.cloned.1.call-done
  906.8 5.9 fusion.31
  912.7 133.3 %reduce-scatter.31.cloned.1.call-done = f32[64,2]{1,0:T(8,128)} async-done(((f32[2048,2]{1,0:T(8,128)}), f32[64,2]{1,0:T(8,128)}) %reduce-scatter.31.cloned.1.call-update) | async-done | bytes 528
  1047.4 174.6 %reduce-scatter.21.cloned.1.call-done = f32[128,1024]{1,0:T(8,128)} async-done(((f32[2048,1024]{1,0:T(8,128)}), f32[128,1024]{1,0:T(8,128)}) %reduce-scatter.21.cloned.1.call-update) | async-done | bytes 524304 | tf_op jit(solution)/shard_map/reduce_scatter | solution.py:254
  1222.0 3.3 multiply_add_fusion.6
  1225.4 179.2 %reduce-scatter.25.cloned.1.call-done = f32[64,2048]{1,0:T(8,128)} async-done(((f32[1024,2048]{1,0:T(8,128)}), f32[64,2048]{1,0:T(8,128)}) %reduce-scatter.25.cloned.1.call-update) | async-done | bytes 524304 | tf_op jit(solution)/shard_map/reduce_scatter | solution.py:256
  1404.5 2.7 multiply_add_fusion.5
  1407.2 475.0 %reduce-scatter.29.cloned.1.call-done = f32[176,2048]{1,0:T(8,128)} async-done(((f32[2816,2048]{1,0:T(8,128)}), f32[176,2048]{1,0:T(8,128)}) %reduce-scatter.29.cloned.1.call-update) | async-done | bytes 1441808 | tf_op jit(solution)/shard_map/reduce_scatter | solution.py:258
  1882.2 6.7 multiply_add_fusion.2
  1888.9 940.8 %reduce-scatter.27.cloned.1.call-done = f32[128,2,2816]{2,0,1:T(8,128)} async-done(((f32[2048,2,2816]{2,0,1:T(8,128)}), f32[128,2,2816]{2,0,1:T(8,128)}) %reduce-scatter.27.cloned.1.call-update) | async-done | bytes 2883600 | tf_op jit(solution)/shard_map/reduce_scatter | solution.py:257
  2829.7 5.9 fusion.24
  2835.6 3.8 copy.198
  2839.4 3.8 copy.195
  2843.2 3.8 copy.196
  2847.0 3.8 copy.197
  (180 shorter events, 28.6 us)
Async XLA Ops:
  7.2 50.3 %copy-start.12 = (f32[128,1024]{1,0:T(8,128)S(1)}, f32[128,1024]{1,0:T(8,128)}, u32[]{:S(2)}) copy-start(f32[128,1024]{1,0:T(8,128)} %param.32) | copy-start | bytes 1572868
  7.2 51.1 %copy-start.13 = (f32[64,2048]{1,0:T(8,128)S(1)}, f32[64,2048]{1,0:T(8,128)}, u32[]{:S(2)}) copy-start(f32[64,2048]{1,0:T(8,128)} %param.40) | copy-start | bytes 1572868
  7.2 58.5 %all-gather.13.cloned.1.call-start = ((), (), s32[]{:S(2)}) async-start(), calls=%async_computation.11 | async-start | bytes 1114112 | tf_op jit(solution)/shard_map/all_gather | solution.py:120
  9.0 68.7 %all-gather.11.cloned.1.call-start = ((), (), s32[]{:S(2)}) async-start(), calls=%async_computation.10 | async-start | bytes 3145728 | tf_op jit(solution)/shard_map/all_gather | solution.py:79
  54.3 4.8 copy-start.41
  54.3 5.0 copy-start.36
  54.9 4.7 copy-start.29
  54.9 10.8 copy-start.23
  57.4 100.9 %all-gather.15.cloned.1.call-start = ((), (), s32[]{:S(2)}) async-start(), calls=%async_computation.12 | async-start | bytes 4456448 | tf_op jit(solution)/shard_map/all_gather | solution.py:119
  58.2 178.0 %all-gather.17.cloned.1.call-start = ((), (), s32[]{:S(2)}) async-start(), calls=%async_computation.13 | async-start | bytes 4456448 | tf_op jit(solution)/shard_map/all_gather | solution.py:121
  59.0 194.6 %reduce-scatter.13.cloned.1.call-start = ((), (), s32[]{:S(2)}) async-start(), calls=%async_computation.14 | async-start | bytes 6291456 | tf_op jit(solution)/shard_map/reduce_scatter | solution.py:83
  77.7 80.6 %copy-start.15 = (bf16[512,2048]{1,0:T(8,128)(2,1)S(1)}, bf16[512,2048]{1,0:T(8,128)(2,1)}, u32[]{:S(2)}) copy-start(bf16[512,2048]{1,0:T(8,128)(2,1)} %all-gather.11.cloned.1.call-done) | copy-start | bytes 6291460
  163.3 1.5 copy-start.7
  163.3 1.5 copy-start.9
  164.8 3.9 copy-start
  166.2 4.6 copy-start.1
  167.4 1.6 copy-start.26
  181.0 55.3 %copy-start.11 = (bf16[512,16,64]{0,2,1:T(8,128)(2,1)}, bf16[512,16,64]{0,2,1:T(8,128)(2,1)S(1)}, u32[]{:S(2)}) copy-start(bf16[512,16,64]{0,2,1:T(8,128)(2,1)S(1)} %pad_maximum_fusion.6) | copy-start | bytes 3145732
  242.8 10.8 copy-start.2
  242.8 26.0 all-gather.19.cloned.1.call-start
  255.6 476.0 %copy-start.27 = (f32[256]{0:T(256)}, f32[256]{0:T(256)S(1)}, u32[]{:S(2)}) copy-start(f32[256]{0:T(256)S(1)} %fusion.92) | copy-start | bytes 3076
  256.8 268.3 %all-gather.21.cloned.1.call-start = ((), (), s32[]{:S(2)}) async-start(), calls=%async_computation.16 | async-start | bytes 24510464 | tf_op jit(solution)/shard_map/all_gather | solution.py:122
  260.0 284.7 %all-gather.25.cloned.1.call-start = ((), (), s32[]{:S(2)}) async-start(), calls=%async_computation.19 | async-start | bytes 3145728 | tf_op jit(solution)/shard_map/all_gather | solution.py:79
  260.7 421.8 %all-gather.23.cloned.1.call-start = ((), (), s32[]{:S(2)}) async-start(), calls=%async_computation.17 | async-start | bytes 12255232 | tf_op jit(solution)/shard_map/all_gather | solution.py:123
  263.1 466.2 %reduce-scatter.17.cloned.1.call-start = ((), (), s32[]{:S(2)}) async-start(), calls=%async_computation.20 | async-start | bytes 6291456 | tf_op jit(solution)/shard_map/reduce_scatter | solution.py:83
  718.9 26.7 all-gather.27.cloned.1.call-start
  729.3 2.3 copy-start.3
  729.3 2.5 copy-start.6
  731.8 1.7 copy-start.31
  733.6 78.9 %reduce-scatter.19.cloned.1.call-start = ((), (), s32[]{:S(2)}) async-start(), calls=%async_computation.22 | async-start | bytes 6291456 | tf_op jit(solution)/shard_map/reduce_scatter | solution.py:83
  754.4 5.0 copy-start.5
  754.4 13.4 slice-start
  759.4 8.4 slice-start.1
  759.4 17.0 slice-start.2
  767.9 4.7 copy-start.8
  767.9 4.7 copy-start.10
  767.9 8.5 slice-start.3
  784.2 2.0 copy-start.18
  789.0 3.1 copy-start.40
  791.5 3.0 copy-start.17
  792.1 2.4 copy-start.16
  797.2 98.2 %reduce-scatter.23.cloned.1.call-start = ((), (), s32[]{:S(2)}) async-start(), calls=%async_computation.24 | async-start | bytes 2228224 | tf_op jit(solution)/shard_map/reduce_scatter | solution.py:255
  800.9 105.9 %reduce-scatter.15.cloned.1.call-start = ((), (), s32[]{:S(2)}) async-start(), calls=%async_computation.18 | async-start | bytes 6291456 | tf_op jit(solution)/shard_map/reduce_scatter | solution.py:83
  812.3 0.7 copy-start.24
  812.3 0.7 copy-start.30
  812.4 233.6 %reduce-scatter.31.cloned.1.call-start = ((), (), s32[]{:S(2)}) async-start(), calls=%async_computation.28 | async-start | bytes 1081344
  816.7 405.3 %reduce-scatter.21.cloned.1.call-start = ((), (), s32[]{:S(2)}) async-start(), calls=%async_computation.23 | async-start | bytes 8912896 | tf_op jit(solution)/shard_map/reduce_scatter | solution.py:254
  824.4 580.1 %reduce-scatter.25.cloned.1.call-start = ((), (), s32[]{:S(2)}) async-start(), calls=%async_computation.25 | async-start | bytes 8912896 | tf_op jit(solution)/shard_map/reduce_scatter | solution.py:256
  832.5 1049.7 %reduce-scatter.29.cloned.1.call-start = ((), (), s32[]{:S(2)}) async-start(), calls=%async_computation.27 | async-start | bytes 24510464 | tf_op jit(solution)/shard_map/reduce_scatter | solution.py:258
  845.8 1983.9 %reduce-scatter.27.cloned.1.call-start = ((), (), s32[]{:S(2)}) async-start(), calls=%async_computation.26 | async-start | bytes 49020928 | tf_op jit(solution)/shard_map/reduce_scatter | solution.py:257
  869.9 25.5 copy-start.22
  869.9 25.5 copy-start.25
  869.9 29.7 %copy-start.34 = (f32[256]{0:T(256)S(1)}, f32[256]{0:T(256)}, u32[]{:S(2)}) copy-start(f32[256]{0:T(256)} %copy-done.33) | copy-start | bytes 3076
  869.9 36.9 %copy-start.28 = (f32[256]{0:T(256)S(1)}, f32[256]{0:T(256)}, u32[]{:S(2)}) copy-start(f32[256]{0:T(256)} %copy-done.27) | copy-start | bytes 3076
  869.9 36.9 %copy-start.32 = (f32[256]{0:T(256)S(1)}, f32[256]{0:T(256)}, u32[]{:S(2)}) copy-start(f32[256]{0:T(256)} %copy-done.31) | copy-start | bytes 3076
  899.6 147.2 %copy-start.35 = (f32[2,64]{1,0:T(2,128)S(1)}, f32[2,64]{1,0:T(2,128)}, u32[]{:S(2)}) copy-start(f32[2,64]{1,0:T(2,128)} %param.52) | copy-start | bytes 1540
  899.6 147.2 %copy-start.37 = (f32[2,64]{1,0:T(2,128)S(1)}, f32[2,64]{1,0:T(2,128)}, u32[]{:S(2)}) copy-start(f32[2,64]{1,0:T(2,128)} %param.55) | copy-start | bytes 1540
  899.6 147.2 %copy-start.38 = (f32[2,64]{1,0:T(2,128)S(1)}, f32[2,64]{1,0:T(2,128)}, u32[]{:S(2)}) copy-start(f32[2,64]{1,0:T(2,128)} %param.53) | copy-start | bytes 1540
  899.6 147.2 %copy-start.39 = (f32[2,64]{1,0:T(2,128)S(1)}, f32[2,64]{1,0:T(2,128)}, u32[]{:S(2)}) copy-start(f32[2,64]{1,0:T(2,128)} %param.54) | copy-start | bytes 1540
  912.7 491.8 %copy-start.14 = (f32[64,2048]{1,0:T(8,128)S(1)}, f32[64,2048]{1,0:T(8,128)}, u32[]{:S(2)}) copy-start(f32[64,2048]{1,0:T(8,128)} %param.40) | copy-start | bytes 1572868
  912.7 491.8 %copy-start.19 = (f32[64,2048]{1,0:T(8,128)S(1)}, f32[64,2048]{1,0:T(8,128)}, u32[]{:S(2)}) copy-start(f32[64,2048]{1,0:T(8,128)} %param.43) | copy-start | bytes 1572868
  912.7 491.8 %copy-start.20 = (f32[64,2048]{1,0:T(8,128)S(1)}, f32[64,2048]{1,0:T(8,128)}, u32[]{:S(2)}) copy-start(f32[64,2048]{1,0:T(8,128)} %param.41) | copy-start | bytes 1572868
  912.7 491.8 %copy-start.21 = (f32[64,2048]{1,0:T(8,128)S(1)}, f32[64,2048]{1,0:T(8,128)}, u32[]{:S(2)}) copy-start(f32[64,2048]{1,0:T(8,128)} %param.42) | copy-start | bytes 1572868
  1407.2 1422.5 %copy-start.4 = (f32[128,2,2816]{2,1,0:T(2,128)S(1)}, f32[128,2,2816]{2,1,0:T(2,128)}, u32[]{:S(2)}) copy-start(f32[128,2,2816]{2,1,0:T(2,128)} %param.44) | copy-start | bytes 8650756
  (1 other events, 0.6 us)
Sparse Core Ops, SparseCore 0:
  11.3 54.3 all-gather.12
  67.8 9.8 all-gather.10
  81.1 77.2 all-gather.14
  161.5 74.6 all-gather.16
  242.9 10.6 reduce-scatter.12
  256.9 11.8 all-gather.18
  272.5 252.4 all-gather.20
  526.7 8.7 all-gather.24
  539.2 143.3 all-gather.22
  719.1 10.2 reduce-scatter.16
  733.7 11.8 all-gather.26
  797.3 13.2 reduce-scatter.18
  813.5 81.8 reduce-scatter.22
  897.6 9.1 reduce-scatter.14
  909.5 136.4 reduce-scatter.30
  1048.2 173.7 reduce-scatter.20
  1224.3 180.2 reduce-scatter.24
  1406.8 475.4 reduce-scatter.28
  1884.7 944.9 reduce-scatter.26
where the time goes:
time: 2870 us; the launch traced here: 2860 us
  waiting for transfers between devices  2520 us (88%)
  matrix products  179 us (6%)
  other arithmetic  68.8 us (2%)
  blocking collectives  43.6 us (2%)
  local copies, waits for them, and re-layouts  31.9 us (1%)
    reduce_scatter x1, waiting for transfers between devices, per_device(): lax.psum_scatter(expand_full, 'dp', scatter_dimension=0, tiled=True)  941 us
    reduce_scatter x1, waiting for transfers between devices, per_device(): lax.psum_scatter(contract_full, 'dp', scatter_dimension=0, tiled=True)  475 us
    all_gather x1, waiting for transfers between devices, per_device(): lax.all_gather(expand_weight.astype(bf_type), 'dp', axis=0, tiled=True)  256 us
    reduce_scatter x1, waiting for transfers between devices, per_device(): lax.psum_scatter(mixing_full, 'dp', scatter_dimension=0, tiled=True)  179 us
    reduce_scatter x1, waiting for transfers between devices, per_device(): lax.psum_scatter(query_full, 'dp', scatter_dimension=0, tiled=True)  175 us
    all_gather x1, waiting for transfers between devices, per_device(): lax.all_gather(contract_weight.astype(bf_type), 'dp', axis=0, tiled=True)  138 us
    unnamed x20, waiting for transfers between devices  134 us
    all_gather x1, waiting for transfers between devices, per_device(): lax.all_gather(query_weight.astype(bf_type), 'dp', axis=0, tiled=True)  77.8 us
  transfers between devices with their start and end apart: 19, of which 17 were waited for; matrix products, arithmetic and copies ran while one was open for 5% of the time, Pallas kernels for 0%

commit v1 on v0

v1 whole, which is shorter than its diff:
```python
import jax
import jax.numpy as jnp
from jax import lax
from jax.experimental import pallas as pl
from jax.experimental.pallas import tpu as pltpu
from jax.sharding import PartitionSpec as P

HEAD_DIM = 64
STEP = 5


NORM_EPS = 1e-05
NEG_FILL = -1e30
ROPE_BASE = 10000.0
BETA_ONE = 0.5
BETA_TWO = 0.5
ADAM_EPS = 1e-08
WEIGHT_DECAY = 0.1
MATRIX_RATE = 0.02
GAIN_RATE = 0.2
EMA_KEEP = 0.9
GAIN_KEEP = 0.5
CONTRACT_LAST = (((1,), (1,)), ((), ()))
CONTRACT_FIRST = (((0,), (0,)), ((), ()))


def normalize(field_rows, gain_row):
    factor = lax.rsqrt(jnp.mean(field_rows * field_rows, axis=-1, keepdims=True) + NORM_EPS)
    return field_rows * factor * gain_row


def rotate(field, cosine_table, sine_table):
    half_dim = field.shape[-1] // 2
    first_half = field[..., :half_dim]
    second_half = field[..., half_dim:]
    return jnp.concatenate(
        [
            first_half * cosine_table - second_half * sine_table,
            second_half * cosine_table + first_half * sine_table,
        ],
        axis=-1,
    )


def layout(lengths, valid_keys, places):
    doc_ends = jnp.cumsum(lengths)
    doc_starts = doc_ends - lengths
    segment = jnp.sum((doc_ends[None, :] <= places[:, None]).astype(jnp.int32), axis=1)
    owned_doc = segment[:, None] == jnp.arange(lengths.shape[0], dtype=jnp.int32)[None, :]
    position = places - jnp.sum(jnp.where(owned_doc, doc_starts[None, :], 0), axis=1)
    allowed = (
        (segment[:, None] == segment[None, :])
        & (places[None, :] <= places[:, None])
        & ((valid_keys[None, :] == 1) | (places[:, None] == places[None, :]))
    )
    return (position, allowed)


def rope_tables(position, head_size):
    half_dim = head_size // 2
    inverse = ROPE_BASE ** (-(2.0 * jnp.arange(half_dim, dtype=jnp.float32)) / head_size)
    angles = position.astype(jnp.float32)[:, None] * inverse[None, :]
    return (jnp.cos(angles)[:, None, :], jnp.sin(angles)[:, None, :])


def adamw(grad_value, weight, moment, second, shadow, step_rate, decay_rate, keep_rate):
    moment_new = BETA_ONE * moment + (1.0 - BETA_ONE) * grad_value
    second_new = BETA_TWO * second + (1.0 - BETA_TWO) * grad_value * grad_value
    moment_hat = moment_new / (1.0 - BETA_ONE**STEP)
    second_hat = second_new / (1.0 - BETA_TWO**STEP)
    weight_new = weight - step_rate * (
        moment_hat / (jnp.sqrt(second_hat) + ADAM_EPS) + decay_rate * weight
    )
    shadow_new = keep_rate * shadow + (1.0 - keep_rate) * weight_new
    return (weight_new, moment_new, second_new, shadow_new)


def cast_halves(weight, pair_bit):
    row_count, planes, columns = weight.shape
    half = columns // 2

    def kernel(bit_ref, weight_ref, keep_ref, send_ref):
        for plane in range(planes):
            low = weight_ref[:, plane, :half].astype(jnp.bfloat16)
            high = weight_ref[:, plane, half:].astype(jnp.bfloat16)
            at = pl.ds(plane * half, half)

            @pl.when(bit_ref[0] == 0)
            def _():
                keep_ref[:, at] = low
                send_ref[:, at] = high

            @pl.when(bit_ref[0] != 0)
            def _():
                keep_ref[:, at] = high
                send_ref[:, at] = low

    out = jax.ShapeDtypeStruct((row_count, planes * half), jnp.bfloat16)
    step = 16
    return pl.pallas_call(
        kernel,
        grid_spec=pltpu.PrefetchScalarGridSpec(
            num_scalar_prefetch=1,
            grid=(row_count // step,),
            in_specs=[pl.BlockSpec((step, planes, columns), lambda i, bit: (i, 0, 0))],
            out_specs=[pl.BlockSpec((step, planes * half), lambda i, bit: (i, 0))] * 2,
        ),
        out_shape=(out, out),
        compiler_params=pltpu.CompilerParams(vmem_limit_bytes=32 * 2**20),
    )(pair_bit.reshape(1), weight)


def cast_projections(query, keyval, pair_bit):
    row_count, columns = query.shape
    half, width = columns // 2, keyval.shape[2]

    def kernel(bit_ref, query_ref, keyval_ref, keep_ref, send_ref):
        left = lax.broadcasted_iota(jnp.int32, (row_count, width), 1) < width // 2
        key, value = keyval_ref[:, 0, :], keyval_ref[:, 1, :]
        low = jnp.where(left, key, pltpu.roll(value, width // 2, 1)).astype(jnp.bfloat16)
        high = jnp.where(left, pltpu.roll(key, width // 2, 1), value).astype(jnp.bfloat16)

        def store(low_ref, high_ref):
            low_ref[:, :half] = query_ref[:, :half].astype(jnp.bfloat16)
            high_ref[:, :half] = query_ref[:, half:].astype(jnp.bfloat16)
            low_ref[:, half:] = low
            high_ref[:, half:] = high

        @pl.when(bit_ref[0] == 0)
        def _():
            store(keep_ref, send_ref)

        @pl.when(bit_ref[0] != 0)
        def _():
            store(send_ref, keep_ref)

    out = jax.ShapeDtypeStruct((row_count, half + width), jnp.bfloat16)
    return pl.pallas_call(
        kernel,
        in_specs=[pl.BlockSpec(memory_space=pltpu.SMEM)]
        + [pl.BlockSpec(memory_space=pltpu.VMEM)] * 2,
        out_specs=[pl.BlockSpec(memory_space=pltpu.VMEM)] * 2,
        out_shape=(out, out),
        compiler_params=pltpu.CompilerParams(vmem_limit_bytes=16 * 2**20),
    )(pair_bit.reshape(1), query, keyval)


def projection_update(parts, pair_bit, queries, keyvals):
    row_count, columns = queries[0].shape
    half, width = columns // 2, keyvals[0].shape[2]

    def kernel(bit_ref, *refs):
        parts, olds, news = refs[:4], refs[4:12], refs[12:]
        one, two, three, four = [ref[...].astype(jnp.float32) for ref in parts]
        own, other = one + two, three + four
        mine = bit_ref[0] == 0
        low, high = jnp.where(mine, own, other), jnp.where(mine, other, own)
        left = lax.broadcasted_iota(jnp.int32, (row_count, width), 1) < width // 2
        low_pair, high_pair = low[:, half:], high[:, half:]
        grads = (
            (0, (slice(None), slice(0, half)), low[:, :half]),
            (0, (slice(None), slice(half, columns)), high[:, :half]),
            (4, (slice(None), 0), jnp.where(left, low_pair, pltpu.roll(high_pair, width // 2, 1))),
            (4, (slice(None), 1), jnp.where(left, pltpu.roll(low_pair, width // 2, 1), high_pair)),
        )
        for first, where, grad in grads:
            results = adamw(
                grad,
                *[ref[where] for ref in olds[first : first + 4]],
                MATRIX_RATE,
                WEIGHT_DECAY,
                EMA_KEEP,
            )
            for ref, result in zip(news[first : first + 4], results):
                ref[where] = result

    outs = [jax.ShapeDtypeStruct(old.shape, jnp.float32) for old in queries + keyvals]
    results = pl.pallas_call(
        kernel,
        in_specs=[pl.BlockSpec(memory_space=pltpu.SMEM)]
        + [pl.BlockSpec(memory_space=pltpu.VMEM)] * 12,
        out_specs=[pl.BlockSpec(memory_space=pltpu.VMEM)] * 8,
        out_shape=outs,
        compiler_params=pltpu.CompilerParams(vmem_limit_bytes=32 * 2**20),
    )(pair_bit.reshape(1), *parts, *queries, *keyvals)
    return results[:4], results[4:]


def expand_update(parts, pair_bit, weight, moment, second, shadow):
    row_count, planes, columns = weight.shape
    half = columns // 2
    step = 16

    def kernel(bit_ref, *refs):
        parts, olds, news = refs[:8], refs[8:12], refs[12:]
        for plane in range(planes):
            one, two, three, four = [
                ref[...].astype(jnp.float32) for ref in parts[plane * 4 : plane * 4 + 4]
            ]
            own, other = one + two, three + four
            mine = bit_ref[0] == 0
            for side, grad in (
                (0, jnp.where(mine, own, other)),
                (1, jnp.where(mine, other, own)),
            ):
                where = (slice(None), plane, pl.ds(side * half, half))
                results = adamw(
                    grad, *[ref[where] for ref in olds], MATRIX_RATE, WEIGHT_DECAY, EMA_KEEP
                )
                for ref, result in zip(news, results):
                    ref[where] = result

    def state_spec():
        return pl.BlockSpec((step, planes, columns), lambda i, bit: (i, 0, 0))

    out = jax.ShapeDtypeStruct(weight.shape, jnp.float32)
    return pl.pallas_call(
        kernel,
        grid_spec=pltpu.PrefetchScalarGridSpec(
            num_scalar_prefetch=1,
            grid=(row_count // step,),
            in_specs=[pl.BlockSpec((step, half), lambda i, bit: (i, 0))] * 8
            + [state_spec() for _ in range(4)],
            out_specs=[state_spec() for _ in range(4)],
        ),
        out_shape=(out,) * 4,
        compiler_params=pltpu.CompilerParams(vmem_limit_bytes=48 * 2**20),
    )(pair_bit.reshape(1), *parts, weight, moment, second, shadow)


def per_device(
    layer_input,
    upstream,
    doc_lengths,
    token_valid,
    query_weight,
    query_moment,
    query_second,
    query_shadow,
    keyval_weight,
    keyval_moment,
    keyval_second,
    keyval_shadow,
    mixing_weight,
    mixing_moment,
    mixing_second,
    mixing_shadow,
    expand_weight,
    expand_moment,
    expand_second,
    expand_shadow,
    contract_weight,
    contract_moment,
    contract_second,
    contract_shadow,
    norms_weight,
    norms_moment,
    norms_second,
    norms_shadow,
):
    bf_type = jnp.bfloat16
    fl_type = jnp.float32
    dp_count = lax.axis_size("dp")
    low_count = dp_count // 4
    dp_index = lax.axis_index("dp")
    outer_bit = dp_index // (2 * low_count)
    pair_bit = (dp_index // low_count) % 2
    core_bit = lax.axis_index("tensor")
    low_groups = [[base * low_count + low for low in range(low_count)] for base in range(4)]

    def move(value, target):
        return lax.ppermute(
            value,
            "dp",
            [
                (place * low_count + low, goal * low_count + low)
                for place, goal in target.items()
                for low in range(low_count)
            ],
        )

    def swap(value, flip):
        return move(value, {place: place ^ flip for place in range(4)})

    def swap_pair(value):
        return swap(value, 1)

    def swap_core(value):
        return lax.ppermute(value, "tensor", [(0, 1), (1, 0)])

    def after(value, *earlier):
        return lax.optimization_barrier((value,) + earlier)[0]

    def pick(bit, zero, one):
        return jnp.where(bit == 0, zero, one)

    def gather_low(blocks):
        return lax.all_gather(blocks, "dp", axis=1, tiled=True, axis_index_groups=low_groups)

    def scatter_low(blocks):
        return lax.psum_scatter(
            blocks, "dp", scatter_dimension=1, tiled=True, axis_index_groups=low_groups
        )

    own_rows, model_width = query_weight.shape[0], norms_weight.shape[1] * dp_count * 2

    def exchange_columns(keep, send):
        return keep, swap(send, 1), swap(keep, 2), swap(send, 3)

    def gather_columns(keep, one, two, three):
        low_pair = [pick(pair_bit, keep, one), pick(pair_bit, one, keep)]
        high_pair = [pick(pair_bit, two, three), pick(pair_bit, three, two)]
        quad = pick(outer_bit, jnp.stack(low_pair + high_pair), jnp.stack(high_pair + low_pair))
        return gather_low(quad).reshape(model_width, keep.shape[-1])

    def exchange_owned(rows):
        return rows, move(rows, {0: 2, 1: 0, 2: 3, 3: 1}), move(rows, {1: 2, 2: 1})

    def gather_owned(rows, first, second):
        second = pick(outer_bit ^ pair_bit, rows, second)
        both = pick(outer_bit, jnp.stack([second, first]), jnp.stack([first, second]))
        return gather_low(both).reshape(2 * low_count * rows.shape[0], rows.shape[1])

    def gather_tokens(rows):
        away = swap_pair(rows)
        return jnp.concatenate([rows, swap_core(rows), away, swap_core(away)])

    def scatter_tokens(partial):
        own, across, away, far = jnp.split(partial, 4)

        def over_cores(mine, sent):
            return mine + swap_core(sent.astype(bf_type)).astype(fl_type)

        moved = swap_pair(over_cores(away, far).astype(bf_type))
        return over_cores(own, across) + moved.astype(fl_type)

    qkv_keep, qkv_send = cast_projections(query_weight, keyval_weight, pair_bit)
    other_lengths, other_valid = swap_pair(doc_lengths), swap_pair(token_valid)
    qkv_moved = exchange_columns(qkv_keep, qkv_send)
    gain_copies = jnp.broadcast_to(
        after(norms_weight, qkv_keep)[None], (2 * dp_count,) + norms_weight.shape
    )
    gain_rows = lax.all_to_all(
        gain_copies, ("dp", "tensor"), split_axis=0, concat_axis=0, tiled=True
    )
    gain_rows = gain_rows.transpose(1, 0, 2).reshape(2, model_width)
    input_rows = layer_input.astype(fl_type)
    normed = normalize(input_rows, gain_rows[0]).astype(bf_type)
    normed_all = gather_tokens(normed)
    mixing_moved = exchange_owned(after(mixing_weight, normed).astype(bf_type))
    expand_keep, expand_send = cast_halves(after(expand_weight, normed), pair_bit)
    expand_moved = exchange_columns(expand_keep, expand_send)
    contract_moved = exchange_owned(after(contract_weight, expand_send).astype(bf_type))
    qkv_low = gather_columns(*after(qkv_moved, normed))
    mixing_low = gather_owned(*mixing_moved)
    group_len = token_valid.shape[1]
    places = (
        jnp.arange(group_len, dtype=jnp.int32) + core_bit * (group_len // 2)
    ) % group_len

    def ordered_valid(valid):
        first, second = valid[: group_len // 2], valid[group_len // 2 :]
        return pick(
            core_bit, jnp.concatenate([first, second]), jnp.concatenate([second, first])
        )

    position_one, allowed_one = layout(doc_lengths[0], ordered_valid(token_valid[0]), places)
    position_two, allowed_two = layout(other_lengths[0], ordered_valid(other_valid[0]), places)
    allowed = (allowed_one, allowed_two)
    cosine_table, sine_table = rope_tables(
        jnp.concatenate([position_one, position_two]), HEAD_DIM
    )
    token_count = 2 * group_len
    query_width = query_weight.shape[1] // 2
    key_width = keyval_weight.shape[2] // 2
    head_count = query_width // HEAD_DIM
    kv_count = key_width // HEAD_DIM
    group_ratio = head_count // kv_count
    hidden_width = expand_weight.shape[2] // 2
    factor = HEAD_DIM ** (-0.5)
    qkv_pre = jnp.dot(normed_all, qkv_low, preferred_element_type=fl_type)
    queries = rotate(
        qkv_pre[:, :query_width].reshape(token_count, head_count, HEAD_DIM),
        cosine_table,
        sine_table,
    ).astype(bf_type)
    keys = rotate(
        qkv_pre[:, query_width : query_width + key_width].reshape(token_count, kv_count, HEAD_DIM),
        cosine_table,
        sine_table,
    ).astype(bf_type)
    values = (
        qkv_pre[:, query_width + key_width :]
        .reshape(token_count, kv_count, HEAD_DIM)
        .astype(bf_type)
    )

    expand_low = gather_columns(*after(expand_moved, queries))
    contract_low = gather_owned(*after(contract_moved, queries))

    def part(array, group_index, kv_index, heads):
        return array[
            group_index * group_len : (group_index + 1) * group_len,
            kv_index * heads : (kv_index + 1) * heads,
        ]

    def head_scores(group_index, kv_index):
        query_block = part(queries, group_index, kv_index, group_ratio)
        key_block = part(keys, group_index, kv_index, 1)[:, 0]
        raw_scores = (
            jnp.einsum("gre,ke->rgk", query_block, key_block, preferred_element_type=fl_type)
            * factor
        )
        return (query_block, key_block, jnp.where(allowed[group_index][None], raw_scores, NEG_FILL))

    mixed_groups = []
    log_totals = {}
    for group_index in range(2):
        mixed_parts = []
        for kv_index in range(kv_count):
            _, _, masked = head_scores(group_index, kv_index)
            largest = jnp.max(masked, axis=-1, keepdims=True)
            exp_scores = jnp.exp(masked - largest)
            totals = jnp.sum(exp_scores, axis=-1, keepdims=True)
            soft_probs = (exp_scores / totals).astype(bf_type)
            log_totals[group_index, kv_index] = largest + jnp.log(totals)
            mixed_parts.append(
                jnp.einsum(
                    "rgk,ke->gre",
                    soft_probs,
                    part(values, group_index, kv_index, 1)[:, 0],
                    preferred_element_type=fl_type,
                )
            )
        mixed_groups.append(jnp.concatenate(mixed_parts, axis=1))
    mixed = jnp.concatenate(mixed_groups).reshape(token_count, query_width).astype(bf_type)
    attended = scatter_tokens(jnp.dot(mixed, mixing_low, preferred_element_type=fl_type))
    middle = input_rows + attended
    normed_two = normalize(middle, gain_rows[1]).astype(bf_type)
    normed_two_all = gather_tokens(normed_two)
    gate_up = jnp.dot(normed_two_all, expand_low, preferred_element_type=fl_type)
    gate, up = gate_up[:, :hidden_width], gate_up[:, hidden_width:]
    gate_sig = jax.nn.sigmoid(gate)
    gate_act = gate * gate_sig
    hidden = (gate_act * up).astype(bf_type)
    out_grad = upstream.astype(fl_type)
    out_grad_all = gather_tokens(after(upstream, normed_two))

    def reduce_columns(full):
        return scatter_low(full.reshape(4, low_count * own_rows, full.shape[1]))

    def scatter_columns(reduced):
        place = 2 * outer_bit + pair_bit
        kept, one, two, three = [
            lax.dynamic_index_in_dim(reduced, place ^ flip, 0, keepdims=False) for flip in range(4)
        ]
        return kept, swap(two, 2), swap(one, 1), swap(three, 3)

    def reduce_owned(full):
        return scatter_low(full.reshape(2, full.shape[0] // 2, full.shape[1]))

    def scatter_owned(reduced):
        first = move(pick(outer_bit, reduced[1], reduced[0]), {0: 1, 1: 3, 2: 0, 3: 2})
        rest = pick(outer_bit, reduced[0], reduced[1])
        second = pick(outer_bit ^ pair_bit, rest, move(rest, {1: 2, 2: 1}))
        return first.astype(fl_type) + second.astype(fl_type)

    contract_full = lax.dot_general(
        hidden, out_grad_all, CONTRACT_FIRST, preferred_element_type=fl_type
    ).astype(bf_type)
    contract_reduced = reduce_owned(contract_full)
    hidden_grad = lax.dot_general(
        after(out_grad_all, contract_full), contract_low, CONTRACT_LAST, preferred_element_type=fl_type
    )
    gate_grad = hidden_grad * up * gate_sig * (1.0 + gate * (1.0 - gate_sig))
    up_grad = hidden_grad * gate_act
    gate_grad, up_grad = gate_grad.astype(bf_type), up_grad.astype(bf_type)
    gate_full = lax.dot_general(
        normed_two_all, gate_grad, CONTRACT_FIRST, preferred_element_type=fl_type
    ).astype(bf_type)
    up_full = lax.dot_general(
        after(normed_two_all, gate_full), up_grad, CONTRACT_FIRST, preferred_element_type=fl_type
    ).astype(bf_type)
    gate_reduced, up_reduced = reduce_columns(gate_full), reduce_columns(up_full)
    gate_up_grad = after(jnp.concatenate([gate_grad, up_grad], axis=1), up_full)
    normed_two_grad = scatter_tokens(
        lax.dot_general(gate_up_grad, expand_low, CONTRACT_LAST, preferred_element_type=fl_type)
    )
    middle_pull = jax.vjp(normalize, middle, gain_rows[1])[1]
    middle_part, gain_two_grad = middle_pull(normed_two_grad)
    middle_grad = out_grad + middle_part
    attended_all = gather_tokens(middle_grad.astype(bf_type))
    branch = scatter_tokens(
        jnp.dot(after(hidden, middle_grad), contract_low, preferred_element_type=fl_type)
    )
    layer_output = (middle + branch).astype(bf_type)
    mixing_full = lax.dot_general(
        mixed, attended_all, CONTRACT_FIRST, preferred_element_type=fl_type
    ).astype(bf_type)
    mixing_reduced = reduce_owned(mixing_full)
    attended_all = after(attended_all, mixing_full, contract_reduced)
    contract_grad = scatter_owned(contract_reduced)
    mixed_grad = (
        lax.dot_general(attended_all, mixing_low, CONTRACT_LAST, preferred_element_type=fl_type)
        .astype(bf_type)
        .reshape(token_count, head_count, HEAD_DIM)
    )
    query_grads = []
    key_grads = []
    value_grads = []
    for group_index in range(2):
        for kv_index in range(kv_count):
            query_block, key_block, masked = head_scores(group_index, kv_index)
            soft_exact = jnp.exp(masked - log_totals[group_index, kv_index])
            out_block = part(mixed_grad, group_index, kv_index, group_ratio)
            prob_grad = jnp.einsum(
                "gre,ke->rgk",
                out_block,
                part(values, group_index, kv_index, 1)[:, 0],
                preferred_element_type=fl_type,
            )
            inner_sum = jnp.sum(prob_grad * soft_exact, axis=-1, keepdims=True)
            score_grad = (soft_exact * (prob_grad - inner_sum)).astype(bf_type)
            query_grads.append(
                jnp.einsum("rgk,ke->gre", score_grad, key_block, preferred_element_type=fl_type)
                * factor
            )
            key_grads.append(
                jnp.einsum("rgk,gre->ke", score_grad, query_block, preferred_element_type=fl_type)
                * factor
            )
            value_grads.append(
                jnp.einsum(
                    "rgk,gre->ke",
                    soft_exact.astype(bf_type),
                    out_block,
                    preferred_element_type=fl_type,
                )
            )

    def assemble(blocks, axis):
        return jnp.concatenate(
            [
                jnp.concatenate(blocks[:kv_count], axis=axis),
                jnp.concatenate(blocks[kv_count:], axis=axis),
            ]
        )

    query_back = (
        rotate(assemble(query_grads, 1), cosine_table, -sine_table)
        .astype(bf_type)
        .reshape(token_count, query_width)
    )
    key_back = rotate(
        assemble(key_grads, 1).reshape(token_count, kv_count, HEAD_DIM), cosine_table, -sine_table
    ).reshape(token_count, key_width)
    value_back = assemble(value_grads, 1)
    qkv_back = jnp.concatenate(
        [query_back, key_back.astype(bf_type), value_back.astype(bf_type)], axis=1
    )
    qkv_back = after(qkv_back, gate_reduced)
    qkv_full = lax.dot_general(
        normed_all, qkv_back, CONTRACT_FIRST, preferred_element_type=fl_type
    ).astype(bf_type)
    qkv_reduced = reduce_columns(qkv_full)
    qkv_back = after(qkv_back, qkv_full, up_reduced, contract_grad)
    expand_parts = scatter_columns(gate_reduced) + scatter_columns(up_reduced)
    mixing_grad = scatter_owned(after(mixing_reduced, qkv_back))
    qkv_parts = scatter_columns(after(qkv_reduced, qkv_back))
    normed_grad = scatter_tokens(
        lax.dot_general(qkv_back, qkv_low, CONTRACT_LAST, preferred_element_type=fl_type)
    )
    rows_pull = jax.vjp(normalize, input_rows, gain_rows[0])[1]
    rows_part, gain_one_grad = rows_pull(normed_grad)
    input_grad = middle_grad + rows_part
    gain_parts = jnp.stack([gain_one_grad, gain_two_grad]).reshape(2, 2 * dp_count, -1)
    gain_sums = jnp.sum(
        lax.all_to_all(gain_parts, ("dp", "tensor"), split_axis=1, concat_axis=1, tiled=True),
        axis=1,
    )
    (
        (query_master, query_momentum, query_variance, query_average),
        (keyval_master, keyval_momentum, keyval_variance, keyval_average),
    ) = projection_update(
        qkv_parts,
        pair_bit,
        [query_weight, query_moment, query_second, query_shadow],
        [keyval_weight, keyval_moment, keyval_second, keyval_shadow],
    )
    mixing_master, mixing_momentum, mixing_variance, mixing_average = adamw(
        mixing_grad,
        mixing_weight,
        mixing_moment,
        mixing_second,
        mixing_shadow,
        MATRIX_RATE,
        WEIGHT_DECAY,
        EMA_KEEP,
    )
    expand_master, expand_momentum, expand_variance, expand_average = expand_update(
        expand_parts, pair_bit, expand_weight, expand_moment, expand_second, expand_shadow
    )
    contract_master, contract_momentum, contract_variance, contract_average = adamw(
        contract_grad,
        contract_weight,
        contract_moment,
        contract_second,
        contract_shadow,
        MATRIX_RATE,
        WEIGHT_DECAY,
        EMA_KEEP,
    )
    norms_master, norms_momentum, norms_variance, norms_average = adamw(
        gain_sums, norms_weight, norms_moment, norms_second, norms_shadow, GAIN_RATE, 0.0, GAIN_KEEP
    )
    return (
        layer_output,
        input_grad,
        query_master,
        query_momentum,
        query_variance,
        query_average,
        keyval_master,
        keyval_momentum,
        keyval_variance,
        keyval_average,
        mixing_master,
        mixing_momentum,
        mixing_variance,
        mixing_average,
        expand_master,
        expand_momentum,
        expand_variance,
        expand_average,
        contract_master,
        contract_momentum,
        contract_variance,
        contract_average,
        norms_master,
        norms_momentum,
        norms_variance,
        norms_average,
    )


def solution(mesh):
    in_specs = (
        P(("dp", "tensor"), None),
        P(("dp", "tensor"), None),
        P("dp", None),
        P("dp", None),
        P("dp", "tensor"),
        P("dp", "tensor"),
        P("dp", "tensor"),
        P("dp", "tensor"),
        P("dp", None, "tensor"),
        P("dp", None, "tensor"),
        P("dp", None, "tensor"),
        P("dp", None, "tensor"),
        P(("tensor", "dp"), None),
        P(("tensor", "dp"), None),
        P(("tensor", "dp"), None),
        P(("tensor", "dp"), None),
        P("dp", None, "tensor"),
        P("dp", None, "tensor"),
        P("dp", None, "tensor"),
        P("dp", None, "tensor"),
        P(("tensor", "dp"), None),
        P(("tensor", "dp"), None),
        P(("tensor", "dp"), None),
        P(("tensor", "dp"), None),
        P(None, ("dp", "tensor")),
        P(None, ("dp", "tensor")),
        P(None, ("dp", "tensor")),
        P(None, ("dp", "tensor")),
    )
    out_specs = (
        P(("dp", "tensor"), None),
        P(("dp", "tensor"), None),
        P("dp", "tensor"),
        P("dp", "tensor"),
        P("dp", "tensor"),
        P("dp", "tensor"),
        P("dp", None, "tensor"),
        P("dp", None, "tensor"),
        P("dp", None, "tensor"),
        P("dp", None, "tensor"),
        P(("tensor", "dp"), None),
        P(("tensor", "dp"), None),
        P(("tensor", "dp"), None),
        P(("tensor", "dp"), None),
        P("dp", None, "tensor"),
        P("dp", None, "tensor"),
        P("dp", None, "tensor"),
        P("dp", None, "tensor"),
        P(("tensor", "dp"), None),
        P(("tensor", "dp"), None),
        P(("tensor", "dp"), None),
        P(("tensor", "dp"), None),
        P(None, ("dp", "tensor")),
        P(None, ("dp", "tensor")),
        P(None, ("dp", "tensor")),
        P(None, ("dp", "tensor")),
    )
    return jax.shard_map(
        per_device, mesh=mesh, in_specs=in_specs, out_specs=out_specs, check_vma=False
    )
```

time: 2870 us -> 702 us (0.24)
  waiting for transfers between devices: 2520 us -> 297 us
  starting transfers between devices: 1.19 us -> 72.2 us
  blocking collectives: 43.6 us -> 0 us
    reduce_scatter x9 -> x5, waiting for transfers between devices: 1820 us -> 36.4 us  [scatter_low(): lax.psum_scatter(blocks, 'dp', scatter_dimension=1, tiled=True, axis_inde...]
    all_gather x9 -> x4, waiting for transfers between devices: 561 us -> 20.2 us  [gather_low(): lax.all_gather(blocks, 'dp', axis=1, tiled=True, axis_index_groups=low_gr...]
    ppermute x0 -> x49, waiting for transfers between devices: none -> 235 us  [the longest x33 233 us: move(): lax.ppermute(value, 'dp', [(place * low_count + low, goal * low_count + l...]
    unnamed x20 -> x9, waiting for transfers between devices: 134 us -> 0.15 us
    ppermute x0 -> x49, starting transfers between devices: none -> 60.2 us  [the longest x33 57.9 us: move(): lax.ppermute(value, 'dp', [(place * low_count + low, goal * low_count + l...]
    all_gather x1 -> x0, blocking collectives: 43.6 us -> none  [per_device(): lax.all_gather(norms_weight, ('dp', 'tensor'), axis=1, tiled=True)]
    dot_general x18 -> x17, matrix products: 132 us -> 128 us  [the longest x1 18.9 us: per_device(): jnp.dot(normed_two_all, expand_low, preferred_element_type=fl_type)]
  transfers between devices with their start and end apart: 19 -> 60, of which waited for: 17 -> 22; matrix products, arithmetic and copies ran while one was open for 5% -> 39% of each run, Pallas kernels for 0% -> 3%
where the time goes in v1:
time: 702 us; the launch traced here: 694 us
  waiting for transfers between devices  297 us (42%)
  matrix products  155 us (22%)
  other arithmetic  91.7 us (13%)
  starting transfers between devices  72.2 us (10%)
  local copies, waits for them, and re-layouts  41 us (6%)
  Pallas kernels  20.7 us (3%)
  between operations  15.9 us (2%)
    ppermute x33, waiting for transfers between devices, move(): lax.ppermute(value, 'dp', [(place * low_count + low, goal * low_count + l...  233 us
    ppermute x33, starting transfers between devices, move(): lax.ppermute(value, 'dp', [(place * low_count + low, goal * low_count + l...  57.9 us
    reduce_scatter x5, waiting for transfers between devices, scatter_low(): lax.psum_scatter(blocks, 'dp', scatter_dimension=1, tiled=True, axis_inde...  36.4 us
    unnamed x195, local copies, waits for them, and re-layouts  23.4 us
    all_gather x4, waiting for transfers between devices, gather_low(): lax.all_gather(blocks, 'dp', axis=1, tiled=True, axis_index_groups=low_gr...  20.2 us
    dot_general x1, matrix products, per_device(): jnp.dot(normed_two_all, expand_low, preferred_element_type=fl_type)  18.9 us
    dot_general x1, matrix products, per_device(): lax.dot_general(gate_up_grad, expand_low, CONTRACT_LAST, preferred_elemen...  18.1 us
    dot_general x1, matrix products, per_device(): lax.dot_general(after(out_grad_all, contract_full), contract_low, CONTRAC...  15.3 us
  transfers between devices with their start and end apart: 60, of which 22 were waited for; matrix products, arithmetic and copies ran while one was open for 39% of the time, Pallas kernels for 3%

profile of v1, /device:TPU:0, one launch (start us, length us, event | category | flops | bytes accessed | tf_op | source)
XLA Modules:
  0.0 694.0 jit_solution(17076676503519464196)
XLA Ops:
  9.4 5.1 collective-permute-start.5
  17.9 6.0 all-to-all-start
  26.6 4.4 all-to-all-done
  36.5 2.5 fusion.21
  47.4 19.2 %collective-permute-done.1 = bf16[256,2048]{1,0:T(8,128)(2,1)} collective-permute-done((bf16[256,2048]{1,0:T(8,128)(2,1)}, bf16[256,2048]{1,0:T(8,128)(2,1)}, u32[]{:S(2)}, u32[]{:S(2)}) %collective-permute-start.1) | collective-permute-done | bytes 1048608 | tf_op jit(solution)/shard_map/ppermute | solution.py:272
  70.0 5.0 shard_map.468
  77.9 2.6 collective-permute-start.17
  81.5 7.0 %fusion.125 = (bf16[1024,640]{0,1:T(8,128)(2,1)}, f32[1024,640]{0,1:T(8,128)S(1)}) fusion(bf16[2048,640]{1,0:T(8,128)(2,1)} %bitcast.211, bf16[256,2048]{1,0:T(8,128)(2,1)} %collective-permute-done.2, bf16[256,2048]{1,0:T(8,128)(2,1)} %collective-permute-done.1, bf16[256,2048]{1,0:T(8,128)(2,1)} %collective-permute-done, bf16[256,2048]{1,0:T(8,128)(2,1)} %fusion.21), kind=kOutput, calls=%fused_computation.258 | convolution fusion | flops 2701787136 | bytes 10747904 | tf_op jit(solution)/shard_map/dot_general | solution.py:381
  90.7 49.7 %collective-permute-done.17 = bf16[128,2816]{1,0:T(8,128)(2,1)} collective-permute-done((bf16[128,2816]{1,0:T(8,128)(2,1)}, bf16[128,2816]{1,0:T(8,128)(2,1)}, u32[]{:S(2)}, u32[]{:S(2)}) %collective-permute-start.17) | collective-permute-done | bytes 720928 | tf_op jit(solution)/shard_map/ppermute | solution.py:272
  145.9 3.5 collective-permute-done.7
  152.0 2.5 fusion.126
  159.0 2.5 fusion.41
  161.5 3.2 fusion.40
  164.7 4.1 fusion.127
  177.8 16.0 %collective-permute-done.22 = bf16[176,2048]{1,0:T(8,128)(2,1)} collective-permute-done((bf16[176,2048]{1,0:T(8,128)(2,1)}, bf16[176,2048]{1,0:T(8,128)(2,1)}, u32[]{:S(2)}, u32[]{:S(2)}) %collective-permute-start.22) | collective-permute-done | bytes 720928 | tf_op jit(solution)/shard_map/ppermute | solution.py:272
  195.2 19.0 %collective-permute-done.12 = bf16[256,2048]{1,0:T(8,128)(2,1)} collective-permute-done((bf16[256,2048]{1,0:T(8,128)(2,1)}, bf16[256,2048]{1,0:T(8,128)(2,1)}, u32[]{:S(2)}, u32[]{:S(2)}) %collective-permute-start.12) | collective-permute-done | bytes 1048608 | tf_op jit(solution)/shard_map/ppermute | solution.py:272
  214.3 3.1 multiply_reduce_fusion.2
  222.0 2.7 maximum_select_fusion.1
  224.9 21.5 %collective-permute-done.20 = bf16[256,2048]{1,0:T(8,128)(2,1)} collective-permute-done((bf16[256,2048]{1,0:T(8,128)(2,1)}, bf16[256,2048]{1,0:T(8,128)(2,1)}, u32[]{:S(2)}, u32[]{:S(2)}) %collective-permute-start.20) | collective-permute-done | bytes 1048608 | tf_op jit(solution)/shard_map/ppermute | solution.py:272
  246.9 19.4 %collective-permute-done.14 = bf16[256,2048]{1,0:T(8,128)(2,1)S(1)} collective-permute-done((bf16[256,2048]{1,0:T(8,128)(2,1)}, bf16[256,2048]{1,0:T(8,128)(2,1)S(1)}, u32[]{:S(2)}, u32[]{:S(2)}) %collective-permute-start.14) | collective-permute-done | bytes 1048608 | tf_op jit(solution)/shard_map/ppermute | solution.py:272
  272.6 18.9 %fusion.111 = f32[1024,2816]{1,0:T(8,128)S(1)} fusion(bf16[2048,2816]{1,0:T(8,128)(2,1)} %bitcast.226, bf16[256,2048]{1,0:T(8,128)(2,1)} %collective-permute-done.15, bf16[256,2048]{1,0:T(8,128)(2,1)} %copy-done.41, bf16[256,2048]{1,0:T(8,128)(2,1)} %copy-done.43, bf16[256,2048]{1,0:T(8,128)(2,1)} %multiply_convert_fusion.3), kind=kOutput, calls=%fused_computation.248 | convolution fusion | flops 11827937280 | bytes 27262976 | tf_op jit(solution)/shard_map/dot_general | solution.py:441
  293.3 3.6 copy-done.19
  296.9 8.1 %convolution_convert_fusion.2 = bf16[1408,2048]{1,0:T(8,128)(2,1)} fusion(bf16[1024,1408]{1,0:T(8,128)(2,1)S(1)} %multiply_convert_fusion.2, bf16[1024,2048]{1,0:T(8,128)(2,1)S(1)} %copy-done.59), kind=kOutput, calls=%fused_computation.20 | convolution fusion | flops 5908463616 | bytes 12845056 | tf_op jit(solution)/shard_map/dot_general | solution.py:468
  305.3 20.2 %all-gather.11.cloned.1.call-done = bf16[2,704,2048]{2,1,0:T(8,128)(2,1)} async-done(((bf16[2,176,2048]{2,1,0:T(8,128)(2,1)}), bf16[2,704,2048]{2,1,0:T(8,128)(2,1)}) %all-gather.11.cloned.1.call-update) | async-done | bytes 5767184 | tf_op jit(solution)/shard_map/all_gather | solution.py:298
  325.5 15.3 %multiply_convert_fusion.1 = (bf16[1024,1408]{1,0:T(8,128)(2,1)S(1)}, bf16[1024,1408]{1,0:T(8,128)(2,1)}) fusion(f32[1024,2816]{1,0:T(8,128)} %copy-done.19, bf16[1024,2048]{1,0:T(8,128)(2,1)} %copy-done.58, bf16[1408,2048]{1,0:T(8,128)(2,1)} %bitcast.228), kind=kOutput, calls=%fused_computation.27 | convolution fusion | flops 5924323328 | bytes 27262976 | tf_op jit(solution)/shard_map/dot_general | solution.py:472
  340.8 10.8 %convolution_convert_fusion.1 = bf16[2048,1408]{1,0:T(8,128)(2,1)} fusion(bf16[1024,1408]{1,0:T(8,128)(2,1)S(1)} %get-tuple-element.133, bf16[256,2048]{1,0:T(8,128)(2,1)} %collective-permute-done.15, bf16[256,2048]{1,0:T(8,128)(2,1)S(1)} %copy-done.42, bf16[256,2048]{1,0:T(8,128)(2,1)S(1)} %copy-done.44, bf16[256,2048]{1,0:T(8,128)(2,1)S(1)} %copy-done.29), kind=kOutput, calls=%fused_computation.19 | convolution fusion | flops 5925240832 | bytes 12845056 | tf_op jit(solution)/shard_map/dot_general | solution.py:478
  351.7 2.5 pad_maximum_fusion.2
  356.0 2.9 pad_maximum_fusion
  359.0 8.6 %convolution_convert_fusion = bf16[2048,1408]{1,0:T(8,128)(2,1)} fusion(bf16[1024,2048]{1,0:T(8,128)(2,1)S(1)} %pad_maximum_fusion.2, bf16[1024,1408]{1,0:T(8,128)(2,1)S(1)} %copy-done.32), kind=kOutput, calls=%fused_computation.18 | convolution fusion | flops 5908463616 | bytes 12845056 | tf_op jit(solution)/shard_map/dot_general | solution.py:481
  368.1 18.1 %fusion.128 = (bf16[1024,2048]{1,0:T(8,128)(2,1)}, f32[1024,2048]{1,0:T(8,128)S(1)}) fusion(bf16[1024,2816]{1,0:T(8,128)(2,1)} %pad_maximum_fusion, bf16[2048,2816]{1,0:T(8,128)(2,1)} %bitcast.227), kind=kOutput, calls=%fused_computation.261 | convolution fusion | flops 11813257216 | bytes 29884416 | tf_op jit(solution)/shard_map/dot_general | solution.py:487
  392.7 23.7 %collective-permute-done.26 = bf16[256,2048]{1,0:T(8,128)(2,1)S(1)} collective-permute-done((bf16[256,2048]{1,0:T(8,128)(2,1)S(1)}, bf16[256,2048]{1,0:T(8,128)(2,1)S(1)}, u32[]{:S(2)}, u32[]{:S(2)}) %collective-permute-start.26) | collective-permute-done | bytes 1048608 | tf_op jit(solution)/shard_map/ppermute | solution.py:272
  417.4 3.9 fusion.115
  422.7 8.8 %fusion.129 = (bf16[1024,2048]{1,0:T(8,128)(2,1)S(1)}, f32[1024,2048]{1,0:T(8,128)S(1)}) fusion(bf16[1024,1408]{1,0:T(8,128)(2,1)S(1)} %copy-done.31, bf16[1408,2048]{1,0:T(8,128)(2,1)} %bitcast.229), kind=kOutput, calls=%fused_computation.262 | convolution fusion | flops 5907677184 | bytes 21233664 | tf_op jit(solution)/shard_map/dot_general | solution.py:494
  433.4 12.4 %collective-permute-done.31 = bf16[256,2048]{1,0:T(8,128)(2,1)S(1)} collective-permute-done((bf16[256,2048]{1,0:T(8,128)(2,1)S(1)}, bf16[256,2048]{1,0:T(8,128)(2,1)S(1)}, u32[]{:S(2)}, u32[]{:S(2)}) %collective-permute-start.31) | collective-permute-done | bytes 1048608 | tf_op jit(solution)/shard_map/ppermute | solution.py:272
  449.3 3.6 convolution_convert_fusion.4
  453.0 3.8 pad_maximum_fusion.3
  456.8 2.5 select_bitcast_fusion.1
  461.7 6.1 convolution_convert_fusion.5
  468.0 6.3 fusion.3
  474.2 4.6 fusion.5
  480.1 5.9 fusion
  486.0 5.1 fusion.2
  500.7 7.7 %convolution_convert_fusion.3 = bf16[2048,640]{1,0:T(8,128)(2,1)} fusion(bf16[1024,640]{0,1:T(8,128)(2,1)} %maximum_maximum_fusion, bf16[256,2048]{1,0:T(8,128)(2,1)} %collective-permute-done.2, bf16[256,2048]{1,0:T(8,128)(2,1)} %collective-permute-done.1, bf16[256,2048]{1,0:T(8,128)(2,1)} %collective-permute-done, bf16[256,2048]{1,0:T(8,128)(2,1)} %fusion.21), kind=kOutput, calls=%fused_computation.45 | convolution fusion | flops 2702442496 | bytes 8126464 | tf_op jit(solution)/shard_map/dot_general | solution.py:562
  508.5 6.7 multiply_add_fusion.1
  515.2 16.5 %reduce-scatter.10.cloned.1.call-done = bf16[4,128,1408]{2,1,0:T(8,128)(2,1)} async-done(((bf16[4,512,1408]{2,1,0:T(8,128)(2,1)}), bf16[4,128,1408]{2,1,0:T(8,128)(2,1)}) %reduce-scatter.10.cloned.1.call-update) | async-done | bytes 1441808 | tf_op jit(solution)/shard_map/reduce_scatter | solution.py:301
  531.7 9.2 %fusion.130 = (bf16[1024,2048]{1,0:T(8,128)(2,1)S(1)}, f32[1024,2048]{1,0:T(8,128)}) fusion(bf16[1024,640]{0,1:T(8,128)(2,1)} %maximum_maximum_fusion, bf16[2048,640]{1,0:T(8,128)(2,1)} %bitcast.212), kind=kOutput, calls=%fused_computation.263 | convolution fusion | flops 2686451712 | bytes 16515072 | tf_op jit(solution)/shard_map/dot_general | solution.py:571
  544.9 3.3 collective-permute-start.45
  548.2 2.4 dynamic-slice_bitcast_fusion
  550.6 19.8 %reduce-scatter.14.cloned.1.call-done = bf16[2,64,2048]{2,1,0:T(8,128)(2,1)} async-done(((bf16[2,256,2048]{2,1,0:T(8,128)(2,1)}), bf16[2,64,2048]{2,1,0:T(8,128)(2,1)}) %reduce-scatter.14.cloned.1.call-update) | async-done | bytes 524304 | tf_op jit(solution)/shard_map/reduce_scatter | solution.py:301
  571.7 2.5 collective-permute-start.43
  577.9 2.9 collective-permute-start.46
  581.4 19.3 %collective-permute-done.43.refs_1_ = bf16[128,1408]{1,0:T(8,128)(2,1)S(1)} collective-permute-done((bf16[128,1408]{1,0:T(8,128)(2,1)}, bf16[128,1408]{1,0:T(8,128)(2,1)S(1)}, u32[]{:S(2)}, u32[]{:S(2)}) %collective-permute-start.43) | collective-permute-done | bytes 360480 | tf_op jit(solution)/shard_map/ppermute | solution.py:272
  601.5 14.2 %collective-permute-start.37 = (bf16[256,2048]{1,0:T(8,128)(2,1)S(1)}, bf16[256,2048]{1,0:T(8,128)(2,1)S(1)}, u32[]{:S(2)}, u32[]{:S(2)}) collective-permute-start(bf16[256,2048]{1,0:T(8,128)(2,1)S(1)} %fusion.27), channel_id=1, source_target_pairs={{0,8},{2,10},{4,12},{6,14},{8,0},{10,2},{12,4},{14,6},{16,24},{18,... | collective-permute-start | bytes 3145736 | tf_op jit(solution)/shard_map/ppermute | solution.py:272
  615.7 3.7 fusion.32
  619.4 3.4 collective-permute-done.46.refs_5_
  622.9 12.7 %shard_map.470 = (f32[128,2,2816]{2,1,0:T(2,128)}, f32[128,2,2816]{2,1,0:T(2,128)}, f32[128,2,2816]{2,1,0:T(2,128)}, f32[128,2,2816]{2,1,0:T(2,128)}) custom-call(s32[1]{0:T(128)} %bitcast.bit_ref, bf16[128,1408]{1,0:T(8,128)(2,1)S(1)} %get-tuple-element.154.refs_0_, bf16[128,1408]{1,0:T(8,128)(2,1)S(1)} %collective-permute-done.43.refs_1_, ...), custom_call_target="tpu_custom_call" | custom-call | tf_op jit(solution)/shard_map/pallas_call | solution.py:217
  637.3 12.4 %collective-permute-done.37 = bf16[256,2048]{1,0:T(8,128)(2,1)S(1)} collective-permute-done((bf16[256,2048]{1,0:T(8,128)(2,1)S(1)}, bf16[256,2048]{1,0:T(8,128)(2,1)S(1)}, u32[]{:S(2)}, u32[]{:S(2)}) %collective-permute-start.37) | collective-permute-done | bytes 1048608 | tf_op jit(solution)/shard_map/ppermute | solution.py:272
  649.8 3.0 fusion.22
  653.7 4.6 all-to-all-start.1
  658.4 5.6 fusion.24
  672.4 3.9 collective-permute-done.40.refs_3_
  676.3 4.3 collective-permute-done.39.refs_2_
  680.6 3.5 collective-permute-done.38.refs_1_
  684.2 2.9 shard_map.469
  (382 shorter events, 118.8 us)
Async XLA Ops:
  9.2 60.8 %copy-start = (f32[128,2,2816]{2,1,0:T(2,128)S(1)}, f32[128,2,2816]{2,1,0:T(2,128)}, u32[]{:S(2)}) copy-start(f32[128,2,2816]{2,1,0:T(2,128)} %refs_8_.3) | copy-start | bytes 8650756
  9.4 29.7 %collective-permute-start.5 = (bf16[128,640]{1,0:T(8,128)(2,1)S(1)}, bf16[128,640]{1,0:T(8,128)(2,1)S(1)}, u32[]{:S(2)}, u32[]{:S(2)}) collective-permute-start(bf16[128,640]{1,0:T(8,128)(2,1)S(1)} %get-tuple-element.69), channel_id=1, source_target_pairs={{0,24},{2,26},{4,28},{6,30},{8,16},{10,18},{12,20},{14,22},{16,8},... | collective-permute-start | bytes 491528 | tf_op jit(solution)/shard_map/ppermute | solution.py:272
  14.5 24.5 %collective-permute-start.3 = (bf16[128,640]{1,0:T(8,128)(2,1)S(1)}, bf16[128,640]{1,0:T(8,128)(2,1)S(1)}, u32[]{:S(2)}, u32[]{:S(2)}) collective-permute-start(bf16[128,640]{1,0:T(8,128)(2,1)S(1)} %get-tuple-element.69), channel_id=1, source_target_pairs={{0,8},{2,10},{4,12},{6,14},{8,0},{10,2},{12,4},{14,6},{16,24},{18,... | collective-permute-start | bytes 491528 | tf_op jit(solution)/shard_map/ppermute | solution.py:272
  14.5 24.5 %collective-permute-start.4 = (bf16[128,640]{1,0:T(8,128)(2,1)S(1)}, bf16[128,640]{1,0:T(8,128)(2,1)}, u32[]{:S(2)}, u32[]{:S(2)}) collective-permute-start(bf16[128,640]{1,0:T(8,128)(2,1)S(1)} %get-tuple-element.70), channel_id=1, source_target_pairs={{0,16},{2,18},{4,20},{6,22},{8,24},{10,26},{12,28},{14,30},{16,0},... | collective-permute-start | bytes 491528 | tf_op jit(solution)/shard_map/ppermute | solution.py:272
  17.9 13.1 %all-to-all-start = ((f32[32,1,128]{2,1,0:T(1,128)}), f32[32,1,128]{2,1,0:T(1,128)S(1)}, u32[]{:S(2)}, u32[]{:S(2)}) async-start(f32[32,1,128]{2,1,0:T(1,128)} %reshape.691), calls=%async_computation | async-start | bytes 32768 | tf_op jit(solution)/shard_map/all_to_all | solution.py:343
  23.9 57.6 %all-gather.5.cloned.1.call-start = ((), (), s32[]{:S(2)}) async-start(), calls=%async_computation.7 | async-start | bytes 3276800 | tf_op jit(solution)/shard_map/all_gather | solution.py:298
  41.1 123.6 %all-gather.7.cloned.1.call-start = ((), (), s32[]{:S(2)}) async-start(), calls=%async_computation.8 | async-start | bytes 2621440 | tf_op jit(solution)/shard_map/all_gather | solution.py:298
  41.1 3.6 collective-permute-start.6
  41.8 24.9 %collective-permute-start.1 = (bf16[256,2048]{1,0:T(8,128)(2,1)}, bf16[256,2048]{1,0:T(8,128)(2,1)}, u32[]{:S(2)}, u32[]{:S(2)}) collective-permute-start(bf16[256,2048]{1,0:T(8,128)(2,1)} %fusion.21), channel_id=1, source_target_pairs={{0,8},{2,10},{4,12},{6,14},{8,0},{10,2},{12,4},{14,6},{16,24},{18,... | collective-permute-start | bytes 3145736 | tf_op jit(solution)/shard_map/ppermute | solution.py:272
  45.6 35.9 %collective-permute-start = (bf16[256,2048]{1,0:T(8,128)(2,1)}, bf16[256,2048]{1,0:T(8,128)(2,1)}, u32[]{:S(2)}, u32[]{:S(2)}) collective-permute-start(bf16[256,2048]{1,0:T(8,128)(2,1)} %fusion.21), channel_id=1, source_target_pairs={{0,1},{1,0},{2,3},{3,2},{4,5},{5,4},{6,7},{7,6},{8,9},{9,8},{10,11... | collective-permute-start | bytes 3145736 | tf_op jit(solution)/shard_map/ppermute | solution.py:289
  46.7 30.1 %collective-permute-start.8 = (bf16[64,2048]{1,0:T(8,128)(2,1)S(1)}, bf16[64,2048]{1,0:T(8,128)(2,1)S(1)}, u32[]{:S(2)}, u32[]{:S(2)}) collective-permute-start(bf16[64,2048]{1,0:T(8,128)(2,1)S(1)} %convert_element_type.185), channel_id=1, source_target_pairs={{8,16},{10,18},{12,20},{14,22},{16,8},{18,10},{20,12},{22,14},{9,1... | collective-permute-start | bytes 786440 | tf_op jit(solution)/shard_map/ppermute | solution.py:272
  66.6 14.9 %collective-permute-start.2 = (bf16[256,2048]{1,0:T(8,128)(2,1)}, bf16[256,2048]{1,0:T(8,128)(2,1)}, u32[]{:S(2)}, u32[]{:S(2)}) collective-permute-start(bf16[256,2048]{1,0:T(8,128)(2,1)} %collective-permute-done.1), channel_id=1, source_target_pairs={{0,1},{1,0},{2,3},{3,2},{4,5},{5,4},{6,7},{7,6},{8,9},{9,8},{10,11... | collective-permute-start | bytes 3145736 | tf_op jit(solution)/shard_map/ppermute | solution.py:289
  66.6 84.8 %copy-start.62 = (f32[1024]{0:T(1024)}, f32[1024]{0:T(1024)S(1)}, u32[]{:S(2)}) copy-start(f32[1024]{0:T(1024)S(1)} %add_convert_fusion.2) | copy-start | bytes 12292
  67.9 10.0 %collective-permute-start.9 = (bf16[64,2048]{1,0:T(8,128)(2,1)S(1)}, bf16[64,2048]{1,0:T(8,128)(2,1)S(1)}, u32[]{:S(2)}, u32[]{:S(2)}) collective-permute-start(bf16[64,2048]{1,0:T(8,128)(2,1)S(1)} %convert_element_type.185), channel_id=1, source_target_pairs={{0,16},{2,18},{4,20},{6,22},{8,0},{10,2},{12,4},{14,6},{16,24},{18... | collective-permute-start | bytes 786440 | tf_op jit(solution)/shard_map/ppermute | solution.py:272
  75.0 65.5 %collective-permute-start.18 = (bf16[128,2816]{1,0:T(8,128)(2,1)}, bf16[128,2816]{1,0:T(8,128)(2,1)}, u32[]{:S(2)}, u32[]{:S(2)}) collective-permute-start(bf16[128,2816]{1,0:T(8,128)(2,1)} %get-tuple-element.77), channel_id=1, source_target_pairs={{0,24},{2,26},{4,28},{6,30},{8,16},{10,18},{12,20},{14,22},{16,8},... | collective-permute-start | bytes 2162696 | tf_op jit(solution)/shard_map/ppermute | solution.py:272
  76.8 63.6 %collective-permute-start.16 = (bf16[128,2816]{1,0:T(8,128)(2,1)}, bf16[128,2816]{1,0:T(8,128)(2,1)}, u32[]{:S(2)}, u32[]{:S(2)}) collective-permute-start(bf16[128,2816]{1,0:T(8,128)(2,1)} %get-tuple-element.77), channel_id=1, source_target_pairs={{0,8},{2,10},{4,12},{6,14},{8,0},{10,2},{12,4},{14,6},{16,24},{18,... | collective-permute-start | bytes 2162696 | tf_op jit(solution)/shard_map/ppermute | solution.py:272
  77.9 62.5 %collective-permute-start.17 = (bf16[128,2816]{1,0:T(8,128)(2,1)}, bf16[128,2816]{1,0:T(8,128)(2,1)}, u32[]{:S(2)}, u32[]{:S(2)}) collective-permute-start(bf16[128,2816]{1,0:T(8,128)(2,1)} %get-tuple-element.78), channel_id=1, source_target_pairs={{0,16},{2,18},{4,20},{6,22},{8,24},{10,26},{12,28},{14,30},{16,0},... | collective-permute-start | bytes 2162696 | tf_op jit(solution)/shard_map/ppermute | solution.py:272
  81.4 191.2 %all-gather.9.cloned.1.call-start = ((), (), s32[]{:S(2)}) async-start(), calls=%async_computation.9 | async-start | bytes 14417920 | tf_op jit(solution)/shard_map/all_gather | solution.py:298
  88.5 53.3 %copy-start.35 = (f32[1024,640]{0,1:T(8,128)}, f32[1024,640]{0,1:T(8,128)S(1)}, u32[]{:S(2)}) copy-start(f32[1024,640]{0,1:T(8,128)S(1)} %get-tuple-element.189) | copy-start | bytes 7864324
  90.7 63.9 %copy-start.22 = (bf16[1024,8,32]{0,2,1:T(8,128)(2,1)}, bf16[1024,8,32]{0,2,1:T(8,128)(2,1)S(1)}, u32[]{:S(2)}) copy-start(bf16[1024,8,32]{0,2,1:T(8,128)(2,1)S(1)} %get-tuple-element.145) | copy-start | bytes 1572868
  145.3 180.2 %all-gather.11.cloned.1.call-start = ((), (), s32[]{:S(2)}) async-start(), calls=%async_computation.10 | async-start | bytes 7208960 | tf_op jit(solution)/shard_map/all_gather | solution.py:298
  145.8 3.7 collective-permute-start.7
  170.0 6.3 collective-permute-start.11
  172.8 5.1 collective-permute-start.23
  174.3 19.5 %collective-permute-start.22 = (bf16[176,2048]{1,0:T(8,128)(2,1)}, bf16[176,2048]{1,0:T(8,128)(2,1)}, u32[]{:S(2)}, u32[]{:S(2)}) collective-permute-start(bf16[176,2048]{1,0:T(8,128)(2,1)} %convert_element_type.194), channel_id=1, source_target_pairs={{0,16},{2,18},{4,20},{6,22},{8,0},{10,2},{12,4},{14,6},{16,24},{18... | collective-permute-start | bytes 2162696 | tf_op jit(solution)/shard_map/ppermute | solution.py:272
  176.3 18.9 %collective-permute-start.10 = (bf16[256,2048]{1,0:T(8,128)(2,1)}, bf16[256,2048]{1,0:T(8,128)(2,1)}, u32[]{:S(2)}, u32[]{:S(2)}) collective-permute-start(bf16[256,2048]{1,0:T(8,128)(2,1)} %get-tuple-element.141), channel_id=1, source_target_pairs={{0,1},{1,0},{2,3},{3,2},{4,5},{5,4},{6,7},{7,6},{8,9},{9,8},{10,11... | collective-permute-start | bytes 3145736 | tf_op jit(solution)/shard_map/ppermute | solution.py:289
  177.6 36.7 %collective-permute-start.12 = (bf16[256,2048]{1,0:T(8,128)(2,1)}, bf16[256,2048]{1,0:T(8,128)(2,1)}, u32[]{:S(2)}, u32[]{:S(2)}) collective-permute-start(bf16[256,2048]{1,0:T(8,128)(2,1)} %fusion.35), channel_id=1, source_target_pairs={{0,8},{2,10},{4,12},{6,14},{8,0},{10,2},{12,4},{14,6},{16,24},{18,... | collective-permute-start | bytes 3145736 | tf_op jit(solution)/shard_map/ppermute | solution.py:272
  219.9 26.4 %collective-permute-start.20 = (bf16[256,2048]{1,0:T(8,128)(2,1)}, bf16[256,2048]{1,0:T(8,128)(2,1)}, u32[]{:S(2)}, u32[]{:S(2)}) collective-permute-start(bf16[256,2048]{1,0:T(8,128)(2,1)} %param.29), channel_id=1, source_target_pairs={{0,8},{2,10},{4,12},{6,14},{8,0},{10,2},{12,4},{14,6},{16,24},{18,... | collective-permute-start | bytes 3145736 | tf_op jit(solution)/shard_map/ppermute | solution.py:272
  224.7 232.2 %reduce-scatter.6.cloned.1.call-start = ((), (), s32[]{:S(2)}) async-start(), calls=%async_computation.11 | async-start | bytes 7208960 | tf_op jit(solution)/shard_map/reduce_scatter | solution.py:301
  224.7 41.5 %collective-permute-start.14 = (bf16[256,2048]{1,0:T(8,128)(2,1)}, bf16[256,2048]{1,0:T(8,128)(2,1)S(1)}, u32[]{:S(2)}, u32[]{:S(2)}) collective-permute-start(bf16[256,2048]{1,0:T(8,128)(2,1)} %multiply_convert_fusion.3), channel_id=1, source_target_pairs={{0,8},{2,10},{4,12},{6,14},{8,0},{10,2},{12,4},{14,6},{16,24},{18,... | collective-permute-start | bytes 3145736 | tf_op jit(solution)/shard_map/ppermute | solution.py:272
  224.8 43.3 %collective-permute-start.19 = (bf16[256,2048]{1,0:T(8,128)(2,1)}, bf16[256,2048]{1,0:T(8,128)(2,1)S(1)}, u32[]{:S(2)}, u32[]{:S(2)}) collective-permute-start(bf16[256,2048]{1,0:T(8,128)(2,1)} %param.29), channel_id=1, source_target_pairs={{0,1},{1,0},{2,3},{3,2},{4,5},{5,4},{6,7},{7,6},{8,9},{9,8},{10,11... | collective-permute-start | bytes 3145736 | tf_op jit(solution)/shard_map/ppermute | solution.py:289
  246.3 23.2 %collective-permute-start.21 = (bf16[256,2048]{1,0:T(8,128)(2,1)}, bf16[256,2048]{1,0:T(8,128)(2,1)S(1)}, u32[]{:S(2)}, u32[]{:S(2)}) collective-permute-start(bf16[256,2048]{1,0:T(8,128)(2,1)} %collective-permute-done.20), channel_id=1, source_target_pairs={{0,1},{1,0},{2,3},{3,2},{4,5},{5,4},{6,7},{7,6},{8,9},{9,8},{10,11... | collective-permute-start | bytes 3145736 | tf_op jit(solution)/shard_map/ppermute | solution.py:289
  246.3 23.3 %collective-permute-start.13 = (bf16[256,2048]{1,0:T(8,128)(2,1)}, bf16[256,2048]{1,0:T(8,128)(2,1)S(1)}, u32[]{:S(2)}, u32[]{:S(2)}) collective-permute-start(bf16[256,2048]{1,0:T(8,128)(2,1)} %multiply_convert_fusion.3), channel_id=1, source_target_pairs={{0,1},{1,0},{2,3},{3,2},{4,5},{5,4},{6,7},{7,6},{8,9},{9,8},{10,11... | collective-permute-start | bytes 3145736 | tf_op jit(solution)/shard_map/ppermute | solution.py:289
  266.2 6.4 collective-permute-start.15
  305.0 195.7 %reduce-scatter.8.cloned.1.call-start = ((), (), s32[]{:S(2)}) async-start(), calls=%async_computation.12 | async-start | bytes 7208960 | tf_op jit(solution)/shard_map/reduce_scatter | solution.py:301
  351.7 180.0 %reduce-scatter.10.cloned.1.call-start = ((), (), s32[]{:S(2)}) async-start(), calls=%async_computation.13 | async-start | bytes 7208960 | tf_op jit(solution)/shard_map/reduce_scatter | solution.py:301
  367.6 202.8 %reduce-scatter.14.cloned.1.call-start = ((), (), s32[]{:S(2)}) async-start(), calls=%async_computation.15 | async-start | bytes 2621440 | tf_op jit(solution)/shard_map/reduce_scatter | solution.py:301
  388.1 2.7 collective-permute-start.25
  388.2 4.5 collective-permute-start.24
  391.1 25.3 %collective-permute-start.26 = (bf16[256,2048]{1,0:T(8,128)(2,1)S(1)}, bf16[256,2048]{1,0:T(8,128)(2,1)S(1)}, u32[]{:S(2)}, u32[]{:S(2)}) collective-permute-start(bf16[256,2048]{1,0:T(8,128)(2,1)S(1)} %fusion.33), channel_id=1, source_target_pairs={{0,8},{2,10},{4,12},{6,14},{8,0},{10,2},{12,4},{14,6},{16,24},{18,... | collective-permute-start | bytes 3145736 | tf_op jit(solution)/shard_map/ppermute | solution.py:272
  421.3 24.5 %collective-permute-start.31 = (bf16[256,2048]{1,0:T(8,128)(2,1)S(1)}, bf16[256,2048]{1,0:T(8,128)(2,1)S(1)}, u32[]{:S(2)}, u32[]{:S(2)}) collective-permute-start(bf16[256,2048]{1,0:T(8,128)(2,1)S(1)} %get-tuple-element.129), channel_id=1, source_target_pairs={{0,8},{2,10},{4,12},{6,14},{8,0},{10,2},{12,4},{14,6},{16,24},{18,... | collective-permute-start | bytes 3145736 | tf_op jit(solution)/shard_map/ppermute | solution.py:272
  432.9 13.7 %collective-permute-start.28 = (bf16[256,2048]{1,0:T(8,128)(2,1)S(1)}, bf16[256,2048]{1,0:T(8,128)(2,1)S(1)}, u32[]{:S(2)}, u32[]{:S(2)}) collective-permute-start(bf16[256,2048]{1,0:T(8,128)(2,1)S(1)} %get-tuple-element.138), channel_id=1, source_target_pairs={{0,1},{1,0},{2,3},{3,2},{4,5},{5,4},{6,7},{7,6},{8,9},{9,8},{10,11... | collective-permute-start | bytes 3145736 | tf_op jit(solution)/shard_map/ppermute | solution.py:289
  432.9 16.4 %collective-permute-start.30 = (bf16[256,2048]{1,0:T(8,128)(2,1)S(1)}, bf16[256,2048]{1,0:T(8,128)(2,1)S(1)}, u32[]{:S(2)}, u32[]{:S(2)}) collective-permute-start(bf16[256,2048]{1,0:T(8,128)(2,1)S(1)} %get-tuple-element.129), channel_id=1, source_target_pairs={{0,1},{1,0},{2,3},{3,2},{4,5},{5,4},{6,7},{7,6},{8,9},{9,8},{10,11... | collective-permute-start | bytes 3145736 | tf_op jit(solution)/shard_map/ppermute | solution.py:289
  445.8 3.6 collective-permute-start.32
  446.0 125.7 %collective-permute-start.27 = (bf16[256,2048]{1,0:T(8,128)(2,1)}, bf16[256,2048]{1,0:T(8,128)(2,1)}, u32[]{:S(2)}, u32[]{:S(2)}) collective-permute-start(bf16[256,2048]{1,0:T(8,128)(2,1)} %get-tuple-element.137), channel_id=1, source_target_pairs={{0,1},{1,0},{2,3},{3,2},{4,5},{5,4},{6,7},{7,6},{8,9},{9,8},{10,11... | collective-permute-start | bytes 3145736 | tf_op jit(solution)/shard_map/ppermute | solution.py:289
  447.8 126.3 %collective-permute-start.29 = (bf16[256,2048]{1,0:T(8,128)(2,1)}, bf16[256,2048]{1,0:T(8,128)(2,1)}, u32[]{:S(2)}, u32[]{:S(2)}) collective-permute-start(bf16[256,2048]{1,0:T(8,128)(2,1)} %fusion.29), channel_id=1, source_target_pairs={{0,8},{2,10},{4,12},{6,14},{8,0},{10,2},{12,4},{14,6},{16,24},{18,... | collective-permute-start | bytes 3145736 | tf_op jit(solution)/shard_map/ppermute | solution.py:272
  452.9 213.2 %reduce-scatter.12.cloned.1.call-start = ((), (), s32[]{:S(2)}) async-start(), calls=%async_computation.14 | async-start | bytes 3276800 | tf_op jit(solution)/shard_map/reduce_scatter | solution.py:301
  459.3 49.1 %collective-permute-start.33 = (bf16[176,2048]{1,0:T(8,128)(2,1)}, bf16[176,2048]{1,0:T(8,128)(2,1)}, u32[]{:S(2)}, u32[]{:S(2)}) collective-permute-start(bf16[176,2048]{1,0:T(8,128)(2,1)} %get-tuple-element.155), channel_id=1, source_target_pairs={{0,8},{2,10},{4,12},{6,14},{8,24},{10,26},{12,28},{14,30},{16,0},{... | collective-permute-start | bytes 2162696 | tf_op jit(solution)/shard_map/ppermute | solution.py:272
  459.9 48.6 %collective-permute-start.34 = (bf16[176,2048]{1,0:T(8,128)(2,1)}, bf16[176,2048]{1,0:T(8,128)(2,1)}, u32[]{:S(2)}, u32[]{:S(2)}) collective-permute-start(bf16[176,2048]{1,0:T(8,128)(2,1)} %get-tuple-element.156), channel_id=1, source_target_pairs={{8,16},{10,18},{12,20},{14,22},{16,8},{18,10},{20,12},{22,14},{9,1... | collective-permute-start | bytes 2162696 | tf_op jit(solution)/shard_map/ppermute | solution.py:272
  542.5 33.2 %collective-permute-start.36 = (bf16[256,2048]{1,0:T(8,128)(2,1)}, bf16[256,2048]{1,0:T(8,128)(2,1)}, u32[]{:S(2)}, u32[]{:S(2)}) collective-permute-start(bf16[256,2048]{1,0:T(8,128)(2,1)} %get-tuple-element.136), channel_id=1, source_target_pairs={{0,1},{1,0},{2,3},{3,2},{4,5},{5,4},{6,7},{7,6},{8,9},{9,8},{10,11... | collective-permute-start | bytes 3145736 | tf_op jit(solution)/shard_map/ppermute | solution.py:289
  544.9 33.0 %collective-permute-start.45 = (bf16[128,1408]{1,0:T(8,128)(2,1)}, bf16[128,1408]{1,0:T(8,128)(2,1)}, u32[]{:S(2)}, u32[]{:S(2)}) collective-permute-start(bf16[128,1408]{1,0:T(8,128)(2,1)} %get-tuple-element.151), channel_id=1, source_target_pairs={{0,24},{2,26},{4,28},{6,30},{8,16},{10,18},{12,20},{14,22},{16,8},... | collective-permute-start | bytes 1081352 | tf_op jit(solution)/shard_map/ppermute | solution.py:272
  548.2 32.6 %collective-permute-start.44 = (bf16[128,1408]{1,0:T(8,128)(2,1)}, bf16[128,1408]{1,0:T(8,128)(2,1)}, u32[]{:S(2)}, u32[]{:S(2)}) collective-permute-start(bf16[128,1408]{1,0:T(8,128)(2,1)} %get-tuple-element.152), channel_id=1, source_target_pairs={{0,8},{2,10},{4,12},{6,14},{8,0},{10,2},{12,4},{14,6},{16,24},{18,... | collective-permute-start | bytes 1081352 | tf_op jit(solution)/shard_map/ppermute | solution.py:272
  571.7 29.0 %collective-permute-start.43 = (bf16[128,1408]{1,0:T(8,128)(2,1)}, bf16[128,1408]{1,0:T(8,128)(2,1)S(1)}, u32[]{:S(2)}, u32[]{:S(2)}) collective-permute-start(bf16[128,1408]{1,0:T(8,128)(2,1)} %get-tuple-element.153), channel_id=1, source_target_pairs={{0,16},{2,18},{4,20},{6,22},{8,24},{10,26},{12,28},{14,30},{16,0},... | collective-permute-start | bytes 1081352 | tf_op jit(solution)/shard_map/ppermute | solution.py:272
  574.2 27.2 %collective-permute-start.48 = (bf16[128,1408]{1,0:T(8,128)(2,1)}, bf16[128,1408]{1,0:T(8,128)(2,1)S(1)}, u32[]{:S(2)}, u32[]{:S(2)}) collective-permute-start(bf16[128,1408]{1,0:T(8,128)(2,1)} %get-tuple-element.147), channel_id=1, source_target_pairs={{0,24},{2,26},{4,28},{6,30},{8,16},{10,18},{12,20},{14,22},{16,8},... | collective-permute-start | bytes 1081352 | tf_op jit(solution)/shard_map/ppermute | solution.py:272
  575.6 25.8 %collective-permute-start.47 = (bf16[128,1408]{1,0:T(8,128)(2,1)}, bf16[128,1408]{1,0:T(8,128)(2,1)S(1)}, u32[]{:S(2)}, u32[]{:S(2)}) collective-permute-start(bf16[128,1408]{1,0:T(8,128)(2,1)} %get-tuple-element.148), channel_id=1, source_target_pairs={{0,8},{2,10},{4,12},{6,14},{8,0},{10,2},{12,4},{14,6},{16,24},{18,... | collective-permute-start | bytes 1081352 | tf_op jit(solution)/shard_map/ppermute | solution.py:272
  577.9 44.9 %collective-permute-start.46 = (bf16[128,1408]{1,0:T(8,128)(2,1)S(1)}, bf16[128,1408]{1,0:T(8,128)(2,1)S(1)}, u32[]{:S(2)}, u32[]{:S(2)}) collective-permute-start(bf16[128,1408]{1,0:T(8,128)(2,1)S(1)} %copy-done.57), channel_id=1, source_target_pairs={{0,16},{2,18},{4,20},{6,22},{8,24},{10,26},{12,28},{14,30},{16,0},... | collective-permute-start | bytes 1081352 | tf_op jit(solution)/shard_map/ppermute | solution.py:272
  580.8 54.7 %collective-permute-start.41 = (bf16[64,2048]{1,0:T(8,128)(2,1)S(1)}, bf16[64,2048]{1,0:T(8,128)(2,1)S(1)}, u32[]{:S(2)}, u32[]{:S(2)}) collective-permute-start(bf16[64,2048]{1,0:T(8,128)(2,1)S(1)} %get-tuple-element.167), channel_id=1, source_target_pairs={{0,8},{2,10},{4,12},{6,14},{8,24},{10,26},{12,28},{14,30},{16,0},{... | collective-permute-start | bytes 786440 | tf_op jit(solution)/shard_map/ppermute | solution.py:272
  600.7 34.9 %collective-permute-start.42 = (bf16[64,2048]{1,0:T(8,128)(2,1)S(1)}, bf16[64,2048]{1,0:T(8,128)(2,1)S(1)}, u32[]{:S(2)}, u32[]{:S(2)}) collective-permute-start(bf16[64,2048]{1,0:T(8,128)(2,1)S(1)} %get-tuple-element.168), channel_id=1, source_target_pairs={{8,16},{10,18},{12,20},{14,22},{16,8},{18,10},{20,12},{22,14},{9,1... | collective-permute-start | bytes 786440 | tf_op jit(solution)/shard_map/ppermute | solution.py:272
  601.4 36.0 %collective-permute-start.35 = (bf16[256,2048]{1,0:T(8,128)(2,1)S(1)}, bf16[256,2048]{1,0:T(8,128)(2,1)S(1)}, u32[]{:S(2)}, u32[]{:S(2)}) collective-permute-start(bf16[256,2048]{1,0:T(8,128)(2,1)S(1)} %copy-done.40), channel_id=1, source_target_pairs={{0,1},{1,0},{2,3},{3,2},{4,5},{5,4},{6,7},{7,6},{8,9},{9,8},{10,11... | collective-permute-start | bytes 3145736 | tf_op jit(solution)/shard_map/ppermute | solution.py:289
  601.5 48.3 %collective-permute-start.37 = (bf16[256,2048]{1,0:T(8,128)(2,1)S(1)}, bf16[256,2048]{1,0:T(8,128)(2,1)S(1)}, u32[]{:S(2)}, u32[]{:S(2)}) collective-permute-start(bf16[256,2048]{1,0:T(8,128)(2,1)S(1)} %fusion.27), channel_id=1, source_target_pairs={{0,8},{2,10},{4,12},{6,14},{8,0},{10,2},{12,4},{14,6},{16,24},{18,... | collective-permute-start | bytes 3145736 | tf_op jit(solution)/shard_map/ppermute | solution.py:272
  653.7 11.6 %all-to-all-start.1 = ((f32[32,1,128]{2,1,0:T(1,128)}), f32[32,1,128]{2,1,0:T(1,128)S(1)}, u32[]{:S(2)}, u32[]{:S(2)}) async-start(f32[32,1,128]{2,1,0:T(1,128)} %reshape.693), calls=%async_computation.6 | async-start | bytes 32768 | tf_op jit(solution)/shard_map/all_to_all | solution.py:578
  667.4 8.9 %collective-permute-start.40 = (bf16[128,640]{1,0:T(8,128)(2,1)S(1)}, bf16[128,640]{1,0:T(8,128)(2,1)S(1)}, u32[]{:S(2)}, u32[]{:S(2)}) collective-permute-start(bf16[128,640]{1,0:T(8,128)(2,1)S(1)} %get-tuple-element.163), channel_id=1, source_target_pairs={{0,24},{2,26},{4,28},{6,30},{8,16},{10,18},{12,20},{14,22},{16,8},... | collective-permute-start | bytes 491528 | tf_op jit(solution)/shard_map/ppermute | solution.py:272
  669.7 10.9 %collective-permute-start.39 = (bf16[128,640]{1,0:T(8,128)(2,1)S(1)}, bf16[128,640]{1,0:T(8,128)(2,1)S(1)}, u32[]{:S(2)}, u32[]{:S(2)}) collective-permute-start(bf16[128,640]{1,0:T(8,128)(2,1)S(1)} %get-tuple-element.164), channel_id=1, source_target_pairs={{0,8},{2,10},{4,12},{6,14},{8,0},{10,2},{12,4},{14,6},{16,24},{18,... | collective-permute-start | bytes 491528 | tf_op jit(solution)/shard_map/ppermute | solution.py:272
  669.7 14.4 %collective-permute-start.38 = (bf16[128,640]{1,0:T(8,128)(2,1)S(1)}, bf16[128,640]{1,0:T(8,128)(2,1)S(1)}, u32[]{:S(2)}, u32[]{:S(2)}) collective-permute-start(bf16[128,640]{1,0:T(8,128)(2,1)S(1)} %get-tuple-element.165), channel_id=1, source_target_pairs={{0,16},{2,18},{4,20},{6,22},{8,24},{10,26},{12,28},{14,30},{16,0},... | collective-permute-start | bytes 491528 | tf_op jit(solution)/shard_map/ppermute | solution.py:272
  (90 other events, 1038.8 us)
Sparse Core Ops, SparseCore 0:
  41.2 37.5 all-gather.4
  81.5 34.9 all-gather.6
  145.4 111.9 all-gather.8
  259.7 65.7 all-gather.10
  328.3 65.8 reduce-scatter.5
  397.0 65.8 reduce-scatter.7
  465.8 65.8 reduce-scatter.9
  535.2 35.1 reduce-scatter.13
  573.7 39.5 reduce-scatter.11

commit v2 on v1

--- a/solution.py
+++ b/solution.py
@@ -75,74 +75,99 @@
     return (weight_new, moment_new, second_new, shadow_new)
 
 
-def cast_halves(weight, pair_bit):
+def chunks_of(width):
+    first = width // 256 * 128
+    return ((0, first), (first, width - first))
+
+
+def cast_chunks(weight, pair_bit):
     row_count, planes, columns = weight.shape
     half = columns // 2
-
-    def kernel(bit_ref, weight_ref, keep_ref, send_ref):
-        for plane in range(planes):
-            low = weight_ref[:, plane, :half].astype(jnp.bfloat16)
-            high = weight_ref[:, plane, half:].astype(jnp.bfloat16)
-            at = pl.ds(plane * half, half)
-
-            @pl.when(bit_ref[0] == 0)
-            def _():
-                keep_ref[:, at] = low
-                send_ref[:, at] = high
-
-            @pl.when(bit_ref[0] != 0)
-            def _():
-                keep_ref[:, at] = high
-                send_ref[:, at] = low
-
-    out = jax.ShapeDtypeStruct((row_count, planes * half), jnp.bfloat16)
-    step = 16
-    return pl.pallas_call(
+    chunks = chunks_of(half)
+
+    def kernel(bit_ref, weight_ref, keep_ref, send_ref, last_ref):
+        mine = bit_ref[0] == 0
+        for number, (start, width) in enumerate(chunks):
+            for plane in range(planes):
+                low, high = [
+                    weight_ref[:, plane, pl.ds(side * half + start, width)].astype(jnp.bfloat16)
+                    for side in range(2)
+                ]
+                at = pl.ds(plane * width, width)
+                if number == 0:
+                    keep_ref[:, at] = jnp.where(mine, low, high)
+                    send_ref[:, at] = jnp.where(mine, high, low)
+                else:
+                    for outer in range(2):
+                        last_ref[2 * outer, :, at] = low
+                        last_ref[2 * outer + 1, :, at] = high
+
+    first, last = [planes * width for _, width in chunks]
+    step = 32
+    rows = pl.BlockSpec((step, first), lambda i, bit: (i, 0))
+    keep, send, blocks = pl.pallas_call(
         kernel,
         grid_spec=pltpu.PrefetchScalarGridSpec(
             num_scalar_prefetch=1,
             grid=(row_count // step,),
             in_specs=[pl.BlockSpec((step, planes, columns), lambda i, bit: (i, 0, 0))],
-            out_specs=[pl.BlockSpec((step, planes * half), lambda i, bit: (i, 0))] * 2,
+            out_specs=[rows, rows, pl.BlockSpec((4, step, last), lambda i, bit: (0, i, 0))],
         ),
-        out_shape=(out, out),
+        out_shape=[
+            jax.ShapeDtypeStruct((row_count, first), jnp.bfloat16),
+            jax.ShapeDtypeStruct((row_count, first), jnp.bfloat16),
+            jax.ShapeDtypeStruct((4, row_count, last), jnp.bfloat16),
+        ],
         compiler_params=pltpu.CompilerParams(vmem_limit_bytes=32 * 2**20),
     )(pair_bit.reshape(1), weight)
-
-
-def cast_projections(query, keyval, pair_bit):
+    return (keep, send), blocks
+
+
+def join_low(blocks, low_index):
+    parts, rows, columns = blocks[0].shape
+    count = len(blocks)
+
+    def kernel(low_ref, *refs):
+        for flip in range(count):
+            refs[count][0, low_ref[0] ^ flip] = refs[flip][0]
+
+    return pl.pallas_call(
+        kernel,
+        grid_spec=pltpu.PrefetchScalarGridSpec(
+            num_scalar_prefetch=1,
+            grid=(parts,),
+            in_specs=[pl.BlockSpec((1, rows, columns), lambda i, low: (i, 0, 0))] * count,
+            out_specs=pl.BlockSpec((1, count, rows, columns), lambda i, low: (i, 0, 0, 0)),
+        ),
+        out_shape=jax.ShapeDtypeStruct((parts, count, rows, columns), blocks[0].dtype),
+        compiler_params=pltpu.CompilerParams(vmem_limit_bytes=32 * 2**20),
+    )(low_index.reshape(1), *blocks)
+
+
+def cast_projections(query, keyval):
     row_count, columns = query.shape
     half, width = columns // 2, keyval.shape[2]
 
-    def kernel(bit_ref, query_ref, keyval_ref, keep_ref, send_ref):
+    def kernel(query_ref, keyval_ref, out_ref):
         left = lax.broadcasted_iota(jnp.int32, (row_count, width), 1) < width // 2
         key, value = keyval_ref[:, 0, :], keyval_ref[:, 1, :]
-        low = jnp.where(left, key, pltpu.roll(value, width // 2, 1)).astype(jnp.bfloat16)
-        high = jnp.where(left, pltpu.roll(key, width // 2, 1), value).astype(jnp.bfloat16)
-
-        def store(low_ref, high_ref):
-            low_ref[:, :half] = query_ref[:, :half].astype(jnp.bfloat16)
-            high_ref[:, :half] = query_ref[:, half:].astype(jnp.bfloat16)
-            low_ref[:, half:] = low
-            high_ref[:, half:] = high
-
-        @pl.when(bit_ref[0] == 0)
-        def _():
-            store(keep_ref, send_ref)
-
-        @pl.when(bit_ref[0] != 0)
-        def _():
-            store(send_ref, keep_ref)
-
-    out = jax.ShapeDtypeStruct((row_count, half + width), jnp.bfloat16)
+        pairs = (
+            jnp.where(left, key, pltpu.roll(value, width // 2, 1)).astype(jnp.bfloat16),
+            jnp.where(left, pltpu.roll(key, width // 2, 1), value).astype(jnp.bfloat16),
+        )
+        for place in range(4):
+            side = place % 2
+            part = query_ref[:, pl.ds(side * half, half)]
+            out_ref[place, :, :half] = part.astype(jnp.bfloat16)
+            out_ref[place, :, half:] = pairs[side]
+
     return pl.pallas_call(
         kernel,
-        in_specs=[pl.BlockSpec(memory_space=pltpu.SMEM)]
-        + [pl.BlockSpec(memory_space=pltpu.VMEM)] * 2,
-        out_specs=[pl.BlockSpec(memory_space=pltpu.VMEM)] * 2,
-        out_shape=(out, out),
+        in_specs=[pl.BlockSpec(memory_space=pltpu.VMEM)] * 2,
+        out_specs=pl.BlockSpec(memory_space=pltpu.VMEM),
+        out_shape=jax.ShapeDtypeStruct((4, row_count, half + width), jnp.bfloat16),
         compiler_params=pltpu.CompilerParams(vmem_limit_bytes=16 * 2**20),
-    )(pair_bit.reshape(1), query, keyval)
+    )(query, keyval)
 
 
 def projection_update(parts, pair_bit, queries, keyvals):
@@ -186,46 +211,45 @@
     return results[:4], results[4:]
 
 
-def expand_update(parts, pair_bit, weight, moment, second, shadow):
-    row_count, planes, columns = weight.shape
+def expand_update(parts, olds):
+    row_count, planes, columns = olds[0].shape
     half = columns // 2
+    chunks = chunks_of(half)
     step = 16
 
-    def kernel(bit_ref, *refs):
-        parts, olds, news = refs[:8], refs[8:12], refs[12:]
-        for plane in range(planes):
-            one, two, three, four = [
-                ref[...].astype(jnp.float32) for ref in parts[plane * 4 : plane * 4 + 4]
-            ]
-            own, other = one + two, three + four
-            mine = bit_ref[0] == 0
-            for side, grad in (
-                (0, jnp.where(mine, own, other)),
-                (1, jnp.where(mine, other, own)),
-            ):
-                where = (slice(None), plane, pl.ds(side * half, half))
-                results = adamw(
-                    grad, *[ref[where] for ref in olds], MATRIX_RATE, WEIGHT_DECAY, EMA_KEEP
-                )
-                for ref, result in zip(news, results):
-                    ref[where] = result
+    def kernel(*refs):
+        part_refs, old_refs, new_refs = refs[:2], refs[2:6], refs[6:]
+        for (start, width), part_ref in zip(chunks, part_refs):
+            for plane in range(planes):
+                at = pl.ds(plane * width, width)
+                for side in range(2):
+                    where = (slice(None), plane, pl.ds(side * half + start, width))
+                    results = adamw(
+                        part_ref[side, :, at].astype(jnp.float32)
+                        + part_ref[side + 2, :, at].astype(jnp.float32),
+                        *[ref[where] for ref in old_refs],
+                        MATRIX_RATE,
+                        WEIGHT_DECAY,
+                        EMA_KEEP,
+                    )
+                    for ref, result in zip(new_refs, results):
+                        ref[where] = result
 
     def state_spec():
-        return pl.BlockSpec((step, planes, columns), lambda i, bit: (i, 0, 0))
-
-    out = jax.ShapeDtypeStruct(weight.shape, jnp.float32)
+        return pl.BlockSpec((step, planes, columns), lambda i: (i, 0, 0))
+
+    out = jax.ShapeDtypeStruct(olds[0].shape, jnp.float32)
     return pl.pallas_call(
         kernel,
-        grid_spec=pltpu.PrefetchScalarGridSpec(
-            num_scalar_prefetch=1,
-            grid=(row_count // step,),
-            in_specs=[pl.BlockSpec((step, half), lambda i, bit: (i, 0))] * 8
-            + [state_spec() for _ in range(4)],
-            out_specs=[state_spec() for _ in range(4)],
-        ),
+        grid=(row_count // step,),
+        in_specs=[
+            pl.BlockSpec((4, step, planes * width), lambda i: (0, i, 0)) for _, width in chunks
+        ]
+        + [state_spec() for _ in range(4)],
+        out_specs=[state_spec() for _ in range(4)],
         out_shape=(out,) * 4,
         compiler_params=pltpu.CompilerParams(vmem_limit_bytes=48 * 2**20),
-    )(pair_bit.reshape(1), *parts, weight, moment, second, shadow)
+    )(*parts, *olds)
 
 
 def per_device(
@@ -265,6 +289,7 @@
     dp_index = lax.axis_index("dp")
     outer_bit = dp_index // (2 * low_count)
     pair_bit = (dp_index // low_count) % 2
+    low_index = dp_index % low_count
     core_bit = lax.axis_index("tensor")
     low_groups = [[base * low_count + low for low in range(low_count)] for base in range(4)]
 
@@ -279,8 +304,20 @@
             ],
         )
 
+    place_groups = [
+        [place * low_count + low for place in range(4)] for low in range(low_count)
+    ]
+
+    def spread(blocks):
+        return lax.all_to_all(
+            blocks, "dp", split_axis=0, concat_axis=0, tiled=True, axis_index_groups=place_groups
+        )
+
     def swap(value, flip):
         return move(value, {place: place ^ flip for place in range(4)})
+
+    def swap_low(value, flip):
+        return lax.ppermute(value, "dp", [(index, index ^ flip) for index in range(dp_count)])
 
     def swap_pair(value):
         return swap(value, 1)
@@ -307,53 +344,106 @@
     def exchange_columns(keep, send):
         return keep, swap(send, 1), swap(keep, 2), swap(send, 3)
 
-    def gather_columns(keep, one, two, three):
+    def join_columns(keep, one, two, three):
         low_pair = [pick(pair_bit, keep, one), pick(pair_bit, one, keep)]
         high_pair = [pick(pair_bit, two, three), pick(pair_bit, three, two)]
-        quad = pick(outer_bit, jnp.stack(low_pair + high_pair), jnp.stack(high_pair + low_pair))
-        return gather_low(quad).reshape(model_width, keep.shape[-1])
+        return pick(outer_bit, jnp.stack(low_pair + high_pair), jnp.stack(high_pair + low_pair))
 
     def exchange_owned(rows):
         return rows, move(rows, {0: 2, 1: 0, 2: 3, 3: 1}), move(rows, {1: 2, 2: 1})
 
-    def gather_owned(rows, first, second):
+    def join_owned(rows, first, second):
         second = pick(outer_bit ^ pair_bit, rows, second)
-        both = pick(outer_bit, jnp.stack([second, first]), jnp.stack([first, second]))
-        return gather_low(both).reshape(2 * low_count * rows.shape[0], rows.shape[1])
+        return pick(outer_bit, jnp.stack([second, first]), jnp.stack([first, second]))
+
+    def flat(blocks):
+        return blocks.reshape(-1, blocks.shape[-1])
+
+    def exchange_low(blocks):
+        return [blocks] + [swap_low(blocks, flip) for flip in range(1, low_count)]
+
+    def gather_direct(moved):
+        return flat(join_low(moved, low_index))
+
+    def low_blocks(full, parts):
+        blocks = full.reshape(parts, low_count, -1, full.shape[1])
+        return [
+            lax.dynamic_index_in_dim(blocks, low_index ^ flip, 1, keepdims=False)
+            for flip in range(low_count)
+        ]
+
+    def sent_low(blocks):
+        return [swap_low(block, flip) if flip else block for flip, block in enumerate(blocks)]
+
+    def total_low(terms):
+        return sum(term.astype(fl_type) for term in terms).astype(bf_type)
+
+    def columns_moved(reduced):
+        place = 2 * outer_bit + pair_bit
+        kept, one, two, three = [
+            lax.dynamic_index_in_dim(reduced, place ^ flip, 0, keepdims=False) for flip in range(4)
+        ]
+        return kept, swap(two, 2), swap(one, 1), swap(three, 3)
 
     def gather_tokens(rows):
         away = swap_pair(rows)
         return jnp.concatenate([rows, swap_core(rows), away, swap_core(away)])
 
-    def scatter_tokens(partial):
+    def token_sums(partial, hold=()):
         own, across, away, far = jnp.split(partial, 4)
 
         def over_cores(mine, sent):
             return mine + swap_core(sent.astype(bf_type)).astype(fl_type)
 
-        moved = swap_pair(over_cores(away, far).astype(bf_type))
-        return over_cores(own, across) + moved.astype(fl_type)
-
-    qkv_keep, qkv_send = cast_projections(query_weight, keyval_weight, pair_bit)
-    other_lengths, other_valid = swap_pair(doc_lengths), swap_pair(token_valid)
-    qkv_moved = exchange_columns(qkv_keep, qkv_send)
-    gain_copies = jnp.broadcast_to(
-        after(norms_weight, qkv_keep)[None], (2 * dp_count,) + norms_weight.shape
-    )
-    gain_rows = lax.all_to_all(
-        gain_copies, ("dp", "tensor"), split_axis=0, concat_axis=0, tiled=True
-    )
-    gain_rows = gain_rows.transpose(1, 0, 2).reshape(2, model_width)
+        return over_cores(own, across), after(over_cores(away, far).astype(bf_type), *hold)
+
+    def scatter_tokens(partial, fill=lambda: (), hold=()):
+        kept, sent = token_sums(partial, hold)
+        return kept + after(swap_pair(sent), *fill()).astype(fl_type)
+
+    group_len = token_valid.shape[1]
+    doc_count = doc_lengths.shape[1]
+    gain_count = norms_weight.size
+    first_rows, last_blocks = cast_chunks(expand_weight, pair_bit)
+    first_moved = exchange_columns(*first_rows)
+    mixing_moved = exchange_owned(after(mixing_weight, first_rows[0]).astype(bf_type))
+    own_facts = jnp.concatenate(
+        [
+            norms_weight.reshape(-1),
+            doc_lengths[0].astype(fl_type),
+            token_valid[0].astype(fl_type),
+        ]
+    )
+    facts = lax.all_to_all(
+        jnp.broadcast_to(
+            own_facts[None], (2 * dp_count, own_facts.size)
+        ),
+        ("dp", "tensor"),
+        split_axis=0,
+        concat_axis=0,
+        tiled=True,
+    )
+    gain_rows = facts[:, :gain_count].reshape(2 * dp_count, 2, -1).transpose(1, 0, 2)
+    gain_rows = gain_rows.reshape(2, model_width)
+    partner = 2 * (dp_index ^ low_count) + core_bit
+    partner_facts = lax.dynamic_index_in_dim(facts, partner, 0, keepdims=False)[gain_count:]
+    partner_facts = partner_facts.astype(jnp.int32)
+    other_lengths, other_valid = partner_facts[:doc_count], partner_facts[doc_count:]
     input_rows = layer_input.astype(fl_type)
     normed = normalize(input_rows, gain_rows[0]).astype(bf_type)
     normed_all = gather_tokens(normed)
-    mixing_moved = exchange_owned(after(mixing_weight, normed).astype(bf_type))
-    expand_keep, expand_send = cast_halves(after(expand_weight, normed), pair_bit)
-    expand_moved = exchange_columns(expand_keep, expand_send)
-    contract_moved = exchange_owned(after(contract_weight, expand_send).astype(bf_type))
-    qkv_low = gather_columns(*after(qkv_moved, normed))
-    mixing_low = gather_owned(*mixing_moved)
-    group_len = token_valid.shape[1]
+    qkv_quad = spread(after(cast_projections(query_weight, keyval_weight), normed))
+    qkv_moved = exchange_low(after(qkv_quad, normed))
+    first_low = flat(gather_low(join_columns(*after(first_moved, normed))))
+    mixing_both = join_owned(*mixing_moved)
+    last_quad = spread(after(last_blocks, mixing_both, qkv_quad))
+    contract_moved = exchange_owned(after(contract_weight, last_quad).astype(bf_type))
+    qkv_low = gather_direct(after(qkv_moved, mixing_both))
+    mixing_low = gather_direct(exchange_low(after(mixing_both, qkv_low)))
+    last_low = flat(gather_low(after(last_quad, normed_all)))
+    contract_both = join_owned(*contract_moved)
+    contract_low = flat(gather_low(contract_both))
+    out_grad_all = gather_tokens(after(upstream, normed_all))
     places = (
         jnp.arange(group_len, dtype=jnp.int32) + core_bit * (group_len // 2)
     ) % group_len
@@ -365,7 +455,7 @@
         )
 
     position_one, allowed_one = layout(doc_lengths[0], ordered_valid(token_valid[0]), places)
-    position_two, allowed_two = layout(other_lengths[0], ordered_valid(other_valid[0]), places)
+    position_two, allowed_two = layout(other_lengths, ordered_valid(other_valid), places)
     allowed = (allowed_one, allowed_two)
     cosine_table, sine_table = rope_tables(
         jnp.concatenate([position_one, position_two]), HEAD_DIM
@@ -395,8 +485,6 @@
         .astype(bf_type)
     )
 
-    expand_low = gather_columns(*after(expand_moved, queries))
-    contract_low = gather_owned(*after(contract_moved, queries))
 
     def part(array, group_index, kv_index, heads):
         return array[
@@ -434,36 +522,42 @@
             )
         mixed_groups.append(jnp.concatenate(mixed_parts, axis=1))
     mixed = jnp.concatenate(mixed_groups).reshape(token_count, query_width).astype(bf_type)
-    attended = scatter_tokens(jnp.dot(mixed, mixing_low, preferred_element_type=fl_type))
+    attended = scatter_tokens(
+        jnp.dot(
+            after(mixed, contract_both, out_grad_all), mixing_low, preferred_element_type=fl_type
+        )
+    )
     middle = input_rows + attended
     normed_two = normalize(middle, gain_rows[1]).astype(bf_type)
     normed_two_all = gather_tokens(normed_two)
-    gate_up = jnp.dot(normed_two_all, expand_low, preferred_element_type=fl_type)
-    gate, up = gate_up[:, :hidden_width], gate_up[:, hidden_width:]
-    gate_sig = jax.nn.sigmoid(gate)
-    gate_act = gate * gate_sig
-    hidden = (gate_act * up).astype(bf_type)
+    def gated(rows, weights):
+        gate_up = jnp.dot(rows, weights, preferred_element_type=fl_type)
+        return jnp.split(gate_up, 2, axis=1)
+
+    gate_first, up_first = gated(normed_two_all, first_low)
+    gate_last, up_last = gated(after(normed_two_all, gate_first), last_low)
+    hidden = jnp.concatenate(
+        [
+            (jax.nn.silu(gate) * up).astype(bf_type)
+            for gate, up in ((gate_first, up_first), (gate_last, up_last))
+        ],
+        axis=1,
+    )
     out_grad = upstream.astype(fl_type)
-    out_grad_all = gather_tokens(after(upstream, normed_two))
 
     def reduce_columns(full):
         return scatter_low(full.reshape(4, low_count * own_rows, full.shape[1]))
 
-    def scatter_columns(reduced):
-        place = 2 * outer_bit + pair_bit
-        kept, one, two, three = [
-            lax.dynamic_index_in_dim(reduced, place ^ flip, 0, keepdims=False) for flip in range(4)
-        ]
-        return kept, swap(two, 2), swap(one, 1), swap(three, 3)
-
     def reduce_owned(full):
         return scatter_low(full.reshape(2, full.shape[0] // 2, full.shape[1]))
 
-    def scatter_owned(reduced):
+    def owned_sent(reduced):
+        rest = pick(outer_bit, reduced[0], reduced[1])
         first = move(pick(outer_bit, reduced[1], reduced[0]), {0: 1, 1: 3, 2: 0, 3: 2})
-        rest = pick(outer_bit, reduced[0], reduced[1])
-        second = pick(outer_bit ^ pair_bit, rest, move(rest, {1: 2, 2: 1}))
-        return first.astype(fl_type) + second.astype(fl_type)
+        return first, rest, move(rest, {1: 2, 2: 1})
+
+    def owned_total(first, rest, second):
+        return first.astype(fl_type) + pick(outer_bit ^ pair_bit, rest, second).astype(fl_type)
 
     contract_full = lax.dot_general(
         hidden, out_grad_all, CONTRACT_FIRST, preferred_element_type=fl_type
@@ -472,43 +566,56 @@
     hidden_grad = lax.dot_general(
         after(out_grad_all, contract_full), contract_low, CONTRACT_LAST, preferred_element_type=fl_type
     )
-    gate_grad = hidden_grad * up * gate_sig * (1.0 + gate * (1.0 - gate_sig))
-    up_grad = hidden_grad * gate_act
-    gate_grad, up_grad = gate_grad.astype(bf_type), up_grad.astype(bf_type)
-    gate_full = lax.dot_general(
-        normed_two_all, gate_grad, CONTRACT_FIRST, preferred_element_type=fl_type
+
+    def gated_grad(gate, up, grad):
+        gate_sig = jax.nn.sigmoid(gate)
+        gate_grad = grad * up * gate_sig * (1.0 + gate * (1.0 - gate_sig))
+        up_grad = grad * (gate * gate_sig)
+        return jnp.concatenate([gate_grad.astype(bf_type), up_grad.astype(bf_type)], axis=1)
+
+    first_width = first_low.shape[1] // 2
+    first_grad = gated_grad(gate_first, up_first, hidden_grad[:, :first_width])
+    last_grad = gated_grad(gate_last, up_last, hidden_grad[:, first_width:])
+    last_full = lax.dot_general(
+        normed_two_all, last_grad, CONTRACT_FIRST, preferred_element_type=fl_type
     ).astype(bf_type)
-    up_full = lax.dot_general(
-        after(normed_two_all, gate_full), up_grad, CONTRACT_FIRST, preferred_element_type=fl_type
+    first_full = lax.dot_general(
+        after(normed_two_all, last_full),
+        first_grad,
+        CONTRACT_FIRST,
+        preferred_element_type=fl_type,
     ).astype(bf_type)
-    gate_reduced, up_reduced = reduce_columns(gate_full), reduce_columns(up_full)
-    gate_up_grad = after(jnp.concatenate([gate_grad, up_grad], axis=1), up_full)
-    normed_two_grad = scatter_tokens(
-        lax.dot_general(gate_up_grad, expand_low, CONTRACT_LAST, preferred_element_type=fl_type)
-    )
+    last_reduced, first_reduced = reduce_columns(last_full), reduce_columns(first_full)
+    normed_two_partial = lax.dot_general(
+        after(last_grad, first_full), last_low, CONTRACT_LAST, preferred_element_type=fl_type
+    ) + lax.dot_general(first_grad, first_low, CONTRACT_LAST, preferred_element_type=fl_type)
+    branch_partial = jnp.dot(
+        after(hidden, normed_two_partial), contract_low, preferred_element_type=fl_type
+    )
+    normed_two_grad = scatter_tokens(normed_two_partial, lambda: (branch_partial,))
     middle_pull = jax.vjp(normalize, middle, gain_rows[1])[1]
     middle_part, gain_two_grad = middle_pull(normed_two_grad)
     middle_grad = out_grad + middle_part
     attended_all = gather_tokens(middle_grad.astype(bf_type))
-    branch = scatter_tokens(
-        jnp.dot(after(hidden, middle_grad), contract_low, preferred_element_type=fl_type)
-    )
-    layer_output = (middle + branch).astype(bf_type)
+    contract_sent = owned_sent(after(contract_reduced, middle_grad))
     mixing_full = lax.dot_general(
         mixed, attended_all, CONTRACT_FIRST, preferred_element_type=fl_type
     ).astype(bf_type)
     mixing_reduced = reduce_owned(mixing_full)
-    attended_all = after(attended_all, mixing_full, contract_reduced)
-    contract_grad = scatter_owned(contract_reduced)
+    attended_all = after(attended_all, mixing_full)
     mixed_grad = (
         lax.dot_general(attended_all, mixing_low, CONTRACT_LAST, preferred_element_type=fl_type)
         .astype(bf_type)
         .reshape(token_count, head_count, HEAD_DIM)
     )
+    mixed_grad = after(mixed_grad, last_reduced)
+    last_parts = spread(last_reduced)
     query_grads = []
     key_grads = []
     value_grads = []
     for group_index in range(2):
+        if group_index == 1:
+            mixed_grad = after(mixed_grad, query_grads[0], *contract_sent)
         for kv_index in range(kv_count):
             query_block, key_block, masked = head_scores(group_index, kv_index)
             soft_exact = jnp.exp(masked - log_totals[group_index, kv_index])
@@ -521,6 +628,8 @@
             )
             inner_sum = jnp.sum(prob_grad * soft_exact, axis=-1, keepdims=True)
             score_grad = (soft_exact * (prob_grad - inner_sum)).astype(bf_type)
+            if group_index == 1:
+                score_grad = after(score_grad, last_parts)
             query_grads.append(
                 jnp.einsum("rgk,ke->gre", score_grad, key_block, preferred_element_type=fl_type)
                 * factor
@@ -558,22 +667,43 @@
     qkv_back = jnp.concatenate(
         [query_back, key_back.astype(bf_type), value_back.astype(bf_type)], axis=1
     )
-    qkv_back = after(qkv_back, gate_reduced)
+    expand_states = [expand_weight, expand_moment, expand_second, expand_shadow]
+    branch = scatter_tokens(
+        branch_partial, lambda: (query_grads[-1],), hold=(attended_all,)
+    )
+    layer_output = (middle + branch).astype(bf_type)
+    contract_news = adamw(
+        owned_total(*contract_sent),
+        contract_weight,
+        contract_moment,
+        contract_second,
+        contract_shadow,
+        MATRIX_RATE,
+        WEIGHT_DECAY,
+        EMA_KEEP,
+    )
+    qkv_back = after(qkv_back, layer_output, last_parts)
     qkv_full = lax.dot_general(
         normed_all, qkv_back, CONTRACT_FIRST, preferred_element_type=fl_type
     ).astype(bf_type)
-    qkv_reduced = reduce_columns(qkv_full)
-    qkv_back = after(qkv_back, qkv_full, up_reduced, contract_grad)
-    expand_parts = scatter_columns(gate_reduced) + scatter_columns(up_reduced)
-    mixing_grad = scatter_owned(after(mixing_reduced, qkv_back))
-    qkv_parts = scatter_columns(after(qkv_reduced, qkv_back))
-    normed_grad = scatter_tokens(
-        lax.dot_general(qkv_back, qkv_low, CONTRACT_LAST, preferred_element_type=fl_type)
-    )
+    qkv_blocks = low_blocks(qkv_full, 4)
+    qkv_moved = sent_low(qkv_blocks)
+    normed_partial = lax.dot_general(
+        after(qkv_back, *qkv_blocks), qkv_low, CONTRACT_LAST, preferred_element_type=fl_type
+    )
+    first_parts = spread(after(first_reduced, normed_partial))
+    normed_kept, normed_sent = token_sums(normed_partial)
+    normed_away = swap_pair(normed_sent)
+    qkv_total = total_low(after(qkv_moved, normed_sent))
+    normed_away = after(normed_away, first_parts, qkv_total, *contract_news)
+    normed_grad = normed_kept + normed_away.astype(fl_type)
+    expand_news = expand_update((first_parts, last_parts), expand_states)
+    qkv_parts = after(columns_moved(qkv_total), *expand_news)
+    mixing_grad = owned_total(*owned_sent(after(mixing_reduced, first_parts)))
     rows_pull = jax.vjp(normalize, input_rows, gain_rows[0])[1]
     rows_part, gain_one_grad = rows_pull(normed_grad)
     input_grad = middle_grad + rows_part
-    gain_parts = jnp.stack([gain_one_grad, gain_two_grad]).reshape(2, 2 * dp_count, -1)
+    gain_parts = after(jnp.stack([gain_one_grad, gain_two_grad]), first_parts).reshape(2, 2 * dp_count, -1)
     gain_sums = jnp.sum(
         lax.all_to_all(gain_parts, ("dp", "tensor"), split_axis=1, concat_axis=1, tiled=True),
         axis=1,
@@ -597,19 +727,8 @@
         WEIGHT_DECAY,
         EMA_KEEP,
     )
-    expand_master, expand_momentum, expand_variance, expand_average = expand_update(
-        expand_parts, pair_bit, expand_weight, expand_moment, expand_second, expand_shadow
-    )
-    contract_master, contract_momentum, contract_variance, contract_average = adamw(
-        contract_grad,
-        contract_weight,
-        contract_moment,
-        contract_second,
-        contract_shadow,
-        MATRIX_RATE,
-        WEIGHT_DECAY,
-        EMA_KEEP,
-    )
+    expand_master, expand_momentum, expand_variance, expand_average = expand_news
+    contract_master, contract_momentum, contract_variance, contract_average = contract_news
     norms_master, norms_momentum, norms_variance, norms_average = adamw(
         gain_sums, norms_weight, norms_moment, norms_second, norms_shadow, GAIN_RATE, 0.0, GAIN_KEEP
     )

time: 702 us -> 645 us (0.919)
  waiting for transfers between devices: 297 us -> 227 us
  starting transfers between devices: 72.2 us -> 86.8 us
    ppermute x33 -> x22, waiting for transfers between devices: 233 us -> 137 us  [move(): lax.ppermute(value, 'dp', [(place * low_count + low, goal * low_count + l...]
    ppermute x0 -> x9, waiting for transfers between devices: none -> 55.5 us  [swap_low(): lax.ppermute(value, 'dp', [(index, index ^ flip) for index in range(dp_co...]
    reduce_scatter x5 -> x4, waiting for transfers between devices: 36.4 us -> 0.04 us  [scatter_low(): lax.psum_scatter(blocks, 'dp', scatter_dimension=1, tiled=True, axis_inde...]
    all_to_all x1 -> x5, waiting for transfers between devices: 4.38 us -> 26 us  [the longest x1 14.4 us: per_device(): lax.all_to_all(jnp.broadcast_to(own_facts[None], (2 * dp_count, own_facts...]
    all_gather x4 -> x3, waiting for transfers between devices: 20.2 us -> 0.04 us  [gather_low(): lax.all_gather(blocks, 'dp', axis=1, tiled=True, axis_index_groups=low_gr...]
    all_to_all x1 -> x5, starting transfers between devices: 5.99 us -> 22.5 us  [the longest x4 18.2 us: spread(): lax.all_to_all(blocks, 'dp', split_axis=0, concat_axis=0, tiled=True, axi...]
    ppermute x33 -> x22, starting transfers between devices: 57.9 us -> 45.3 us  [move(): lax.ppermute(value, 'dp', [(place * low_count + low, goal * low_count + l...]
    convert_element_type x7 -> x13, other arithmetic: 9.49 us -> 21.3 us  [the longest x2 10.6 us: gated_grad(): gate_grad.astype(bf_type)]
  transfers between devices with their start and end apart: 60 -> 60, of which waited for: 22 -> 21; matrix products, arithmetic and copies ran while one was open for 39% -> 40% of each run, Pallas kernels for 3% -> 3%
where the time goes in v2:
time: 645 us; the launch traced here: 636 us
  waiting for transfers between devices  227 us (35%)
  matrix products  155 us (24%)
  other arithmetic  87.8 us (14%)
  starting transfers between devices  86.8 us (13%)
  local copies, waits for them, and re-layouts  41.5 us (6%)
  Pallas kernels  21.1 us (3%)
  between operations  16.3 us (3%)
    ppermute x22, waiting for transfers between devices, move(): lax.ppermute(value, 'dp', [(place * low_count + low, goal * low_count + l...  137 us
    ppermute x9, waiting for transfers between devices, swap_low(): lax.ppermute(value, 'dp', [(index, index ^ flip) for index in range(dp_co...  55.5 us
    ppermute x22, starting transfers between devices, move(): lax.ppermute(value, 'dp', [(place * low_count + low, goal * low_count + l...  45.3 us
    unnamed x234, local copies, waits for them, and re-layouts  28.3 us
    dot_general x2, matrix products, gated(): gate_up = jnp.dot(rows, weights, preferred_element_type=fl_type)  20.3 us
    all_to_all x4, starting transfers between devices, spread(): lax.all_to_all(blocks, 'dp', split_axis=0, concat_axis=0, tiled=True, axi...  18.2 us
    all_to_all x1, waiting for transfers between devices, per_device(): lax.all_to_all(jnp.broadcast_to(own_facts[None], (2 * dp_count, own_facts...  14.4 us
    pallas_call x1, Pallas kernels, expand_update(): pl.pallas_call(kernel, grid=(row_count // step,), in_specs=[pl.BlockSpec(...  13.4 us
  transfers between devices with their start and end apart: 60, of which 21 were waited for; matrix products, arithmetic and copies ran while one was open for 40% of the time, Pallas kernels for 3%

profile of v2, /device:TPU:0, one launch (start us, length us, event | category | flops | bytes accessed | tf_op | source)
XLA Modules:
  0.0 635.8 jit_solution(14247506702326193859)
XLA Ops:
  9.1 3.4 shard_map.468
  13.6 5.0 collective-permute-start.24
  22.5 4.3 all-to-all-start
  26.8 2.7 collective-permute-start.23
  29.8 14.4 %all-to-all-done = f32[32,1,646]{2,1,0:T(1,128)S(1)} async-done(((f32[32,1,646]{2,1,0:T(1,128)}), f32[32,1,646]{2,1,0:T(1,128)S(1)}, u32[]{:S(2)}, u32[]{:S(2)}) %all-to-all-start) | async-done | bytes 82720 | tf_op jit(solution)/shard_map/all_to_all | solution.py:417
  52.6 4.8 collective-permute-start.1
  58.3 3.5 all-to-all-start.1
  64.0 24.9 %collective-permute-done.1 = bf16[256,2048]{1,0:T(8,128)(2,1)} collective-permute-done((bf16[256,2048]{1,0:T(8,128)(2,1)}, bf16[256,2048]{1,0:T(8,128)(2,1)}, u32[]{:S(2)}, u32[]{:S(2)}) %collective-permute-start.1) | collective-permute-done | bytes 1048608 | tf_op jit(solution)/shard_map/ppermute | solution.py:297
  95.6 4.4 all-to-all-start.2
  103.0 20.2 %collective-permute-done.5.refs_3_ = bf16[4,128,640]{2,1,0:T(8,128)(2,1)S(1)} collective-permute-done((bf16[4,128,640]{2,1,0:T(8,128)(2,1)S(1)}, bf16[4,128,640]{2,1,0:T(8,128)(2,1)S(1)}, u32[]{:S(2)}, u32[]{:S(2)}) %collective-permute-start.5) | collective-permute-done | bytes 655392 | tf_op jit(solution)/shard_map/ppermute | solution.py:320
  123.2 14.0 %collective-permute-done.4.refs_2_ = bf16[4,128,640]{2,1,0:T(8,128)(2,1)S(1)} collective-permute-done((bf16[4,128,640]{2,1,0:T(8,128)(2,1)S(1)}, bf16[4,128,640]{2,1,0:T(8,128)(2,1)S(1)}, u32[]{:S(2)}, u32[]{:S(2)}) %collective-permute-start.4) | collective-permute-done | bytes 655392 | tf_op jit(solution)/shard_map/ppermute | solution.py:320
  147.5 4.1 fusion.131
  162.8 2.5 fusion.44
  174.4 3.7 collective-permute-start.9
  179.5 15.4 %collective-permute-done.9 = bf16[176,2048]{1,0:T(8,128)(2,1)S(1)} collective-permute-done((bf16[176,2048]{1,0:T(8,128)(2,1)S(1)}, bf16[176,2048]{1,0:T(8,128)(2,1)S(1)}, u32[]{:S(2)}, u32[]{:S(2)}) %collective-permute-start.9) | collective-permute-done | bytes 720928 | tf_op jit(solution)/shard_map/ppermute | solution.py:297
  202.2 2.7 collective-permute-done.17
  206.2 8.9 %collective-permute-start.18 = (bf16[256,2048]{1,0:T(8,128)(2,1)}, bf16[256,2048]{1,0:T(8,128)(2,1)}, u32[]{:S(2)}, u32[]{:S(2)}) collective-permute-start(bf16[256,2048]{1,0:T(8,128)(2,1)} %fusion.37), channel_id=1, source_target_pairs={{0,8},{2,10},{4,12},{6,14},{8,0},{10,2},{12,4},{14,6},{16,24},{18,... | collective-permute-start | bytes 3145736 | tf_op jit(solution)/shard_map/ppermute | solution.py:297
  215.7 23.2 %collective-permute-done.18 = bf16[256,2048]{1,0:T(8,128)(2,1)} collective-permute-done((bf16[256,2048]{1,0:T(8,128)(2,1)}, bf16[256,2048]{1,0:T(8,128)(2,1)}, u32[]{:S(2)}, u32[]{:S(2)}) %collective-permute-start.18) | collective-permute-done | bytes 1048608 | tf_op jit(solution)/shard_map/ppermute | solution.py:297
  238.8 2.9 multiply_reduce_fusion.2
  245.1 22.9 %collective-permute-done.20 = bf16[256,2048]{1,0:T(8,128)(2,1)S(1)} collective-permute-done((bf16[256,2048]{1,0:T(8,128)(2,1)S(1)}, bf16[256,2048]{1,0:T(8,128)(2,1)S(1)}, u32[]{:S(2)}, u32[]{:S(2)}) %collective-permute-start.20) | collective-permute-done | bytes 1048608 | tf_op jit(solution)/shard_map/ppermute | solution.py:297
  268.1 2.6 collective-permute-done.21
  273.9 10.3 %fusion.118 = f32[1024,1280]{1,0:T(8,128)S(1)} fusion(bf16[2048,1280]{1,0:T(8,128)(2,1)} %bitcast.235, bf16[256,2048]{1,0:T(8,128)(2,1)} %copy-done.71, bf16[256,2048]{1,0:T(8,128)(2,1)} %copy-done.67, bf16[256,2048]{1,0:T(8,128)(2,1)} %copy-done.69, bf16[256,2048]{1,0:T(8,128)(2,1)S(1)} %multiply_convert_fusion.6), kind=kOutput, calls=%fused_computation.255 | convolution fusion | flops 5385486336 | bytes 14680064 | tf_op jit(solution)/shard_map/dot_general | solution.py:534
  287.3 10.0 %fusion.137 = f32[1024,1536]{1,0:T(8,128)S(1)} fusion(bf16[1024,2048]{1,0:T(8,128)(2,1)} %pad_maximum_fusion.1, bf16[2048,1536]{1,0:T(8,128)(2,1)} %bitcast.227), kind=kOutput, calls=%fused_computation.272 | convolution fusion | flops 6442450944 | bytes 16777216 | tf_op jit(solution)/shard_map/dot_general | solution.py:534
  297.3 2.6 copy-done.30
  302.1 8.0 %convolution_convert_fusion.2 = bf16[1408,2048]{1,0:T(8,128)(2,1)} fusion(bf16[1024,2048]{1,0:T(8,128)(2,1)S(1)} %copy-done.80, bf16[1024,768]{1,0:T(8,128)(2,1)S(1)} %multiply_convert_fusion.2, bf16[1024,640]{1,0:T(8,128)(2,1)S(1)} %multiply_convert_fusion.5), kind=kOutput, calls=%fused_computation.20 | convolution fusion | flops 5914230784 | bytes 12845056 | tf_op jit(solution)/shard_map/dot_general | solution.py:562
  310.4 10.6 %fusion.138 = f32[1024,1408]{1,0:T(8,128)S(1)} fusion(bf16[1024,2048]{1,0:T(8,128)(2,1)} %constant_dynamic-update-slice_fusion, bf16[1408,2048]{1,0:T(8,128)(2,1)} %bitcast.231), kind=kOutput, calls=%fused_computation.273 | convolution fusion | flops 5905580032 | bytes 15728640 | tf_op jit(solution)/shard_map/dot_general | solution.py:566
  321.0 5.8 multiply_convert_fusion.1
  327.3 8.7 %convolution_convert_fusion.1 = bf16[2048,1536]{1,0:T(8,128)(2,1)} fusion(bf16[1024,768]{1,0:T(8,128)(2,1)S(1)} %get-tuple-element.169, bf16[1024,768]{1,0:T(8,128)(2,1)S(1)} %get-tuple-element.168, bf16[256,2048]{1,0:T(8,128)(2,1)S(1)} %copy-done.72, bf16[256,2048]{1,0:T(8,128)(2,1)S(1)} %copy-done.68, bf16[256,2048]{1,0:T(8,128)(2,1)S(1)} %copy-done.70, ...), kind=kOutput, calls=%fused_computation.19 | convolution fusion | flops 6468665344 | bytes 13631488 | tf_op jit(solution)/shard_map/dot_general | solution.py:579
  338.2 4.8 multiply_convert_fusion.4
  343.1 7.5 %convolution_convert_fusion = bf16[2048,1280]{1,0:T(8,128)(2,1)} fusion(bf16[1024,2048]{1,0:T(8,128)(2,1)S(1)} %copy-done.49, bf16[1024,640]{1,0:T(8,128)(2,1)S(1)} %get-tuple-element.171, bf16[1024,640]{1,0:T(8,128)(2,1)S(1)} %get-tuple-element.170), kind=kOutput, calls=%fused_computation.18 | convolution fusion | flops 5376573440 | bytes 12058624 | tf_op jit(solution)/shard_map/dot_general | solution.py:582
  350.6 9.1 %fusion.139 = f32[1024,2048]{1,0:T(8,128)} fusion(bf16[1024,1536]{1,0:T(8,128)(2,1)S(1)} %pad_maximum_fusion.3, bf16[2048,1536]{1,0:T(8,128)(2,1)S(1)} %bitcast.230), kind=kOutput, calls=%fused_computation.274 | convolution fusion | flops 6442450944 | bytes 17825792 | tf_op jit(solution)/shard_map/dot_general | solution.py:589
  360.1 9.6 %fusion.135 = (bf16[1024,2048]{1,0:T(8,128)(2,1)S(1)}, f32[1024,2048]{1,0:T(8,128)S(1)}) fusion(f32[1024,2048]{1,0:T(8,128)} %fusion.139, bf16[2048,1280]{1,0:T(8,128)(2,1)} %bitcast.236, bf16[1024,640]{1,0:T(8,128)(2,1)} %copy-done.60, bf16[1024,640]{1,0:T(8,128)(2,1)} %copy-done.59), kind=kOutput, calls=%fused_computation.268 | convolution fusion | flops 5378146304 | bytes 28835840 | tf_op jit(solution)/shard_map/dot_general | solution.py:591
  374.6 9.0 %fusion.134 = (bf16[1024,2048]{1,0:T(8,128)(2,1)S(1)}, f32[1024,2048]{1,0:T(8,128)}) fusion(bf16[1024,1408]{1,0:T(8,128)(2,1)S(1)} %pad_maximum_fusion.4, bf16[1408,2048]{1,0:T(8,128)(2,1)S(1)} %bitcast.234), kind=kOutput, calls=%fused_computation.267 | convolution fusion | flops 5907677184 | bytes 21233664 | tf_op jit(solution)/shard_map/dot_general | solution.py:592
  383.5 14.8 %collective-permute-done.29 = bf16[256,2048]{1,0:T(8,128)(2,1)S(1)} collective-permute-done((bf16[256,2048]{1,0:T(8,128)(2,1)S(1)}, bf16[256,2048]{1,0:T(8,128)(2,1)S(1)}, u32[]{:S(2)}, u32[]{:S(2)}) %collective-permute-start.29) | collective-permute-done | bytes 1048608 | tf_op jit(solution)/shard_map/ppermute | solution.py:297
  399.8 3.7 fusion.122
  407.0 21.2 %collective-permute-done.31 = bf16[256,2048]{1,0:T(8,128)(2,1)} collective-permute-done((bf16[256,2048]{1,0:T(8,128)(2,1)S(1)}, bf16[256,2048]{1,0:T(8,128)(2,1)}, u32[]{:S(2)}, u32[]{:S(2)}) %collective-permute-start.31) | collective-permute-done | bytes 1048608 | tf_op jit(solution)/shard_map/ppermute | solution.py:297
  429.4 3.1 fusion.33
  434.7 5.6 convolution_convert_fusion.4
  441.8 3.4 convolution_convert_fusion.5
  449.9 5.4 fusion.3
  455.7 3.8 fusion.5
  459.6 5.8 all-to-all-start.3
  465.4 4.0 fusion.41
  469.4 11.6 %collective-permute-done.34 = bf16[176,2048]{1,0:T(8,128)(2,1)} collective-permute-done((bf16[176,2048]{1,0:T(8,128)(2,1)}, bf16[176,2048]{1,0:T(8,128)(2,1)}, u32[]{:S(2)}, u32[]{:S(2)}) %collective-permute-start.34) | collective-permute-done | bytes 720928 | tf_op jit(solution)/shard_map/ppermute | solution.py:297
  481.1 4.9 fusion.54
  486.0 11.5 %fusion.2 = bf16[8,512,512]{1,2,0:T(8,128)(2,1)} fusion(f32[8,512,512]{1,2,0:T(8,128)} %copy-done.22, f32[8,512]{1,0:T(8,128)} %log_add_fusion.1, bf16[1024,8,64]{0,2,1:T(8,128)(2,1)S(1)} %bitcast.211, bf16[1024,640]{0,1:T(8,128)(2,1)} %get-tuple-element.217), kind=kOutput, calls=%fused_computation.4 | convolution fusion | flops 549458432 | bytes 22183936 | tf_op jit(solution)/shard_map/sub | solution.py:630
  497.4 5.6 fusion.57
  505.1 10.5 %all-to-all-done.3.refs_1_ = bf16[4,128,1536]{2,1,0:T(8,128)(2,1)S(1)} async-done(((bf16[4,128,1536]{2,1,0:T(8,128)(2,1)}), bf16[4,128,1536]{2,1,0:T(8,128)(2,1)S(1)}, u32[]{:S(2)}, u32[]{:S(2)}) %all-to-all-start.3) | async-done | bytes 1572896 | tf_op jit(solution)/shard_map/all_to_all | solution.py:312
  515.6 3.6 fusion.40
  524.0 4.0 fusion.36
  528.0 3.8 convolution_convert_fusion.3
  534.5 6.0 fusion.136
  541.6 4.5 all-to-all-start.4
  549.7 3.2 fusion.29
  554.8 5.3 multiply_add_fusion.1
  560.0 5.5 collective-permute-done.41
  565.5 13.3 %collective-permute-done.40 = bf16[4,128,640]{2,1,0:T(8,128)(2,1)S(1)} collective-permute-done((bf16[4,128,640]{2,1,0:T(8,128)(2,1)}, bf16[4,128,640]{2,1,0:T(8,128)(2,1)S(1)}, u32[]{:S(2)}, u32[]{:S(2)}) %collective-permute-start.40) | collective-permute-done | bytes 655392 | tf_op jit(solution)/shard_map/ppermute | solution.py:320
  580.0 3.4 collective-permute-start.44
  587.7 13.4 %shard_map.471 = (f32[128,2,2816]{2,1,0:T(2,128)}, f32[128,2,2816]{2,1,0:T(2,128)}, f32[128,2,2816]{2,1,0:T(2,128)}, f32[128,2,2816]{2,1,0:T(2,128)}) custom-call(bf16[4,128,1280]{2,1,0:T(8,128)(2,1)} %all-to-all-done.4.refs_0_, bf16[4,128,1536]{2,1,0:T(8,128)(2,1)S(1)} %copy-done.5, f32[128,2,2816]{2,1,0:T(2,128)S(1)} %copy-done.1, ...), custom_call_target="tpu_custom_call" | custom-call | tf_op jit(solution)/shard_map/pallas_call | solution.py:242
  604.9 2.9 shard_map.472
  607.8 3.3 fusion.24
  612.0 4.8 all-to-all-start.5
  616.9 5.2 fusion.26
  625.9 2.7 multiply_add_fusion.3
  (432 shorter events, 133.3 us)
Async XLA Ops:
  13.6 33.3 %collective-permute-start.24 = (bf16[128,1280]{1,0:T(8,128)(2,1)S(1)}, bf16[128,1280]{1,0:T(8,128)(2,1)S(1)}, u32[]{:S(2)}, u32[]{:S(2)}) collective-permute-start(bf16[128,1280]{1,0:T(8,128)(2,1)S(1)} %get-tuple-element.99), channel_id=1, source_target_pairs={{0,24},{2,26},{4,28},{6,30},{8,16},{10,18},{12,20},{14,22},{16,8},... | collective-permute-start | bytes 983048 | tf_op jit(solution)/shard_map/ppermute | solution.py:297
  18.7 28.3 %collective-permute-start.22 = (bf16[128,1280]{1,0:T(8,128)(2,1)S(1)}, bf16[128,1280]{1,0:T(8,128)(2,1)S(1)}, u32[]{:S(2)}, u32[]{:S(2)}) collective-permute-start(bf16[128,1280]{1,0:T(8,128)(2,1)S(1)} %get-tuple-element.99), channel_id=1, source_target_pairs={{0,8},{2,10},{4,12},{6,14},{8,0},{10,2},{12,4},{14,6},{16,24},{18,... | collective-permute-start | bytes 983048 | tf_op jit(solution)/shard_map/ppermute | solution.py:297
  22.5 21.7 %all-to-all-start = ((f32[32,1,646]{2,1,0:T(1,128)}), f32[32,1,646]{2,1,0:T(1,128)S(1)}, u32[]{:S(2)}, u32[]{:S(2)}) async-start(f32[32,1,646]{2,1,0:T(1,128)} %broadcast_in_dim.52), calls=%async_computation | async-start | bytes 196608 | tf_op jit(solution)/shard_map/all_to_all | solution.py:417
  26.7 247.2 %all-gather.4.cloned.1.call-start = ((), (), s32[]{:S(2)}) async-start(), calls=%async_computation.10 | async-start | bytes 6553600 | tf_op jit(solution)/shard_map/all_gather | solution.py:335
  26.8 21.9 %collective-permute-start.23 = (bf16[128,1280]{1,0:T(8,128)(2,1)S(1)}, bf16[128,1280]{1,0:T(8,128)(2,1)S(1)}, u32[]{:S(2)}, u32[]{:S(2)}) collective-permute-start(bf16[128,1280]{1,0:T(8,128)(2,1)S(1)} %get-tuple-element.100), channel_id=1, source_target_pairs={{0,16},{2,18},{4,20},{6,22},{8,24},{10,26},{12,28},{14,30},{16,0},... | collective-permute-start | bytes 983048 | tf_op jit(solution)/shard_map/ppermute | solution.py:297
  50.3 43.4 %collective-permute-start.7 = (bf16[64,2048]{1,0:T(8,128)(2,1)S(1)}, bf16[64,2048]{1,0:T(8,128)(2,1)S(1)}, u32[]{:S(2)}, u32[]{:S(2)}) collective-permute-start(bf16[64,2048]{1,0:T(8,128)(2,1)S(1)} %convert_element_type.222), channel_id=1, source_target_pairs={{0,16},{2,18},{4,20},{6,22},{8,0},{10,2},{12,4},{14,6},{16,24},{18... | collective-permute-start | bytes 786440 | tf_op jit(solution)/shard_map/ppermute | solution.py:297
  50.3 38.5 %collective-permute-start.6 = (bf16[64,2048]{1,0:T(8,128)(2,1)S(1)}, bf16[64,2048]{1,0:T(8,128)(2,1)S(1)}, u32[]{:S(2)}, u32[]{:S(2)}) collective-permute-start(bf16[64,2048]{1,0:T(8,128)(2,1)S(1)} %convert_element_type.222), channel_id=1, source_target_pairs={{8,16},{10,18},{12,20},{14,22},{16,8},{18,10},{20,12},{22,14},{9,1... | collective-permute-start | bytes 786440 | tf_op jit(solution)/shard_map/ppermute | solution.py:297
  52.1 38.6 %copy-start.99 = (f32[32]{0:T(128)}, f32[32]{0:T(128)S(1)}, u32[]{:S(2)}) copy-start(f32[32]{0:T(128)S(1)} %multiply_power_fusion) | copy-start | bytes 388
  52.6 36.2 %collective-permute-start.1 = (bf16[256,2048]{1,0:T(8,128)(2,1)}, bf16[256,2048]{1,0:T(8,128)(2,1)}, u32[]{:S(2)}, u32[]{:S(2)}) collective-permute-start(bf16[256,2048]{1,0:T(8,128)(2,1)} %fusion.23), channel_id=1, source_target_pairs={{0,8},{2,10},{4,12},{6,14},{8,0},{10,2},{12,4},{14,6},{16,24},{18,... | collective-permute-start | bytes 3145736 | tf_op jit(solution)/shard_map/ppermute | solution.py:297
  57.4 86.1 %collective-permute-start = (bf16[256,2048]{1,0:T(8,128)(2,1)}, bf16[256,2048]{1,0:T(8,128)(2,1)}, u32[]{:S(2)}, u32[]{:S(2)}) collective-permute-start(bf16[256,2048]{1,0:T(8,128)(2,1)} %fusion.23), channel_id=1, source_target_pairs={{0,1},{1,0},{2,3},{3,2},{4,5},{5,4},{6,7},{7,6},{8,9},{9,8},{10,11... | collective-permute-start | bytes 3145736 | tf_op jit(solution)/shard_map/ppermute | solution.py:326
  58.3 32.4 %all-to-all-start.1 = ((bf16[4,128,640]{2,1,0:T(8,128)(2,1)}), bf16[4,128,640]{2,1,0:T(8,128)(2,1)S(1)}, u32[]{:S(2)}, u32[]{:S(2)}) async-start(bf16[4,128,640]{2,1,0:T(8,128)(2,1)} %shard_map.467), calls=%async_computation.1 | async-start | bytes 1310720 | tf_op jit(solution)/shard_map/all_to_all | solution.py:312
  62.8 88.9 %copy-start.87 = (f32[1024]{0:T(1024)}, f32[1024]{0:T(1024)S(1)}, u32[]{:S(2)}) copy-start(f32[1024]{0:T(1024)S(1)} %add_convert_fusion.3) | copy-start | bytes 12292
  64.0 88.8 %copy-start.61 = (f32[1024,32]{0,1:T(8,128)}, f32[1024,32]{0,1:T(8,128)S(1)}, u32[]{:S(2)}) copy-start(f32[1024,32]{0,1:T(8,128)S(1)} %get-tuple-element.206) | copy-start | bytes 393220
  88.9 54.7 %collective-permute-start.2 = (bf16[256,2048]{1,0:T(8,128)(2,1)}, bf16[256,2048]{1,0:T(8,128)(2,1)}, u32[]{:S(2)}, u32[]{:S(2)}) collective-permute-start(bf16[256,2048]{1,0:T(8,128)(2,1)} %collective-permute-done.1), channel_id=1, source_target_pairs={{0,1},{1,0},{2,3},{3,2},{4,5},{5,4},{6,7},{7,6},{8,9},{9,8},{10,11... | collective-permute-start | bytes 3145736 | tf_op jit(solution)/shard_map/ppermute | solution.py:326
  90.7 32.5 %collective-permute-start.5 = (bf16[4,128,640]{2,1,0:T(8,128)(2,1)S(1)}, bf16[4,128,640]{2,1,0:T(8,128)(2,1)S(1)}, u32[]{:S(2)}, u32[]{:S(2)}) collective-permute-start(bf16[4,128,640]{2,1,0:T(8,128)(2,1)S(1)} %all-to-all-done.1.refs_0_), channel_id=1, source_target_pairs={{0,6},{2,4},{4,2},{6,0},{8,14},{10,12},{12,10},{14,8},{16,22},{18,... | collective-permute-start | bytes 1966088 | tf_op jit(solution)/shard_map/ppermute | solution.py:320
  93.1 44.0 %collective-permute-start.4 = (bf16[4,128,640]{2,1,0:T(8,128)(2,1)S(1)}, bf16[4,128,640]{2,1,0:T(8,128)(2,1)S(1)}, u32[]{:S(2)}, u32[]{:S(2)}) collective-permute-start(bf16[4,128,640]{2,1,0:T(8,128)(2,1)S(1)} %all-to-all-done.1.refs_0_), channel_id=1, source_target_pairs={{0,4},{2,6},{4,0},{6,2},{8,12},{10,14},{12,8},{14,10},{16,20},{18,... | collective-permute-start | bytes 1966088 | tf_op jit(solution)/shard_map/ppermute | solution.py:320
  93.6 46.0 %collective-permute-start.3 = (bf16[4,128,640]{2,1,0:T(8,128)(2,1)S(1)}, bf16[4,128,640]{2,1,0:T(8,128)(2,1)S(1)}, u32[]{:S(2)}, u32[]{:S(2)}) collective-permute-start(bf16[4,128,640]{2,1,0:T(8,128)(2,1)S(1)} %all-to-all-done.1.refs_0_), channel_id=1, source_target_pairs={{0,2},{2,0},{4,6},{6,4},{8,10},{10,8},{12,14},{14,12},{16,18},{18,... | collective-permute-start | bytes 1966088 | tf_op jit(solution)/shard_map/ppermute | solution.py:320
  95.6 57.5 %all-to-all-start.2 = ((bf16[4,128,1536]{2,1,0:T(8,128)(2,1)}), bf16[4,128,1536]{2,1,0:T(8,128)(2,1)}, u32[]{:S(2)}, u32[]{:S(2)}) async-start(bf16[4,128,1536]{2,1,0:T(8,128)(2,1)} %copy-done.8), calls=%async_computation.2 | async-start | bytes 3145728 | tf_op jit(solution)/shard_map/all_to_all | solution.py:312
  100.0 187.3 %all-gather.6.cloned.1.call-start = ((), (), s32[]{:S(2)}) async-start(), calls=%async_computation.11 | async-start | bytes 7864320 | tf_op jit(solution)/shard_map/all_gather | solution.py:335
  140.0 26.6 %collective-permute-start.15 = (bf16[2,64,2048]{2,1,0:T(8,128)(2,1)S(1)}, bf16[2,64,2048]{2,1,0:T(8,128)(2,1)S(1)}, u32[]{:S(2)}, u32[]{:S(2)}) collective-permute-start(bf16[2,64,2048]{2,1,0:T(8,128)(2,1)S(1)} %maximum_select_fusion.2.refs_0_), channel_id=1, source_target_pairs={{0,6},{2,4},{4,2},{6,0},{8,14},{10,12},{12,10},{14,8},{16,22},{18,... | collective-permute-start | bytes 1572872 | tf_op jit(solution)/shard_map/ppermute | solution.py:320
  141.5 27.1 %collective-permute-start.14 = (bf16[2,64,2048]{2,1,0:T(8,128)(2,1)S(1)}, bf16[2,64,2048]{2,1,0:T(8,128)(2,1)S(1)}, u32[]{:S(2)}, u32[]{:S(2)}) collective-permute-start(bf16[2,64,2048]{2,1,0:T(8,128)(2,1)S(1)} %maximum_select_fusion.2.refs_0_), channel_id=1, source_target_pairs={{0,4},{2,6},{4,0},{6,2},{8,12},{10,14},{12,8},{14,10},{16,20},{18,... | collective-permute-start | bytes 1572872 | tf_op jit(solution)/shard_map/ppermute | solution.py:320
  141.8 27.6 %collective-permute-start.13 = (bf16[2,64,2048]{2,1,0:T(8,128)(2,1)S(1)}, bf16[2,64,2048]{2,1,0:T(8,128)(2,1)S(1)}, u32[]{:S(2)}, u32[]{:S(2)}) collective-permute-start(bf16[2,64,2048]{2,1,0:T(8,128)(2,1)S(1)} %maximum_select_fusion.2.refs_0_), channel_id=1, source_target_pairs={{0,2},{2,0},{4,6},{6,4},{8,10},{10,8},{12,14},{14,12},{16,18},{18,... | collective-permute-start | bytes 1572872 | tf_op jit(solution)/shard_map/ppermute | solution.py:320
  145.9 26.6 %collective-permute-start.11 = (bf16[256,2048]{1,0:T(8,128)(2,1)}, bf16[256,2048]{1,0:T(8,128)(2,1)}, u32[]{:S(2)}, u32[]{:S(2)}) collective-permute-start(bf16[256,2048]{1,0:T(8,128)(2,1)} %param.29), channel_id=1, source_target_pairs={{0,8},{2,10},{4,12},{6,14},{8,0},{10,2},{12,4},{14,6},{16,24},{18,... | collective-permute-start | bytes 3145736 | tf_op jit(solution)/shard_map/ppermute | solution.py:297
  147.4 25.6 %collective-permute-start.10 = (bf16[256,2048]{1,0:T(8,128)(2,1)}, bf16[256,2048]{1,0:T(8,128)(2,1)}, u32[]{:S(2)}, u32[]{:S(2)}) collective-permute-start(bf16[256,2048]{1,0:T(8,128)(2,1)} %param.29), channel_id=1, source_target_pairs={{0,1},{1,0},{2,3},{3,2},{4,5},{5,4},{6,7},{7,6},{8,9},{9,8},{10,11... | collective-permute-start | bytes 3145736 | tf_op jit(solution)/shard_map/ppermute | solution.py:326
  153.2 157.2 %all-gather.8.cloned.1.call-start = ((), (), s32[]{:S(2)}) async-start(), calls=%async_computation.12 | async-start | bytes 7208960 | tf_op jit(solution)/shard_map/all_gather | solution.py:335
  166.5 12.8 %collective-permute-start.8 = (bf16[176,2048]{1,0:T(8,128)(2,1)S(1)}, bf16[176,2048]{1,0:T(8,128)(2,1)S(1)}, u32[]{:S(2)}, u32[]{:S(2)}) collective-permute-start(bf16[176,2048]{1,0:T(8,128)(2,1)S(1)} %convert_element_type.230), channel_id=1, source_target_pairs={{8,16},{10,18},{12,20},{14,22},{16,8},{18,10},{20,12},{22,14},{9,1... | collective-permute-start | bytes 2162696 | tf_op jit(solution)/shard_map/ppermute | solution.py:297
  172.5 23.8 %collective-permute-start.12 = (bf16[256,2048]{1,0:T(8,128)(2,1)}, bf16[256,2048]{1,0:T(8,128)(2,1)}, u32[]{:S(2)}, u32[]{:S(2)}) collective-permute-start(bf16[256,2048]{1,0:T(8,128)(2,1)} %collective-permute-done.11), channel_id=1, source_target_pairs={{0,1},{1,0},{2,3},{3,2},{4,5},{5,4},{6,7},{7,6},{8,9},{9,8},{10,11... | collective-permute-start | bytes 3145736 | tf_op jit(solution)/shard_map/ppermute | solution.py:326
  174.4 20.5 %collective-permute-start.9 = (bf16[176,2048]{1,0:T(8,128)(2,1)S(1)}, bf16[176,2048]{1,0:T(8,128)(2,1)S(1)}, u32[]{:S(2)}, u32[]{:S(2)}) collective-permute-start(bf16[176,2048]{1,0:T(8,128)(2,1)S(1)} %convert_element_type.230), channel_id=1, source_target_pairs={{0,16},{2,18},{4,20},{6,22},{8,0},{10,2},{12,4},{14,6},{16,24},{18... | collective-permute-start | bytes 2162696 | tf_op jit(solution)/shard_map/ppermute | solution.py:297
  202.2 36.6 %copy-start.28 = (bf16[256,2048]{1,0:T(8,128)(2,1)S(1)}, bf16[256,2048]{1,0:T(8,128)(2,1)}, u32[]{:S(2)}) copy-start(bf16[256,2048]{1,0:T(8,128)(2,1)} %param.28) | copy-start | bytes 3145732
  202.2 2.7 collective-permute-start.17
  206.2 32.7 %collective-permute-start.18 = (bf16[256,2048]{1,0:T(8,128)(2,1)}, bf16[256,2048]{1,0:T(8,128)(2,1)}, u32[]{:S(2)}, u32[]{:S(2)}) collective-permute-start(bf16[256,2048]{1,0:T(8,128)(2,1)} %fusion.37), channel_id=1, source_target_pairs={{0,8},{2,10},{4,12},{6,14},{8,0},{10,2},{12,4},{14,6},{16,24},{18,... | collective-permute-start | bytes 3145736 | tf_op jit(solution)/shard_map/ppermute | solution.py:297
  215.1 23.8 %collective-permute-start.16 = (bf16[256,2048]{1,0:T(8,128)(2,1)}, bf16[256,2048]{1,0:T(8,128)(2,1)}, u32[]{:S(2)}, u32[]{:S(2)}) collective-permute-start(bf16[256,2048]{1,0:T(8,128)(2,1)} %get-tuple-element.178), channel_id=1, source_target_pairs={{0,1},{1,0},{2,3},{3,2},{4,5},{5,4},{6,7},{7,6},{8,9},{9,8},{10,11... | collective-permute-start | bytes 3145736 | tf_op jit(solution)/shard_map/ppermute | solution.py:326
  215.2 230.0 %reduce-scatter.7.cloned.1.call-start = ((), (), s32[]{:S(2)}) async-start(), calls=%async_computation.14 | async-start | bytes 7208960 | tf_op jit(solution)/shard_map/reduce_scatter | solution.py:338
  243.3 24.8 %collective-permute-start.20 = (bf16[256,2048]{1,0:T(8,128)(2,1)S(1)}, bf16[256,2048]{1,0:T(8,128)(2,1)S(1)}, u32[]{:S(2)}, u32[]{:S(2)}) collective-permute-start(bf16[256,2048]{1,0:T(8,128)(2,1)S(1)} %multiply_convert_fusion.6), channel_id=1, source_target_pairs={{0,8},{2,10},{4,12},{6,14},{8,0},{10,2},{12,4},{14,6},{16,24},{18,... | collective-permute-start | bytes 3145736 | tf_op jit(solution)/shard_map/ppermute | solution.py:297
  245.1 23.0 %collective-permute-start.19 = (bf16[256,2048]{1,0:T(8,128)(2,1)S(1)}, bf16[256,2048]{1,0:T(8,128)(2,1)S(1)}, u32[]{:S(2)}, u32[]{:S(2)}) collective-permute-start(bf16[256,2048]{1,0:T(8,128)(2,1)S(1)} %multiply_convert_fusion.6), channel_id=1, source_target_pairs={{0,1},{1,0},{2,3},{3,2},{4,5},{5,4},{6,7},{7,6},{8,9},{9,8},{10,11... | collective-permute-start | bytes 3145736 | tf_op jit(solution)/shard_map/ppermute | solution.py:326
  268.0 2.7 collective-permute-start.21
  310.2 139.7 %reduce-scatter.5.cloned.1.call-start = ((), (), s32[]{:S(2)}) async-start(), calls=%async_computation.13 | async-start | bytes 7864320 | tf_op jit(solution)/shard_map/reduce_scatter | solution.py:338
  336.0 205.6 %reduce-scatter.9.cloned.1.call-start = ((), (), s32[]{:S(2)}) async-start(), calls=%async_computation.15 | async-start | bytes 6553600 | tf_op jit(solution)/shard_map/reduce_scatter | solution.py:338
  359.7 224.7 %reduce-scatter.11.cloned.1.call-start = ((), (), s32[]{:S(2)}) async-start(), calls=%async_computation.16 | async-start | bytes 2621440 | tf_op jit(solution)/shard_map/reduce_scatter | solution.py:338
  370.0 2.7 collective-permute-start.28
  371.4 26.9 %collective-permute-start.27 = (bf16[256,2048]{1,0:T(8,128)(2,1)S(1)}, bf16[256,2048]{1,0:T(8,128)(2,1)S(1)}, u32[]{:S(2)}, u32[]{:S(2)}) collective-permute-start(bf16[256,2048]{1,0:T(8,128)(2,1)S(1)} %get-tuple-element.176), channel_id=1, source_target_pairs={{0,1},{1,0},{2,3},{3,2},{4,5},{5,4},{6,7},{7,6},{8,9},{9,8},{10,11... | collective-permute-start | bytes 3145736 | tf_op jit(solution)/shard_map/ppermute | solution.py:326
  373.1 25.3 %collective-permute-start.29 = (bf16[256,2048]{1,0:T(8,128)(2,1)S(1)}, bf16[256,2048]{1,0:T(8,128)(2,1)S(1)}, u32[]{:S(2)}, u32[]{:S(2)}) collective-permute-start(bf16[256,2048]{1,0:T(8,128)(2,1)S(1)} %fusion.31), channel_id=1, source_target_pairs={{0,8},{2,10},{4,12},{6,14},{8,0},{10,2},{12,4},{14,6},{16,24},{18,... | collective-permute-start | bytes 3145736 | tf_op jit(solution)/shard_map/ppermute | solution.py:297
  403.6 24.6 %collective-permute-start.31 = (bf16[256,2048]{1,0:T(8,128)(2,1)S(1)}, bf16[256,2048]{1,0:T(8,128)(2,1)}, u32[]{:S(2)}, u32[]{:S(2)}) collective-permute-start(bf16[256,2048]{1,0:T(8,128)(2,1)S(1)} %get-tuple-element.164), channel_id=1, source_target_pairs={{0,8},{2,10},{4,12},{6,14},{8,0},{10,2},{12,4},{14,6},{16,24},{18,... | collective-permute-start | bytes 3145736 | tf_op jit(solution)/shard_map/ppermute | solution.py:297
  406.5 22.9 %collective-permute-start.26 = (bf16[256,2048]{1,0:T(8,128)(2,1)}, bf16[256,2048]{1,0:T(8,128)(2,1)}, u32[]{:S(2)}, u32[]{:S(2)}) collective-permute-start(bf16[256,2048]{1,0:T(8,128)(2,1)} %get-tuple-element.175), channel_id=1, source_target_pairs={{0,1},{1,0},{2,3},{3,2},{4,5},{5,4},{6,7},{7,6},{8,9},{9,8},{10,11... | collective-permute-start | bytes 3145736 | tf_op jit(solution)/shard_map/ppermute | solution.py:326
  406.5 26.0 %collective-permute-start.30 = (bf16[256,2048]{1,0:T(8,128)(2,1)S(1)}, bf16[256,2048]{1,0:T(8,128)(2,1)}, u32[]{:S(2)}, u32[]{:S(2)}) collective-permute-start(bf16[256,2048]{1,0:T(8,128)(2,1)S(1)} %get-tuple-element.164), channel_id=1, source_target_pairs={{0,1},{1,0},{2,3},{3,2},{4,5},{5,4},{6,7},{7,6},{8,9},{9,8},{10,11... | collective-permute-start | bytes 3145736 | tf_op jit(solution)/shard_map/ppermute | solution.py:326
  428.2 4.3 collective-permute-start.32
  428.8 93.5 %collective-permute-start.25 = (bf16[256,2048]{1,0:T(8,128)(2,1)}, bf16[256,2048]{1,0:T(8,128)(2,1)}, u32[]{:S(2)}, u32[]{:S(2)}) collective-permute-start(bf16[256,2048]{1,0:T(8,128)(2,1)} %get-tuple-element.174), channel_id=1, source_target_pairs={{0,1},{1,0},{2,3},{3,2},{4,5},{5,4},{6,7},{7,6},{8,9},{9,8},{10,11... | collective-permute-start | bytes 3145736 | tf_op jit(solution)/shard_map/ppermute | solution.py:326
  440.3 80.8 %collective-permute-start.33 = (bf16[256,2048]{1,0:T(8,128)(2,1)}, bf16[256,2048]{1,0:T(8,128)(2,1)}, u32[]{:S(2)}, u32[]{:S(2)}) collective-permute-start(bf16[256,2048]{1,0:T(8,128)(2,1)} %fusion.33), channel_id=1, source_target_pairs={{0,8},{2,10},{4,12},{6,14},{8,0},{10,2},{12,4},{14,6},{16,24},{18,... | collective-permute-start | bytes 3145736 | tf_op jit(solution)/shard_map/ppermute | solution.py:297
  447.5 33.5 %collective-permute-start.34 = (bf16[176,2048]{1,0:T(8,128)(2,1)}, bf16[176,2048]{1,0:T(8,128)(2,1)}, u32[]{:S(2)}, u32[]{:S(2)}) collective-permute-start(bf16[176,2048]{1,0:T(8,128)(2,1)} %get-tuple-element.189), channel_id=1, source_target_pairs={{0,8},{2,10},{4,12},{6,14},{8,24},{10,26},{12,28},{14,30},{16,0},{... | collective-permute-start | bytes 2162696 | tf_op jit(solution)/shard_map/ppermute | solution.py:297
  448.1 32.9 %collective-permute-start.35 = (bf16[176,2048]{1,0:T(8,128)(2,1)S(1)}, bf16[176,2048]{1,0:T(8,128)(2,1)}, u32[]{:S(2)}, u32[]{:S(2)}) collective-permute-start(bf16[176,2048]{1,0:T(8,128)(2,1)S(1)} %get-tuple-element.188), channel_id=1, source_target_pairs={{8,16},{10,18},{12,20},{14,22},{16,8},{18,10},{20,12},{22,14},{9,1... | collective-permute-start | bytes 2162696 | tf_op jit(solution)/shard_map/ppermute | solution.py:297
  459.6 56.1 %all-to-all-start.3 = ((bf16[4,128,1536]{2,1,0:T(8,128)(2,1)}), bf16[4,128,1536]{2,1,0:T(8,128)(2,1)S(1)}, u32[]{:S(2)}, u32[]{:S(2)}) async-start(bf16[4,128,1536]{2,1,0:T(8,128)(2,1)} %reduce-scatter.5.cloned.1.call-done), calls=%async_computation.5 | async-start | bytes 3145728 | tf_op jit(solution)/shard_map/all_to_all | solution.py:312
  541.6 8.1 %collective-permute-start.37 = (bf16[256,2048]{1,0:T(8,128)(2,1)S(1)}, bf16[256,2048]{1,0:T(8,128)(2,1)}, u32[]{:S(2)}, u32[]{:S(2)}) collective-permute-start(bf16[256,2048]{1,0:T(8,128)(2,1)S(1)} %get-tuple-element.173), channel_id=1, source_target_pairs={{0,1},{1,0},{2,3},{3,2},{4,5},{5,4},{6,7},{7,6},{8,9},{9,8},{10,11... | collective-permute-start | bytes 3145736 | tf_op jit(solution)/shard_map/ppermute | solution.py:326
  541.6 42.7 %all-to-all-start.4 = ((bf16[4,128,1280]{2,1,0:T(8,128)(2,1)}), bf16[4,128,1280]{2,1,0:T(8,128)(2,1)}, u32[]{:S(2)}, u32[]{:S(2)}) async-start(bf16[4,128,1280]{2,1,0:T(8,128)(2,1)} %reduce-scatter.9.cloned.1.call-done), calls=%async_computation.7 | async-start | bytes 2621440 | tf_op jit(solution)/shard_map/all_to_all | solution.py:312
  546.2 19.3 %collective-permute-start.41 = (bf16[4,128,640]{2,1,0:T(8,128)(2,1)}, bf16[4,128,640]{2,1,0:T(8,128)(2,1)S(1)}, u32[]{:S(2)}, u32[]{:S(2)}) collective-permute-start(bf16[4,128,640]{2,1,0:T(8,128)(2,1)} %get-tuple-element.180), channel_id=1, source_target_pairs={{0,6},{2,4},{4,2},{6,0},{8,14},{10,12},{12,10},{14,8},{16,22},{18,... | collective-permute-start | bytes 1966088 | tf_op jit(solution)/shard_map/ppermute | solution.py:320
  547.9 30.9 %collective-permute-start.40 = (bf16[4,128,640]{2,1,0:T(8,128)(2,1)}, bf16[4,128,640]{2,1,0:T(8,128)(2,1)S(1)}, u32[]{:S(2)}, u32[]{:S(2)}) collective-permute-start(bf16[4,128,640]{2,1,0:T(8,128)(2,1)} %get-tuple-element.181), channel_id=1, source_target_pairs={{0,4},{2,6},{4,0},{6,2},{8,12},{10,14},{12,8},{14,10},{16,20},{18,... | collective-permute-start | bytes 1966088 | tf_op jit(solution)/shard_map/ppermute | solution.py:320
  548.7 30.1 %collective-permute-start.39 = (bf16[4,128,640]{2,1,0:T(8,128)(2,1)}, bf16[4,128,640]{2,1,0:T(8,128)(2,1)S(1)}, u32[]{:S(2)}, u32[]{:S(2)}) collective-permute-start(bf16[4,128,640]{2,1,0:T(8,128)(2,1)} %get-tuple-element.182), channel_id=1, source_target_pairs={{0,2},{2,0},{4,6},{6,4},{8,10},{10,8},{12,14},{14,12},{16,18},{18,... | collective-permute-start | bytes 1966088 | tf_op jit(solution)/shard_map/ppermute | solution.py:320
  549.7 58.0 %collective-permute-start.36 = (bf16[256,2048]{1,0:T(8,128)(2,1)}, bf16[256,2048]{1,0:T(8,128)(2,1)}, u32[]{:S(2)}, u32[]{:S(2)}) collective-permute-start(bf16[256,2048]{1,0:T(8,128)(2,1)} %get-tuple-element.172), channel_id=1, source_target_pairs={{0,1},{1,0},{2,3},{3,2},{4,5},{5,4},{6,7},{7,6},{8,9},{9,8},{10,11... | collective-permute-start | bytes 3145736 | tf_op jit(solution)/shard_map/ppermute | solution.py:326
  552.9 54.8 %collective-permute-start.38 = (bf16[256,2048]{1,0:T(8,128)(2,1)}, bf16[256,2048]{1,0:T(8,128)(2,1)}, u32[]{:S(2)}, u32[]{:S(2)}) collective-permute-start(bf16[256,2048]{1,0:T(8,128)(2,1)} %fusion.29), channel_id=1, source_target_pairs={{0,8},{2,10},{4,12},{6,14},{8,0},{10,2},{12,4},{14,6},{16,24},{18,... | collective-permute-start | bytes 3145736 | tf_op jit(solution)/shard_map/ppermute | solution.py:297
  580.0 21.1 %collective-permute-start.44 = (bf16[128,640]{1,0:T(8,128)(2,1)}, bf16[128,640]{1,0:T(8,128)(2,1)S(1)}, u32[]{:S(2)}, u32[]{:S(2)}) collective-permute-start(bf16[128,640]{1,0:T(8,128)(2,1)} %get-tuple-element.190), channel_id=1, source_target_pairs={{0,24},{2,26},{4,28},{6,30},{8,16},{10,18},{12,20},{14,22},{16,8},... | collective-permute-start | bytes 491528 | tf_op jit(solution)/shard_map/ppermute | solution.py:297
  583.4 20.1 %collective-permute-start.43 = (bf16[128,640]{1,0:T(8,128)(2,1)}, bf16[128,640]{1,0:T(8,128)(2,1)S(1)}, u32[]{:S(2)}, u32[]{:S(2)}) collective-permute-start(bf16[128,640]{1,0:T(8,128)(2,1)} %get-tuple-element.191), channel_id=1, source_target_pairs={{0,8},{2,10},{4,12},{6,14},{8,0},{10,2},{12,4},{14,6},{16,24},{18,... | collective-permute-start | bytes 491528 | tf_op jit(solution)/shard_map/ppermute | solution.py:297
  583.4 21.4 %collective-permute-start.42 = (bf16[128,640]{1,0:T(8,128)(2,1)}, bf16[128,640]{1,0:T(8,128)(2,1)S(1)}, u32[]{:S(2)}, u32[]{:S(2)}) collective-permute-start(bf16[128,640]{1,0:T(8,128)(2,1)} %get-tuple-element.192), channel_id=1, source_target_pairs={{0,16},{2,18},{4,20},{6,22},{8,24},{10,26},{12,28},{14,30},{16,0},... | collective-permute-start | bytes 491528 | tf_op jit(solution)/shard_map/ppermute | solution.py:297
  601.1 24.8 %collective-permute-start.45 = (bf16[64,2048]{1,0:T(8,128)(2,1)}, bf16[64,2048]{1,0:T(8,128)(2,1)S(1)}, u32[]{:S(2)}, u32[]{:S(2)}) collective-permute-start(bf16[64,2048]{1,0:T(8,128)(2,1)} %get-tuple-element.198), channel_id=1, source_target_pairs={{0,8},{2,10},{4,12},{6,14},{8,24},{10,26},{12,28},{14,30},{16,0},{... | collective-permute-start | bytes 786440 | tf_op jit(solution)/shard_map/ppermute | solution.py:297
  603.4 22.4 %collective-permute-start.46 = (bf16[64,2048]{1,0:T(8,128)(2,1)}, bf16[64,2048]{1,0:T(8,128)(2,1)}, u32[]{:S(2)}, u32[]{:S(2)}) collective-permute-start(bf16[64,2048]{1,0:T(8,128)(2,1)} %get-tuple-element.199), channel_id=1, source_target_pairs={{8,16},{10,18},{12,20},{14,22},{16,8},{18,10},{20,12},{22,14},{9,1... | collective-permute-start | bytes 786440 | tf_op jit(solution)/shard_map/ppermute | solution.py:297
  612.0 11.9 %all-to-all-start.5 = ((f32[32,1,128]{2,1,0:T(1,128)}), f32[32,1,128]{2,1,0:T(1,128)S(1)}, u32[]{:S(2)}, u32[]{:S(2)}) async-start(f32[32,1,128]{2,1,0:T(1,128)} %reshape.724), calls=%async_computation.9 | async-start | bytes 32768 | tf_op jit(solution)/shard_map/all_to_all | solution.py:708
  (110 other events, 820.3 us)
Sparse Core Ops, SparseCore 0:
  50.3 89.6 all-gather.3
  153.3 70.3 all-gather.5
  226.1 65.7 all-gather.7
  310.3 65.1 reduce-scatter.6
  378.3 70.1 reduce-scatter.4
  451.4 61.4 reduce-scatter.8
  516.4 35.1 reduce-scatter.10

commit v3 on v2

--- a/solution.py
+++ b/solution.py
@@ -523,9 +523,8 @@
         mixed_groups.append(jnp.concatenate(mixed_parts, axis=1))
     mixed = jnp.concatenate(mixed_groups).reshape(token_count, query_width).astype(bf_type)
     attended = scatter_tokens(
-        jnp.dot(
-            after(mixed, contract_both, out_grad_all), mixing_low, preferred_element_type=fl_type
-        )
+        jnp.dot(after(mixed, out_grad_all), mixing_low, preferred_element_type=fl_type),
+        lambda: (contract_both,),
     )
     middle = input_rows + attended
     normed_two = normalize(middle, gain_rows[1]).astype(bf_type)

time: 645 us -> 641 us (level)
  starting transfers between devices: 86.8 us -> 77.9 us
  waiting for transfers between devices: 227 us -> 234 us
    all_to_all x4, waiting for transfers between devices: 11.6 us -> 39.8 us  [spread(): lax.all_to_all(blocks, 'dp', split_axis=0, concat_axis=0, tiled=True, axi...]
    ppermute x22, waiting for transfers between devices: 137 us -> 117 us  [move(): lax.ppermute(value, 'dp', [(place * low_count + low, goal * low_count + l...]
    ppermute x22, starting transfers between devices: 45.3 us -> 37.7 us  [move(): lax.ppermute(value, 'dp', [(place * low_count + low, goal * low_count + l...]
    unnamed x234 -> x228, local copies, waits for them, and re-layouts: 28.3 us -> 30.1 us
  transfers between devices with their start and end apart: 60 -> 60, of which waited for: 21 -> 18; matrix products, arithmetic and copies ran while one was open for 40% -> 40% of each run, Pallas kernels for 3% -> 3%
where the time goes in v3:
time: 641 us; the launch traced here: 633 us
  waiting for transfers between devices  234 us (37%)
  matrix products  155 us (24%)
  other arithmetic  88.4 us (14%)
  starting transfers between devices  77.9 us (12%)
  local copies, waits for them, and re-layouts  40.9 us (6%)
  Pallas kernels  21.1 us (3%)
  between operations  16.3 us (3%)
    ppermute x22, waiting for transfers between devices, move(): lax.ppermute(value, 'dp', [(place * low_count + low, goal * low_count + l...  117 us
    ppermute x9, waiting for transfers between devices, swap_low(): lax.ppermute(value, 'dp', [(index, index ^ flip) for index in range(dp_co...  56.9 us
    all_to_all x4, waiting for transfers between devices, spread(): lax.all_to_all(blocks, 'dp', split_axis=0, concat_axis=0, tiled=True, axi...  39.8 us
    ppermute x22, starting transfers between devices, move(): lax.ppermute(value, 'dp', [(place * low_count + low, goal * low_count + l...  37.7 us
    unnamed x228, local copies, waits for them, and re-layouts  30.1 us
    dot_general x2, matrix products, gated(): gate_up = jnp.dot(rows, weights, preferred_element_type=fl_type)  20.3 us
    all_to_all x4, starting transfers between devices, spread(): lax.all_to_all(blocks, 'dp', split_axis=0, concat_axis=0, tiled=True, axi...  17.6 us
    all_to_all x1, waiting for transfers between devices, per_device(): lax.all_to_all(jnp.broadcast_to(own_facts[None], (2 * dp_count, own_facts...  14.4 us
  transfers between devices with their start and end apart: 60, of which 18 were waited for; matrix products, arithmetic and copies ran while one was open for 40% of the time, Pallas kernels for 3%

profile of v3, /device:TPU:0, one launch (start us, length us, event | category | flops | bytes accessed | tf_op | source)
XLA Modules:
  0.0 632.8 jit_solution(3452532173278660484)
XLA Ops:
  9.1 3.4 shard_map.468
  13.6 5.0 collective-permute-start.24
  22.5 4.3 all-to-all-start
  26.8 2.7 collective-permute-start.23
  29.8 14.4 %all-to-all-done = f32[32,1,646]{2,1,0:T(1,128)S(1)} async-done(((f32[32,1,646]{2,1,0:T(1,128)}), f32[32,1,646]{2,1,0:T(1,128)S(1)}, u32[]{:S(2)}, u32[]{:S(2)}) %all-to-all-start) | async-done | bytes 82720 | tf_op jit(solution)/shard_map/all_to_all | solution.py:417
  52.1 4.9 collective-permute-start.1
  57.2 3.5 all-to-all-start.1
  61.1 29.5 %all-to-all-done.1.refs_0_ = bf16[4,128,640]{2,1,0:T(8,128)(2,1)S(1)} async-done(((bf16[4,128,640]{2,1,0:T(8,128)(2,1)}), bf16[4,128,640]{2,1,0:T(8,128)(2,1)S(1)}, u32[]{:S(2)}, u32[]{:S(2)}) %all-to-all-start.1) | async-done | bytes 655392 | tf_op jit(solution)/shard_map/all_to_all | solution.py:312
  90.7 4.3 all-to-all-start.2
  101.6 25.1 %collective-permute-done.5.refs_3_ = bf16[4,128,640]{2,1,0:T(8,128)(2,1)S(1)} collective-permute-done((bf16[4,128,640]{2,1,0:T(8,128)(2,1)S(1)}, bf16[4,128,640]{2,1,0:T(8,128)(2,1)S(1)}, u32[]{:S(2)}, u32[]{:S(2)}) %collective-permute-start.5) | collective-permute-done | bytes 655392 | tf_op jit(solution)/shard_map/ppermute | solution.py:320
  126.7 13.0 %collective-permute-done.4.refs_2_ = bf16[4,128,640]{2,1,0:T(8,128)(2,1)S(1)} collective-permute-done((bf16[4,128,640]{2,1,0:T(8,128)(2,1)S(1)}, bf16[4,128,640]{2,1,0:T(8,128)(2,1)S(1)}, u32[]{:S(2)}, u32[]{:S(2)}) %collective-permute-start.4) | collective-permute-done | bytes 655392 | tf_op jit(solution)/shard_map/ppermute | solution.py:320
  147.2 4.1 fusion.131
  162.6 2.5 fusion.45
  165.0 5.2 collective-permute-done.9
  190.2 3.3 collective-permute-start.16
  196.0 36.9 %collective-permute-done.18 = bf16[176,2048]{1,0:T(8,128)(2,1)} collective-permute-done((bf16[176,2048]{1,0:T(8,128)(2,1)}, bf16[176,2048]{1,0:T(8,128)(2,1)}, u32[]{:S(2)}, u32[]{:S(2)}) %collective-permute-start.18) | collective-permute-done | bytes 720928 | tf_op jit(solution)/shard_map/ppermute | solution.py:297
  232.9 2.7 maximum_select_fusion
  235.7 2.9 multiply_reduce_fusion.2
  241.9 23.1 %collective-permute-done.20 = bf16[256,2048]{1,0:T(8,128)(2,1)S(1)} collective-permute-done((bf16[256,2048]{1,0:T(8,128)(2,1)S(1)}, bf16[256,2048]{1,0:T(8,128)(2,1)S(1)}, u32[]{:S(2)}, u32[]{:S(2)}) %collective-permute-start.20) | collective-permute-done | bytes 1048608 | tf_op jit(solution)/shard_map/ppermute | solution.py:297
  265.0 2.6 collective-permute-done.21
  268.6 2.8 pad_maximum_fusion.1
  271.4 10.3 %fusion.118 = f32[1024,1280]{1,0:T(8,128)S(1)} fusion(bf16[2048,1280]{1,0:T(8,128)(2,1)} %bitcast.234, bf16[256,2048]{1,0:T(8,128)(2,1)} %copy-done.72, bf16[256,2048]{1,0:T(8,128)(2,1)} %copy-done.68, bf16[256,2048]{1,0:T(8,128)(2,1)} %copy-done.70, bf16[256,2048]{1,0:T(8,128)(2,1)S(1)} %multiply_convert_fusion.6), kind=kOutput, calls=%fused_computation.255 | convolution fusion | flops 5385486336 | bytes 14680064 | tf_op jit(solution)/shard_map/dot_general | solution.py:533
  284.8 10.0 %fusion.137 = f32[1024,1536]{1,0:T(8,128)S(1)} fusion(bf16[1024,2048]{1,0:T(8,128)(2,1)} %pad_maximum_fusion.1, bf16[2048,1536]{1,0:T(8,128)(2,1)} %bitcast.226), kind=kOutput, calls=%fused_computation.272 | convolution fusion | flops 6442450944 | bytes 16777216 | tf_op jit(solution)/shard_map/dot_general | solution.py:533
  294.8 2.6 copy-done.30
  299.6 8.0 %convolution_convert_fusion.2 = bf16[1408,2048]{1,0:T(8,128)(2,1)} fusion(bf16[1024,2048]{1,0:T(8,128)(2,1)S(1)} %copy-done.81, bf16[1024,768]{1,0:T(8,128)(2,1)S(1)} %multiply_convert_fusion.2, bf16[1024,640]{1,0:T(8,128)(2,1)S(1)} %multiply_convert_fusion.5), kind=kOutput, calls=%fused_computation.20 | convolution fusion | flops 5914230784 | bytes 12845056 | tf_op jit(solution)/shard_map/dot_general | solution.py:561
  307.7 10.7 %fusion.138 = f32[1024,1408]{1,0:T(8,128)S(1)} fusion(bf16[1024,2048]{1,0:T(8,128)(2,1)} %copy-done.80, bf16[1408,2048]{1,0:T(8,128)(2,1)} %bitcast.230), kind=kOutput, calls=%fused_computation.273 | convolution fusion | flops 5905580032 | bytes 15728640 | tf_op jit(solution)/shard_map/dot_general | solution.py:565
  318.5 5.8 multiply_convert_fusion.1
  324.7 8.8 %convolution_convert_fusion.1 = bf16[2048,1536]{1,0:T(8,128)(2,1)} fusion(bf16[1024,768]{1,0:T(8,128)(2,1)S(1)} %get-tuple-element.171, bf16[1024,768]{1,0:T(8,128)(2,1)S(1)} %get-tuple-element.170, bf16[256,2048]{1,0:T(8,128)(2,1)S(1)} %copy-done.73, bf16[256,2048]{1,0:T(8,128)(2,1)S(1)} %copy-done.69, bf16[256,2048]{1,0:T(8,128)(2,1)S(1)} %copy-done.71, ...), kind=kOutput, calls=%fused_computation.19 | convolution fusion | flops 6468665344 | bytes 13631488 | tf_op jit(solution)/shard_map/dot_general | solution.py:578
  335.7 4.8 multiply_convert_fusion.4
  340.5 7.5 %convolution_convert_fusion = bf16[2048,1280]{1,0:T(8,128)(2,1)} fusion(bf16[1024,2048]{1,0:T(8,128)(2,1)S(1)} %copy-done.49, bf16[1024,640]{1,0:T(8,128)(2,1)S(1)} %get-tuple-element.173, bf16[1024,640]{1,0:T(8,128)(2,1)S(1)} %get-tuple-element.172), kind=kOutput, calls=%fused_computation.18 | convolution fusion | flops 5376573440 | bytes 12058624 | tf_op jit(solution)/shard_map/dot_general | solution.py:581
  348.0 8.9 %fusion.139 = f32[1024,2048]{1,0:T(8,128)} fusion(bf16[1024,1536]{1,0:T(8,128)(2,1)S(1)} %pad_maximum_fusion.3, bf16[2048,1536]{1,0:T(8,128)(2,1)S(1)} %bitcast.229), kind=kOutput, calls=%fused_computation.274 | convolution fusion | flops 6442450944 | bytes 17825792 | tf_op jit(solution)/shard_map/dot_general | solution.py:588
  357.0 10.0 %fusion.135 = (bf16[1024,2048]{1,0:T(8,128)(2,1)S(1)}, f32[1024,2048]{1,0:T(8,128)S(1)}) fusion(f32[1024,2048]{1,0:T(8,128)} %fusion.139, bf16[2048,1280]{1,0:T(8,128)(2,1)} %bitcast.235, bf16[1024,640]{1,0:T(8,128)(2,1)} %copy-done.61, bf16[1024,640]{1,0:T(8,128)(2,1)} %copy-done.60), kind=kOutput, calls=%fused_computation.268 | convolution fusion | flops 5378146304 | bytes 28835840 | tf_op jit(solution)/shard_map/dot_general | solution.py:590
  371.8 8.8 %fusion.134 = (bf16[1024,2048]{1,0:T(8,128)(2,1)S(1)}, f32[1024,2048]{1,0:T(8,128)}) fusion(bf16[1024,1408]{1,0:T(8,128)(2,1)S(1)} %pad_maximum_fusion.4, bf16[1408,2048]{1,0:T(8,128)(2,1)S(1)} %bitcast.233), kind=kOutput, calls=%fused_computation.267 | convolution fusion | flops 5907677184 | bytes 21233664 | tf_op jit(solution)/shard_map/dot_general | solution.py:591
  380.6 15.1 %collective-permute-done.29 = bf16[256,2048]{1,0:T(8,128)(2,1)S(1)} collective-permute-done((bf16[256,2048]{1,0:T(8,128)(2,1)S(1)}, bf16[256,2048]{1,0:T(8,128)(2,1)S(1)}, u32[]{:S(2)}, u32[]{:S(2)}) %collective-permute-start.29) | collective-permute-done | bytes 1048608 | tf_op jit(solution)/shard_map/ppermute | solution.py:297
  397.1 3.7 fusion.122
  404.2 21.3 %collective-permute-done.31 = bf16[256,2048]{1,0:T(8,128)(2,1)} collective-permute-done((bf16[256,2048]{1,0:T(8,128)(2,1)S(1)}, bf16[256,2048]{1,0:T(8,128)(2,1)}, u32[]{:S(2)}, u32[]{:S(2)}) %collective-permute-start.31) | collective-permute-done | bytes 1048608 | tf_op jit(solution)/shard_map/ppermute | solution.py:297
  426.7 3.1 fusion.33
  432.0 5.7 convolution_convert_fusion.4
  439.0 3.4 convolution_convert_fusion.5
  447.3 5.4 fusion.3
  453.1 3.9 fusion.5
  457.1 5.4 all-to-all-start.3
  462.5 4.0 fusion.41
  466.5 11.8 %collective-permute-done.34 = bf16[176,2048]{1,0:T(8,128)(2,1)} collective-permute-done((bf16[176,2048]{1,0:T(8,128)(2,1)}, bf16[176,2048]{1,0:T(8,128)(2,1)}, u32[]{:S(2)}, u32[]{:S(2)}) %collective-permute-start.34) | collective-permute-done | bytes 720928 | tf_op jit(solution)/shard_map/ppermute | solution.py:297
  478.3 4.9 fusion.54
  483.2 11.8 %fusion.2 = bf16[8,512,512]{1,2,0:T(8,128)(2,1)} fusion(f32[8,512,512]{1,2,0:T(8,128)} %copy-done.22, f32[8,512]{1,0:T(8,128)} %log_add_fusion.1, bf16[1024,8,64]{0,2,1:T(8,128)(2,1)S(1)} %bitcast.211, bf16[1024,640]{0,1:T(8,128)(2,1)} %get-tuple-element.219), kind=kOutput, calls=%fused_computation.4 | convolution fusion | flops 549458432 | bytes 22183936 | tf_op jit(solution)/shard_map/sub | solution.py:629
  495.0 5.6 fusion.57
  502.7 10.2 %all-to-all-done.3.refs_1_ = bf16[4,128,1536]{2,1,0:T(8,128)(2,1)S(1)} async-done(((bf16[4,128,1536]{2,1,0:T(8,128)(2,1)}), bf16[4,128,1536]{2,1,0:T(8,128)(2,1)S(1)}, u32[]{:S(2)}, u32[]{:S(2)}) %all-to-all-start.3) | async-done | bytes 1572896 | tf_op jit(solution)/shard_map/all_to_all | solution.py:312
  512.9 3.6 fusion.40
  521.2 4.0 fusion.36
  525.2 3.8 convolution_convert_fusion.3
  531.7 5.9 fusion.136
  538.7 4.4 all-to-all-start.4
  546.8 3.2 fusion.29
  551.8 5.3 multiply_add_fusion.1
  557.1 5.6 collective-permute-done.41
  562.6 13.2 %collective-permute-done.40 = bf16[4,128,640]{2,1,0:T(8,128)(2,1)S(1)} collective-permute-done((bf16[4,128,640]{2,1,0:T(8,128)(2,1)}, bf16[4,128,640]{2,1,0:T(8,128)(2,1)S(1)}, u32[]{:S(2)}, u32[]{:S(2)}) %collective-permute-start.40) | collective-permute-done | bytes 655392 | tf_op jit(solution)/shard_map/ppermute | solution.py:320
  577.0 3.4 collective-permute-start.44
  584.7 13.4 %shard_map.471 = (f32[128,2,2816]{2,1,0:T(2,128)}, f32[128,2,2816]{2,1,0:T(2,128)}, f32[128,2,2816]{2,1,0:T(2,128)}, f32[128,2,2816]{2,1,0:T(2,128)}) custom-call(bf16[4,128,1280]{2,1,0:T(8,128)(2,1)} %all-to-all-done.4.refs_0_, bf16[4,128,1536]{2,1,0:T(8,128)(2,1)S(1)} %copy-done.5, f32[128,2,2816]{2,1,0:T(2,128)S(1)} %copy-done.1, ...), custom_call_target="tpu_custom_call" | custom-call | tf_op jit(solution)/shard_map/pallas_call | solution.py:242
  601.9 2.9 shard_map.472
  604.8 3.3 fusion.24
  609.0 4.9 all-to-all-start.5
  614.0 5.2 fusion.26
  622.9 2.7 multiply_add_fusion.3
  (426 shorter events, 124.3 us)
Async XLA Ops:
  13.6 32.7 %collective-permute-start.24 = (bf16[128,1280]{1,0:T(8,128)(2,1)S(1)}, bf16[128,1280]{1,0:T(8,128)(2,1)S(1)}, u32[]{:S(2)}, u32[]{:S(2)}) collective-permute-start(bf16[128,1280]{1,0:T(8,128)(2,1)S(1)} %get-tuple-element.101), channel_id=1, source_target_pairs={{0,24},{2,26},{4,28},{6,30},{8,16},{10,18},{12,20},{14,22},{16,8},... | collective-permute-start | bytes 983048 | tf_op jit(solution)/shard_map/ppermute | solution.py:297
  18.7 27.7 %collective-permute-start.22 = (bf16[128,1280]{1,0:T(8,128)(2,1)S(1)}, bf16[128,1280]{1,0:T(8,128)(2,1)S(1)}, u32[]{:S(2)}, u32[]{:S(2)}) collective-permute-start(bf16[128,1280]{1,0:T(8,128)(2,1)S(1)} %get-tuple-element.101), channel_id=1, source_target_pairs={{0,8},{2,10},{4,12},{6,14},{8,0},{10,2},{12,4},{14,6},{16,24},{18,... | collective-permute-start | bytes 983048 | tf_op jit(solution)/shard_map/ppermute | solution.py:297
  22.5 21.7 %all-to-all-start = ((f32[32,1,646]{2,1,0:T(1,128)}), f32[32,1,646]{2,1,0:T(1,128)S(1)}, u32[]{:S(2)}, u32[]{:S(2)}) async-start(f32[32,1,646]{2,1,0:T(1,128)} %broadcast_in_dim.52), calls=%async_computation | async-start | bytes 196608 | tf_op jit(solution)/shard_map/all_to_all | solution.py:417
  26.7 244.6 %all-gather.4.cloned.1.call-start = ((), (), s32[]{:S(2)}) async-start(), calls=%async_computation.10 | async-start | bytes 6553600 | tf_op jit(solution)/shard_map/all_gather | solution.py:335
  26.8 21.9 %collective-permute-start.23 = (bf16[128,1280]{1,0:T(8,128)(2,1)S(1)}, bf16[128,1280]{1,0:T(8,128)(2,1)S(1)}, u32[]{:S(2)}, u32[]{:S(2)}) collective-permute-start(bf16[128,1280]{1,0:T(8,128)(2,1)S(1)} %get-tuple-element.102), channel_id=1, source_target_pairs={{0,16},{2,18},{4,20},{6,22},{8,24},{10,26},{12,28},{14,30},{16,0},... | collective-permute-start | bytes 983048 | tf_op jit(solution)/shard_map/ppermute | solution.py:297
  50.3 10.8 %collective-permute-start.7 = (bf16[64,2048]{1,0:T(8,128)(2,1)S(1)}, bf16[64,2048]{1,0:T(8,128)(2,1)S(1)}, u32[]{:S(2)}, u32[]{:S(2)}) collective-permute-start(bf16[64,2048]{1,0:T(8,128)(2,1)S(1)} %convert_element_type.222), channel_id=1, source_target_pairs={{0,16},{2,18},{4,20},{6,22},{8,0},{10,2},{12,4},{14,6},{16,24},{18... | collective-permute-start | bytes 786440 | tf_op jit(solution)/shard_map/ppermute | solution.py:297
  50.3 10.7 %collective-permute-start.6 = (bf16[64,2048]{1,0:T(8,128)(2,1)S(1)}, bf16[64,2048]{1,0:T(8,128)(2,1)S(1)}, u32[]{:S(2)}, u32[]{:S(2)}) collective-permute-start(bf16[64,2048]{1,0:T(8,128)(2,1)S(1)} %convert_element_type.222), channel_id=1, source_target_pairs={{8,16},{10,18},{12,20},{14,22},{16,8},{18,10},{20,12},{22,14},{9,1... | collective-permute-start | bytes 786440 | tf_op jit(solution)/shard_map/ppermute | solution.py:297
  52.1 46.8 %copy-start.98 = (f32[32]{0:T(128)}, f32[32]{0:T(128)S(1)}, u32[]{:S(2)}) copy-start(f32[32]{0:T(128)S(1)} %multiply_power_fusion) | copy-start | bytes 388
  52.1 42.9 %collective-permute-start.1 = (bf16[256,2048]{1,0:T(8,128)(2,1)}, bf16[256,2048]{1,0:T(8,128)(2,1)}, u32[]{:S(2)}, u32[]{:S(2)}) collective-permute-start(bf16[256,2048]{1,0:T(8,128)(2,1)} %fusion.23), channel_id=1, source_target_pairs={{0,8},{2,10},{4,12},{6,14},{8,0},{10,2},{12,4},{14,6},{16,24},{18,... | collective-permute-start | bytes 3145736 | tf_op jit(solution)/shard_map/ppermute | solution.py:297
  57.0 86.5 %collective-permute-start = (bf16[256,2048]{1,0:T(8,128)(2,1)}, bf16[256,2048]{1,0:T(8,128)(2,1)}, u32[]{:S(2)}, u32[]{:S(2)}) collective-permute-start(bf16[256,2048]{1,0:T(8,128)(2,1)} %fusion.23), channel_id=1, source_target_pairs={{0,1},{1,0},{2,3},{3,2},{4,5},{5,4},{6,7},{7,6},{8,9},{9,8},{10,11... | collective-permute-start | bytes 3145736 | tf_op jit(solution)/shard_map/ppermute | solution.py:326
  57.2 33.5 %all-to-all-start.1 = ((bf16[4,128,640]{2,1,0:T(8,128)(2,1)}), bf16[4,128,640]{2,1,0:T(8,128)(2,1)S(1)}, u32[]{:S(2)}, u32[]{:S(2)}) async-start(bf16[4,128,640]{2,1,0:T(8,128)(2,1)} %shard_map.467), calls=%async_computation.1 | async-start | bytes 1310720 | tf_op jit(solution)/shard_map/all_to_all | solution.py:312
  90.7 62.1 %all-to-all-start.2 = ((bf16[4,128,1536]{2,1,0:T(8,128)(2,1)}), bf16[4,128,1536]{2,1,0:T(8,128)(2,1)}, u32[]{:S(2)}, u32[]{:S(2)}) async-start(bf16[4,128,1536]{2,1,0:T(8,128)(2,1)} %copy-done.8), calls=%async_computation.2 | async-start | bytes 3145728 | tf_op jit(solution)/shard_map/all_to_all | solution.py:312
  95.0 189.7 %all-gather.6.cloned.1.call-start = ((), (), s32[]{:S(2)}) async-start(), calls=%async_computation.11 | async-start | bytes 7864320 | tf_op jit(solution)/shard_map/all_gather | solution.py:335
  95.1 48.5 %collective-permute-start.2 = (bf16[256,2048]{1,0:T(8,128)(2,1)}, bf16[256,2048]{1,0:T(8,128)(2,1)S(1)}, u32[]{:S(2)}, u32[]{:S(2)}) collective-permute-start(bf16[256,2048]{1,0:T(8,128)(2,1)} %collective-permute-done.1), channel_id=1, source_target_pairs={{0,1},{1,0},{2,3},{3,2},{4,5},{5,4},{6,7},{7,6},{8,9},{9,8},{10,11... | collective-permute-start | bytes 3145736 | tf_op jit(solution)/shard_map/ppermute | solution.py:326
  95.2 57.9 %copy-start.87 = (f32[1024]{0:T(1024)}, f32[1024]{0:T(1024)S(1)}, u32[]{:S(2)}) copy-start(f32[1024]{0:T(1024)S(1)} %add_convert_fusion.3) | copy-start | bytes 12292
  95.3 31.4 %collective-permute-start.5 = (bf16[4,128,640]{2,1,0:T(8,128)(2,1)S(1)}, bf16[4,128,640]{2,1,0:T(8,128)(2,1)S(1)}, u32[]{:S(2)}, u32[]{:S(2)}) collective-permute-start(bf16[4,128,640]{2,1,0:T(8,128)(2,1)S(1)} %all-to-all-done.1.refs_0_), channel_id=1, source_target_pairs={{0,6},{2,4},{4,2},{6,0},{8,14},{10,12},{12,10},{14,8},{16,22},{18,... | collective-permute-start | bytes 1966088 | tf_op jit(solution)/shard_map/ppermute | solution.py:320
  97.8 41.9 %collective-permute-start.4 = (bf16[4,128,640]{2,1,0:T(8,128)(2,1)S(1)}, bf16[4,128,640]{2,1,0:T(8,128)(2,1)S(1)}, u32[]{:S(2)}, u32[]{:S(2)}) collective-permute-start(bf16[4,128,640]{2,1,0:T(8,128)(2,1)S(1)} %all-to-all-done.1.refs_0_), channel_id=1, source_target_pairs={{0,4},{2,6},{4,0},{6,2},{8,12},{10,14},{12,8},{14,10},{16,20},{18,... | collective-permute-start | bytes 1966088 | tf_op jit(solution)/shard_map/ppermute | solution.py:320
  98.3 41.4 %collective-permute-start.3 = (bf16[4,128,640]{2,1,0:T(8,128)(2,1)S(1)}, bf16[4,128,640]{2,1,0:T(8,128)(2,1)S(1)}, u32[]{:S(2)}, u32[]{:S(2)}) collective-permute-start(bf16[4,128,640]{2,1,0:T(8,128)(2,1)S(1)} %all-to-all-done.1.refs_0_), channel_id=1, source_target_pairs={{0,2},{2,0},{4,6},{6,4},{8,10},{10,8},{12,14},{14,12},{16,18},{18,... | collective-permute-start | bytes 1966088 | tf_op jit(solution)/shard_map/ppermute | solution.py:320
  100.1 55.4 %copy-start.62 = (f32[1024,32]{0,1:T(8,128)}, f32[1024,32]{0,1:T(8,128)S(1)}, u32[]{:S(2)}) copy-start(f32[1024,32]{0,1:T(8,128)S(1)} %get-tuple-element.208) | copy-start | bytes 393220
  140.0 34.5 %collective-permute-start.13 = (bf16[2,64,2048]{2,1,0:T(8,128)(2,1)S(1)}, bf16[2,64,2048]{2,1,0:T(8,128)(2,1)S(1)}, u32[]{:S(2)}, u32[]{:S(2)}) collective-permute-start(bf16[2,64,2048]{2,1,0:T(8,128)(2,1)S(1)} %maximum_select_fusion.2.refs_0_), channel_id=1, source_target_pairs={{0,6},{2,4},{4,2},{6,0},{8,14},{10,12},{12,10},{14,8},{16,22},{18,... | collective-permute-start | bytes 1572872 | tf_op jit(solution)/shard_map/ppermute | solution.py:320
  141.5 33.0 %collective-permute-start.12 = (bf16[2,64,2048]{2,1,0:T(8,128)(2,1)S(1)}, bf16[2,64,2048]{2,1,0:T(8,128)(2,1)S(1)}, u32[]{:S(2)}, u32[]{:S(2)}) collective-permute-start(bf16[2,64,2048]{2,1,0:T(8,128)(2,1)S(1)} %maximum_select_fusion.2.refs_0_), channel_id=1, source_target_pairs={{0,4},{2,6},{4,0},{6,2},{8,12},{10,14},{12,8},{14,10},{16,20},{18,... | collective-permute-start | bytes 1572872 | tf_op jit(solution)/shard_map/ppermute | solution.py:320
  143.0 32.3 %collective-permute-start.11 = (bf16[2,64,2048]{2,1,0:T(8,128)(2,1)S(1)}, bf16[2,64,2048]{2,1,0:T(8,128)(2,1)S(1)}, u32[]{:S(2)}, u32[]{:S(2)}) collective-permute-start(bf16[2,64,2048]{2,1,0:T(8,128)(2,1)S(1)} %maximum_select_fusion.2.refs_0_), channel_id=1, source_target_pairs={{0,2},{2,0},{4,6},{6,4},{8,10},{10,8},{12,14},{14,12},{16,18},{18,... | collective-permute-start | bytes 1572872 | tf_op jit(solution)/shard_map/ppermute | solution.py:320
  145.7 24.6 %collective-permute-start.9 = (bf16[256,2048]{1,0:T(8,128)(2,1)}, bf16[256,2048]{1,0:T(8,128)(2,1)}, u32[]{:S(2)}, u32[]{:S(2)}) collective-permute-start(bf16[256,2048]{1,0:T(8,128)(2,1)} %param.29), channel_id=1, source_target_pairs={{0,8},{2,10},{4,12},{6,14},{8,0},{10,2},{12,4},{14,6},{16,24},{18,... | collective-permute-start | bytes 3145736 | tf_op jit(solution)/shard_map/ppermute | solution.py:297
  147.2 31.1 %collective-permute-start.8 = (bf16[256,2048]{1,0:T(8,128)(2,1)}, bf16[256,2048]{1,0:T(8,128)(2,1)}, u32[]{:S(2)}, u32[]{:S(2)}) collective-permute-start(bf16[256,2048]{1,0:T(8,128)(2,1)} %param.29), channel_id=1, source_target_pairs={{0,1},{1,0},{2,3},{3,2},{4,5},{5,4},{6,7},{7,6},{8,9},{9,8},{10,11... | collective-permute-start | bytes 3145736 | tf_op jit(solution)/shard_map/ppermute | solution.py:326
  152.8 154.9 %all-gather.8.cloned.1.call-start = ((), (), s32[]{:S(2)}) async-start(), calls=%async_computation.12 | async-start | bytes 7208960 | tf_op jit(solution)/shard_map/all_gather | solution.py:335
  170.2 10.7 %collective-permute-start.10 = (bf16[256,2048]{1,0:T(8,128)(2,1)}, bf16[256,2048]{1,0:T(8,128)(2,1)S(1)}, u32[]{:S(2)}, u32[]{:S(2)}) collective-permute-start(bf16[256,2048]{1,0:T(8,128)(2,1)} %collective-permute-done.9), channel_id=1, source_target_pairs={{0,1},{1,0},{2,3},{3,2},{4,5},{5,4},{6,7},{7,6},{8,9},{9,8},{10,11... | collective-permute-start | bytes 3145736 | tf_op jit(solution)/shard_map/ppermute | solution.py:326
  184.6 4.3 collective-permute-start.15
  187.4 7.0 %collective-permute-start.17 = (bf16[176,2048]{1,0:T(8,128)(2,1)}, bf16[176,2048]{1,0:T(8,128)(2,1)}, u32[]{:S(2)}, u32[]{:S(2)}) collective-permute-start(bf16[176,2048]{1,0:T(8,128)(2,1)} %convert_element_type.233), channel_id=1, source_target_pairs={{8,16},{10,18},{12,20},{14,22},{16,8},{18,10},{20,12},{22,14},{9,1... | collective-permute-start | bytes 2162696 | tf_op jit(solution)/shard_map/ppermute | solution.py:297
  190.2 45.4 %collective-permute-start.16 = (bf16[256,2048]{1,0:T(8,128)(2,1)}, bf16[256,2048]{1,0:T(8,128)(2,1)}, u32[]{:S(2)}, u32[]{:S(2)}) collective-permute-start(bf16[256,2048]{1,0:T(8,128)(2,1)} %fusion.37), channel_id=1, source_target_pairs={{0,8},{2,10},{4,12},{6,14},{8,0},{10,2},{12,4},{14,6},{16,24},{18,... | collective-permute-start | bytes 3145736 | tf_op jit(solution)/shard_map/ppermute | solution.py:297
  193.6 42.1 %collective-permute-start.14 = (bf16[256,2048]{1,0:T(8,128)(2,1)}, bf16[256,2048]{1,0:T(8,128)(2,1)}, u32[]{:S(2)}, u32[]{:S(2)}) collective-permute-start(bf16[256,2048]{1,0:T(8,128)(2,1)} %get-tuple-element.180), channel_id=1, source_target_pairs={{0,1},{1,0},{2,3},{3,2},{4,5},{5,4},{6,7},{7,6},{8,9},{9,8},{10,11... | collective-permute-start | bytes 3145736 | tf_op jit(solution)/shard_map/ppermute | solution.py:326
  193.6 39.3 %collective-permute-start.18 = (bf16[176,2048]{1,0:T(8,128)(2,1)}, bf16[176,2048]{1,0:T(8,128)(2,1)}, u32[]{:S(2)}, u32[]{:S(2)}) collective-permute-start(bf16[176,2048]{1,0:T(8,128)(2,1)} %convert_element_type.233), channel_id=1, source_target_pairs={{0,16},{2,18},{4,20},{6,22},{8,0},{10,2},{12,4},{14,6},{16,24},{18... | collective-permute-start | bytes 2162696 | tf_op jit(solution)/shard_map/ppermute | solution.py:297
  194.4 41.2 %copy-start.28 = (bf16[256,2048]{1,0:T(8,128)(2,1)S(1)}, bf16[256,2048]{1,0:T(8,128)(2,1)}, u32[]{:S(2)}) copy-start(bf16[256,2048]{1,0:T(8,128)(2,1)} %param.28) | copy-start | bytes 3145732
  235.6 206.8 %reduce-scatter.7.cloned.1.call-start = ((), (), s32[]{:S(2)}) async-start(), calls=%async_computation.14 | async-start | bytes 7208960 | tf_op jit(solution)/shard_map/reduce_scatter | solution.py:338
  240.1 24.9 %collective-permute-start.20 = (bf16[256,2048]{1,0:T(8,128)(2,1)S(1)}, bf16[256,2048]{1,0:T(8,128)(2,1)S(1)}, u32[]{:S(2)}, u32[]{:S(2)}) collective-permute-start(bf16[256,2048]{1,0:T(8,128)(2,1)S(1)} %multiply_convert_fusion.6), channel_id=1, source_target_pairs={{0,8},{2,10},{4,12},{6,14},{8,0},{10,2},{12,4},{14,6},{16,24},{18,... | collective-permute-start | bytes 3145736 | tf_op jit(solution)/shard_map/ppermute | solution.py:297
  241.9 23.1 %collective-permute-start.19 = (bf16[256,2048]{1,0:T(8,128)(2,1)S(1)}, bf16[256,2048]{1,0:T(8,128)(2,1)S(1)}, u32[]{:S(2)}, u32[]{:S(2)}) collective-permute-start(bf16[256,2048]{1,0:T(8,128)(2,1)S(1)} %multiply_convert_fusion.6), channel_id=1, source_target_pairs={{0,1},{1,0},{2,3},{3,2},{4,5},{5,4},{6,7},{7,6},{8,9},{9,8},{10,11... | collective-permute-start | bytes 3145736 | tf_op jit(solution)/shard_map/ppermute | solution.py:326
  265.0 2.7 collective-permute-start.21
  307.6 139.6 %reduce-scatter.5.cloned.1.call-start = ((), (), s32[]{:S(2)}) async-start(), calls=%async_computation.13 | async-start | bytes 7864320 | tf_op jit(solution)/shard_map/reduce_scatter | solution.py:338
  333.5 205.2 %reduce-scatter.9.cloned.1.call-start = ((), (), s32[]{:S(2)}) async-start(), calls=%async_computation.15 | async-start | bytes 6553600 | tf_op jit(solution)/shard_map/reduce_scatter | solution.py:338
  356.9 224.5 %reduce-scatter.11.cloned.1.call-start = ((), (), s32[]{:S(2)}) async-start(), calls=%async_computation.16 | async-start | bytes 2621440 | tf_op jit(solution)/shard_map/reduce_scatter | solution.py:338
  367.2 2.7 collective-permute-start.28
  368.6 27.0 %collective-permute-start.27 = (bf16[256,2048]{1,0:T(8,128)(2,1)S(1)}, bf16[256,2048]{1,0:T(8,128)(2,1)S(1)}, u32[]{:S(2)}, u32[]{:S(2)}) collective-permute-start(bf16[256,2048]{1,0:T(8,128)(2,1)S(1)} %get-tuple-element.178), channel_id=1, source_target_pairs={{0,1},{1,0},{2,3},{3,2},{4,5},{5,4},{6,7},{7,6},{8,9},{9,8},{10,11... | collective-permute-start | bytes 3145736 | tf_op jit(solution)/shard_map/ppermute | solution.py:326
  370.3 25.4 %collective-permute-start.29 = (bf16[256,2048]{1,0:T(8,128)(2,1)S(1)}, bf16[256,2048]{1,0:T(8,128)(2,1)S(1)}, u32[]{:S(2)}, u32[]{:S(2)}) collective-permute-start(bf16[256,2048]{1,0:T(8,128)(2,1)S(1)} %fusion.31), channel_id=1, source_target_pairs={{0,8},{2,10},{4,12},{6,14},{8,0},{10,2},{12,4},{14,6},{16,24},{18,... | collective-permute-start | bytes 3145736 | tf_op jit(solution)/shard_map/ppermute | solution.py:297
  400.8 24.7 %collective-permute-start.31 = (bf16[256,2048]{1,0:T(8,128)(2,1)S(1)}, bf16[256,2048]{1,0:T(8,128)(2,1)}, u32[]{:S(2)}, u32[]{:S(2)}) collective-permute-start(bf16[256,2048]{1,0:T(8,128)(2,1)S(1)} %get-tuple-element.166), channel_id=1, source_target_pairs={{0,8},{2,10},{4,12},{6,14},{8,0},{10,2},{12,4},{14,6},{16,24},{18,... | collective-permute-start | bytes 3145736 | tf_op jit(solution)/shard_map/ppermute | solution.py:297
  403.7 23.1 %collective-permute-start.26 = (bf16[256,2048]{1,0:T(8,128)(2,1)}, bf16[256,2048]{1,0:T(8,128)(2,1)}, u32[]{:S(2)}, u32[]{:S(2)}) collective-permute-start(bf16[256,2048]{1,0:T(8,128)(2,1)} %get-tuple-element.177), channel_id=1, source_target_pairs={{0,1},{1,0},{2,3},{3,2},{4,5},{5,4},{6,7},{7,6},{8,9},{9,8},{10,11... | collective-permute-start | bytes 3145736 | tf_op jit(solution)/shard_map/ppermute | solution.py:326
  403.7 26.2 %collective-permute-start.30 = (bf16[256,2048]{1,0:T(8,128)(2,1)S(1)}, bf16[256,2048]{1,0:T(8,128)(2,1)}, u32[]{:S(2)}, u32[]{:S(2)}) collective-permute-start(bf16[256,2048]{1,0:T(8,128)(2,1)S(1)} %get-tuple-element.166), channel_id=1, source_target_pairs={{0,1},{1,0},{2,3},{3,2},{4,5},{5,4},{6,7},{7,6},{8,9},{9,8},{10,11... | collective-permute-start | bytes 3145736 | tf_op jit(solution)/shard_map/ppermute | solution.py:326
  425.5 4.3 collective-permute-start.32
  426.2 93.4 %collective-permute-start.25 = (bf16[256,2048]{1,0:T(8,128)(2,1)}, bf16[256,2048]{1,0:T(8,128)(2,1)}, u32[]{:S(2)}, u32[]{:S(2)}) collective-permute-start(bf16[256,2048]{1,0:T(8,128)(2,1)} %get-tuple-element.176), channel_id=1, source_target_pairs={{0,1},{1,0},{2,3},{3,2},{4,5},{5,4},{6,7},{7,6},{8,9},{9,8},{10,11... | collective-permute-start | bytes 3145736 | tf_op jit(solution)/shard_map/ppermute | solution.py:326
  437.7 80.6 %collective-permute-start.33 = (bf16[256,2048]{1,0:T(8,128)(2,1)}, bf16[256,2048]{1,0:T(8,128)(2,1)}, u32[]{:S(2)}, u32[]{:S(2)}) collective-permute-start(bf16[256,2048]{1,0:T(8,128)(2,1)} %fusion.33), channel_id=1, source_target_pairs={{0,8},{2,10},{4,12},{6,14},{8,0},{10,2},{12,4},{14,6},{16,24},{18,... | collective-permute-start | bytes 3145736 | tf_op jit(solution)/shard_map/ppermute | solution.py:297
  444.8 33.5 %collective-permute-start.34 = (bf16[176,2048]{1,0:T(8,128)(2,1)}, bf16[176,2048]{1,0:T(8,128)(2,1)}, u32[]{:S(2)}, u32[]{:S(2)}) collective-permute-start(bf16[176,2048]{1,0:T(8,128)(2,1)} %get-tuple-element.191), channel_id=1, source_target_pairs={{0,8},{2,10},{4,12},{6,14},{8,24},{10,26},{12,28},{14,30},{16,0},{... | collective-permute-start | bytes 2162696 | tf_op jit(solution)/shard_map/ppermute | solution.py:297
  445.5 32.8 %collective-permute-start.35 = (bf16[176,2048]{1,0:T(8,128)(2,1)S(1)}, bf16[176,2048]{1,0:T(8,128)(2,1)}, u32[]{:S(2)}, u32[]{:S(2)}) collective-permute-start(bf16[176,2048]{1,0:T(8,128)(2,1)S(1)} %get-tuple-element.190), channel_id=1, source_target_pairs={{8,16},{10,18},{12,20},{14,22},{16,8},{18,10},{20,12},{22,14},{9,1... | collective-permute-start | bytes 2162696 | tf_op jit(solution)/shard_map/ppermute | solution.py:297
  457.1 55.8 %all-to-all-start.3 = ((bf16[4,128,1536]{2,1,0:T(8,128)(2,1)}), bf16[4,128,1536]{2,1,0:T(8,128)(2,1)S(1)}, u32[]{:S(2)}, u32[]{:S(2)}) async-start(bf16[4,128,1536]{2,1,0:T(8,128)(2,1)} %reduce-scatter.5.cloned.1.call-done), calls=%async_computation.5 | async-start | bytes 3145728 | tf_op jit(solution)/shard_map/all_to_all | solution.py:312
  538.7 8.1 %collective-permute-start.37 = (bf16[256,2048]{1,0:T(8,128)(2,1)S(1)}, bf16[256,2048]{1,0:T(8,128)(2,1)}, u32[]{:S(2)}, u32[]{:S(2)}) collective-permute-start(bf16[256,2048]{1,0:T(8,128)(2,1)S(1)} %get-tuple-element.175), channel_id=1, source_target_pairs={{0,1},{1,0},{2,3},{3,2},{4,5},{5,4},{6,7},{7,6},{8,9},{9,8},{10,11... | collective-permute-start | bytes 3145736 | tf_op jit(solution)/shard_map/ppermute | solution.py:326
  538.7 42.7 %all-to-all-start.4 = ((bf16[4,128,1280]{2,1,0:T(8,128)(2,1)}), bf16[4,128,1280]{2,1,0:T(8,128)(2,1)}, u32[]{:S(2)}, u32[]{:S(2)}) async-start(bf16[4,128,1280]{2,1,0:T(8,128)(2,1)} %reduce-scatter.9.cloned.1.call-done), calls=%async_computation.7 | async-start | bytes 2621440 | tf_op jit(solution)/shard_map/all_to_all | solution.py:312
  543.2 19.5 %collective-permute-start.41 = (bf16[4,128,640]{2,1,0:T(8,128)(2,1)}, bf16[4,128,640]{2,1,0:T(8,128)(2,1)S(1)}, u32[]{:S(2)}, u32[]{:S(2)}) collective-permute-start(bf16[4,128,640]{2,1,0:T(8,128)(2,1)} %get-tuple-element.182), channel_id=1, source_target_pairs={{0,6},{2,4},{4,2},{6,0},{8,14},{10,12},{12,10},{14,8},{16,22},{18,... | collective-permute-start | bytes 1966088 | tf_op jit(solution)/shard_map/ppermute | solution.py:320
  544.9 30.9 %collective-permute-start.40 = (bf16[4,128,640]{2,1,0:T(8,128)(2,1)}, bf16[4,128,640]{2,1,0:T(8,128)(2,1)S(1)}, u32[]{:S(2)}, u32[]{:S(2)}) collective-permute-start(bf16[4,128,640]{2,1,0:T(8,128)(2,1)} %get-tuple-element.183), channel_id=1, source_target_pairs={{0,4},{2,6},{4,0},{6,2},{8,12},{10,14},{12,8},{14,10},{16,20},{18,... | collective-permute-start | bytes 1966088 | tf_op jit(solution)/shard_map/ppermute | solution.py:320
  546.4 29.5 %collective-permute-start.39 = (bf16[4,128,640]{2,1,0:T(8,128)(2,1)}, bf16[4,128,640]{2,1,0:T(8,128)(2,1)S(1)}, u32[]{:S(2)}, u32[]{:S(2)}) collective-permute-start(bf16[4,128,640]{2,1,0:T(8,128)(2,1)} %get-tuple-element.184), channel_id=1, source_target_pairs={{0,2},{2,0},{4,6},{6,4},{8,10},{10,8},{12,14},{14,12},{16,18},{18,... | collective-permute-start | bytes 1966088 | tf_op jit(solution)/shard_map/ppermute | solution.py:320
  546.8 58.0 %collective-permute-start.36 = (bf16[256,2048]{1,0:T(8,128)(2,1)}, bf16[256,2048]{1,0:T(8,128)(2,1)}, u32[]{:S(2)}, u32[]{:S(2)}) collective-permute-start(bf16[256,2048]{1,0:T(8,128)(2,1)} %get-tuple-element.174), channel_id=1, source_target_pairs={{0,1},{1,0},{2,3},{3,2},{4,5},{5,4},{6,7},{7,6},{8,9},{9,8},{10,11... | collective-permute-start | bytes 3145736 | tf_op jit(solution)/shard_map/ppermute | solution.py:326
  550.0 54.8 %collective-permute-start.38 = (bf16[256,2048]{1,0:T(8,128)(2,1)}, bf16[256,2048]{1,0:T(8,128)(2,1)}, u32[]{:S(2)}, u32[]{:S(2)}) collective-permute-start(bf16[256,2048]{1,0:T(8,128)(2,1)} %fusion.29), channel_id=1, source_target_pairs={{0,8},{2,10},{4,12},{6,14},{8,0},{10,2},{12,4},{14,6},{16,24},{18,... | collective-permute-start | bytes 3145736 | tf_op jit(solution)/shard_map/ppermute | solution.py:297
  577.0 21.1 %collective-permute-start.44 = (bf16[128,640]{1,0:T(8,128)(2,1)}, bf16[128,640]{1,0:T(8,128)(2,1)S(1)}, u32[]{:S(2)}, u32[]{:S(2)}) collective-permute-start(bf16[128,640]{1,0:T(8,128)(2,1)} %get-tuple-element.192), channel_id=1, source_target_pairs={{0,24},{2,26},{4,28},{6,30},{8,16},{10,18},{12,20},{14,22},{16,8},... | collective-permute-start | bytes 491528 | tf_op jit(solution)/shard_map/ppermute | solution.py:297
  580.4 20.1 %collective-permute-start.43 = (bf16[128,640]{1,0:T(8,128)(2,1)}, bf16[128,640]{1,0:T(8,128)(2,1)S(1)}, u32[]{:S(2)}, u32[]{:S(2)}) collective-permute-start(bf16[128,640]{1,0:T(8,128)(2,1)} %get-tuple-element.193), channel_id=1, source_target_pairs={{0,8},{2,10},{4,12},{6,14},{8,0},{10,2},{12,4},{14,6},{16,24},{18,... | collective-permute-start | bytes 491528 | tf_op jit(solution)/shard_map/ppermute | solution.py:297
  580.4 21.4 %collective-permute-start.42 = (bf16[128,640]{1,0:T(8,128)(2,1)}, bf16[128,640]{1,0:T(8,128)(2,1)S(1)}, u32[]{:S(2)}, u32[]{:S(2)}) collective-permute-start(bf16[128,640]{1,0:T(8,128)(2,1)} %get-tuple-element.194), channel_id=1, source_target_pairs={{0,16},{2,18},{4,20},{6,22},{8,24},{10,26},{12,28},{14,30},{16,0},... | collective-permute-start | bytes 491528 | tf_op jit(solution)/shard_map/ppermute | solution.py:297
  598.1 24.8 %collective-permute-start.45 = (bf16[64,2048]{1,0:T(8,128)(2,1)}, bf16[64,2048]{1,0:T(8,128)(2,1)S(1)}, u32[]{:S(2)}, u32[]{:S(2)}) collective-permute-start(bf16[64,2048]{1,0:T(8,128)(2,1)} %get-tuple-element.200), channel_id=1, source_target_pairs={{0,8},{2,10},{4,12},{6,14},{8,24},{10,26},{12,28},{14,30},{16,0},{... | collective-permute-start | bytes 786440 | tf_op jit(solution)/shard_map/ppermute | solution.py:297
  600.5 22.4 %collective-permute-start.46 = (bf16[64,2048]{1,0:T(8,128)(2,1)}, bf16[64,2048]{1,0:T(8,128)(2,1)}, u32[]{:S(2)}, u32[]{:S(2)}) collective-permute-start(bf16[64,2048]{1,0:T(8,128)(2,1)} %get-tuple-element.201), channel_id=1, source_target_pairs={{8,16},{10,18},{12,20},{14,22},{16,8},{18,10},{20,12},{22,14},{9,1... | collective-permute-start | bytes 786440 | tf_op jit(solution)/shard_map/ppermute | solution.py:297
  609.0 12.0 %all-to-all-start.5 = ((f32[32,1,128]{2,1,0:T(1,128)}), f32[32,1,128]{2,1,0:T(1,128)S(1)}, u32[]{:S(2)}, u32[]{:S(2)}) async-start(f32[32,1,128]{2,1,0:T(1,128)} %reshape.724), calls=%async_computation.9 | async-start | bytes 32768 | tf_op jit(solution)/shard_map/all_to_all | solution.py:707
  (107 other events, 781.9 us)
Sparse Core Ops, SparseCore 0:
  50.3 87.2 all-gather.3
  152.9 71.5 all-gather.5
  235.7 65.0 all-gather.7
  307.7 64.8 reduce-scatter.6
  375.5 70.1 reduce-scatter.4
  448.5 61.4 reduce-scatter.8
  513.6 35.1 reduce-scatter.10

commit v4 on v3

--- a/solution.py
+++ b/solution.py
@@ -614,7 +614,7 @@
     value_grads = []
     for group_index in range(2):
         if group_index == 1:
-            mixed_grad = after(mixed_grad, query_grads[0], *contract_sent)
+            mixed_grad = after(mixed_grad, query_grads[0])
         for kv_index in range(kv_count):
             query_block, key_block, masked = head_scores(group_index, kv_index)
             soft_exact = jnp.exp(masked - log_totals[group_index, kv_index])
@@ -627,8 +627,6 @@
             )
             inner_sum = jnp.sum(prob_grad * soft_exact, axis=-1, keepdims=True)
             score_grad = (soft_exact * (prob_grad - inner_sum)).astype(bf_type)
-            if group_index == 1:
-                score_grad = after(score_grad, last_parts)
             query_grads.append(
                 jnp.einsum("rgk,ke->gre", score_grad, key_block, preferred_element_type=fl_type)
                 * factor
@@ -681,14 +679,14 @@
         WEIGHT_DECAY,
         EMA_KEEP,
     )
-    qkv_back = after(qkv_back, layer_output, last_parts)
+    qkv_back = after(qkv_back, layer_output, *contract_sent)
     qkv_full = lax.dot_general(
         normed_all, qkv_back, CONTRACT_FIRST, preferred_element_type=fl_type
     ).astype(bf_type)
     qkv_blocks = low_blocks(qkv_full, 4)
     qkv_moved = sent_low(qkv_blocks)
     normed_partial = lax.dot_general(
-        after(qkv_back, *qkv_blocks), qkv_low, CONTRACT_LAST, preferred_element_type=fl_type
+        after(qkv_back, last_parts, *qkv_blocks), qkv_low, CONTRACT_LAST, preferred_element_type=fl_type
     )
     first_parts = spread(after(first_reduced, normed_partial))
     normed_kept, normed_sent = token_sums(normed_partial)

time: 641 us -> 636 us (level)
  matrix products: 155 us -> 135 us
  waiting for transfers between devices: 234 us -> 246 us
    sub x1 -> x0, matrix products: 11.8 us -> none  [per_device(): score_grad = (soft_exact * (prob_grad - inner_sum)).astype(bf_type)]
    all_to_all x4, waiting for transfers between devices: 39.8 us -> 49.3 us  [spread(): lax.all_to_all(blocks, 'dp', split_axis=0, concat_axis=0, tiled=True, axi...]
    unnamed x228 -> x220, local copies, waits for them, and re-layouts: 30.1 us -> 29.3 us
  transfers between devices with their start and end apart: 60 -> 60, of which waited for: 18 -> 19; matrix products, arithmetic and copies ran while one was open for 40% -> 38% of each run, Pallas kernels for 3% -> 3%
where the time goes in v4:
time: 636 us; the launch traced here: 628 us
  waiting for transfers between devices  246 us (39%)
  matrix products  135 us (21%)
  other arithmetic  90.4 us (14%)
  starting transfers between devices  78.7 us (12%)
  local copies, waits for them, and re-layouts  40.1 us (6%)
  Pallas kernels  21.5 us (3%)
  between operations  16.3 us (3%)
    ppermute x22, waiting for transfers between devices, move(): lax.ppermute(value, 'dp', [(place * low_count + low, goal * low_count + l...  114 us
    ppermute x9, waiting for transfers between devices, swap_low(): lax.ppermute(value, 'dp', [(index, index ^ flip) for index in range(dp_co...  62.6 us
    all_to_all x4, waiting for transfers between devices, spread(): lax.all_to_all(blocks, 'dp', split_axis=0, concat_axis=0, tiled=True, axi...  49.3 us
    ppermute x22, starting transfers between devices, move(): lax.ppermute(value, 'dp', [(place * low_count + low, goal * low_count + l...  38 us
    unnamed x220, local copies, waits for them, and re-layouts  29.3 us
    dot_general x2, matrix products, gated(): gate_up = jnp.dot(rows, weights, preferred_element_type=fl_type)  20.4 us
    all_to_all x4, starting transfers between devices, spread(): lax.all_to_all(blocks, 'dp', split_axis=0, concat_axis=0, tiled=True, axi...  16.9 us
    all_to_all x1, waiting for transfers between devices, per_device(): lax.all_to_all(jnp.broadcast_to(own_facts[None], (2 * dp_count, own_facts...  14.4 us
  transfers between devices with their start and end apart: 60, of which 19 were waited for; matrix products, arithmetic and copies ran while one was open for 38% of the time, Pallas kernels for 3%

profile of v4, /device:TPU:0, one launch (start us, length us, event | category | flops | bytes accessed | tf_op | source)
XLA Modules:
  0.0 628.0 jit_solution(4241965020944794259)
XLA Ops:
  9.1 3.4 shard_map.468
  13.6 5.0 collective-permute-start.24
  22.5 4.3 all-to-all-start
  26.8 2.7 collective-permute-start.23
  29.8 14.4 %all-to-all-done = f32[32,1,646]{2,1,0:T(1,128)S(1)} async-done(((f32[32,1,646]{2,1,0:T(1,128)}), f32[32,1,646]{2,1,0:T(1,128)S(1)}, u32[]{:S(2)}, u32[]{:S(2)}) %all-to-all-start) | async-done | bytes 82720 | tf_op jit(solution)/shard_map/all_to_all | solution.py:417
  52.1 4.9 collective-permute-start.1
  57.2 3.5 all-to-all-start.1
  61.1 29.5 %all-to-all-done.1.refs_0_ = bf16[4,128,640]{2,1,0:T(8,128)(2,1)S(1)} async-done(((bf16[4,128,640]{2,1,0:T(8,128)(2,1)}), bf16[4,128,640]{2,1,0:T(8,128)(2,1)S(1)}, u32[]{:S(2)}, u32[]{:S(2)}) %all-to-all-start.1) | async-done | bytes 655392 | tf_op jit(solution)/shard_map/all_to_all | solution.py:312
  90.7 4.3 all-to-all-start.2
  95.3 2.4 collective-permute-start.5
  101.6 25.1 %collective-permute-done.5.refs_3_ = bf16[4,128,640]{2,1,0:T(8,128)(2,1)S(1)} collective-permute-done((bf16[4,128,640]{2,1,0:T(8,128)(2,1)S(1)}, bf16[4,128,640]{2,1,0:T(8,128)(2,1)S(1)}, u32[]{:S(2)}, u32[]{:S(2)}) %collective-permute-start.5) | collective-permute-done | bytes 655392 | tf_op jit(solution)/shard_map/ppermute | solution.py:320
  126.7 13.0 %collective-permute-done.4.refs_2_ = bf16[4,128,640]{2,1,0:T(8,128)(2,1)S(1)} collective-permute-done((bf16[4,128,640]{2,1,0:T(8,128)(2,1)S(1)}, bf16[4,128,640]{2,1,0:T(8,128)(2,1)S(1)}, u32[]{:S(2)}, u32[]{:S(2)}) %collective-permute-start.4) | collective-permute-done | bytes 655392 | tf_op jit(solution)/shard_map/ppermute | solution.py:320
  147.2 4.1 fusion.123
  162.5 2.5 fusion.44
  165.0 5.2 collective-permute-done.9
  170.2 2.4 fusion.43
  192.3 3.4 collective-permute-start.16
  198.1 36.9 %collective-permute-done.18 = bf16[176,2048]{1,0:T(8,128)(2,1)} collective-permute-done((bf16[176,2048]{1,0:T(8,128)(2,1)}, bf16[176,2048]{1,0:T(8,128)(2,1)}, u32[]{:S(2)}, u32[]{:S(2)}) %collective-permute-start.18) | collective-permute-done | bytes 720928 | tf_op jit(solution)/shard_map/ppermute | solution.py:297
  235.0 2.7 maximum_select_fusion
  237.8 2.9 multiply_reduce_fusion.2
  244.0 23.1 %collective-permute-done.20 = bf16[256,2048]{1,0:T(8,128)(2,1)S(1)} collective-permute-done((bf16[256,2048]{1,0:T(8,128)(2,1)S(1)}, bf16[256,2048]{1,0:T(8,128)(2,1)S(1)}, u32[]{:S(2)}, u32[]{:S(2)}) %collective-permute-start.20) | collective-permute-done | bytes 1048608 | tf_op jit(solution)/shard_map/ppermute | solution.py:297
  267.1 2.6 collective-permute-done.21
  270.7 2.7 pad_maximum_fusion.1
  273.4 10.3 %fusion.110 = f32[1024,1280]{1,0:T(8,128)S(1)} fusion(bf16[2048,1280]{1,0:T(8,128)(2,1)} %bitcast.234, bf16[256,2048]{1,0:T(8,128)(2,1)} %copy-done.69, bf16[256,2048]{1,0:T(8,128)(2,1)} %copy-done.65, bf16[256,2048]{1,0:T(8,128)(2,1)} %copy-done.67, bf16[256,2048]{1,0:T(8,128)(2,1)S(1)} %multiply_convert_fusion.6), kind=kOutput, calls=%fused_computation.252 | convolution fusion | flops 5385486336 | bytes 14680064 | tf_op jit(solution)/shard_map/dot_general | solution.py:533
  286.7 10.1 %fusion.129 = f32[1024,1536]{1,0:T(8,128)S(1)} fusion(bf16[1024,2048]{1,0:T(8,128)(2,1)} %pad_maximum_fusion.1, bf16[2048,1536]{1,0:T(8,128)(2,1)} %bitcast.226), kind=kOutput, calls=%fused_computation.269 | convolution fusion | flops 6442450944 | bytes 16777216 | tf_op jit(solution)/shard_map/dot_general | solution.py:533
  296.8 2.6 copy-done.27
  301.7 8.0 %convolution_convert_fusion.2 = bf16[1408,2048]{1,0:T(8,128)(2,1)} fusion(bf16[1024,2048]{1,0:T(8,128)(2,1)S(1)} %copy-done.76, bf16[1024,768]{1,0:T(8,128)(2,1)S(1)} %multiply_convert_fusion.2, bf16[1024,640]{1,0:T(8,128)(2,1)S(1)} %multiply_convert_fusion.5), kind=kOutput, calls=%fused_computation.20 | convolution fusion | flops 5914230784 | bytes 12845056 | tf_op jit(solution)/shard_map/dot_general | solution.py:561
  309.8 10.7 %fusion.130 = f32[1024,1408]{1,0:T(8,128)S(1)} fusion(bf16[1024,2048]{1,0:T(8,128)(2,1)} %copy-done.75, bf16[1408,2048]{1,0:T(8,128)(2,1)} %bitcast.230), kind=kOutput, calls=%fused_computation.270 | convolution fusion | flops 5905580032 | bytes 15728640 | tf_op jit(solution)/shard_map/dot_general | solution.py:565
  320.5 5.8 multiply_convert_fusion.1
  326.7 8.8 %convolution_convert_fusion.1 = bf16[2048,1536]{1,0:T(8,128)(2,1)} fusion(bf16[1024,768]{1,0:T(8,128)(2,1)S(1)} %get-tuple-element.169, bf16[1024,768]{1,0:T(8,128)(2,1)S(1)} %get-tuple-element.168, bf16[256,2048]{1,0:T(8,128)(2,1)S(1)} %copy-done.70, bf16[256,2048]{1,0:T(8,128)(2,1)S(1)} %copy-done.66, bf16[256,2048]{1,0:T(8,128)(2,1)S(1)} %copy-done.68, ...), kind=kOutput, calls=%fused_computation.19 | convolution fusion | flops 6468665344 | bytes 13631488 | tf_op jit(solution)/shard_map/dot_general | solution.py:578
  337.7 4.8 multiply_convert_fusion.4
  342.5 7.5 %convolution_convert_fusion = bf16[2048,1280]{1,0:T(8,128)(2,1)} fusion(bf16[1024,2048]{1,0:T(8,128)(2,1)S(1)} %copy-done.46, bf16[1024,640]{1,0:T(8,128)(2,1)S(1)} %get-tuple-element.171, bf16[1024,640]{1,0:T(8,128)(2,1)S(1)} %get-tuple-element.170), kind=kOutput, calls=%fused_computation.18 | convolution fusion | flops 5376573440 | bytes 12058624 | tf_op jit(solution)/shard_map/dot_general | solution.py:581
  350.1 9.0 %fusion.131 = f32[1024,2048]{1,0:T(8,128)} fusion(bf16[1024,1536]{1,0:T(8,128)(2,1)S(1)} %pad_maximum_fusion.3, bf16[2048,1536]{1,0:T(8,128)(2,1)S(1)} %bitcast.229), kind=kOutput, calls=%fused_computation.271 | convolution fusion | flops 6442450944 | bytes 17825792 | tf_op jit(solution)/shard_map/dot_general | solution.py:588
  359.2 9.8 %fusion.127 = (bf16[1024,2048]{1,0:T(8,128)(2,1)S(1)}, f32[1024,2048]{1,0:T(8,128)S(1)}) fusion(f32[1024,2048]{1,0:T(8,128)} %fusion.131, bf16[2048,1280]{1,0:T(8,128)(2,1)} %bitcast.235, bf16[1024,640]{1,0:T(8,128)(2,1)} %copy-done.58, bf16[1024,640]{1,0:T(8,128)(2,1)} %copy-done.57), kind=kOutput, calls=%fused_computation.265 | convolution fusion | flops 5378146304 | bytes 28835840 | tf_op jit(solution)/shard_map/dot_general | solution.py:590
  373.7 8.9 %fusion.126 = (bf16[1024,2048]{1,0:T(8,128)(2,1)S(1)}, f32[1024,2048]{1,0:T(8,128)}) fusion(bf16[1024,1408]{1,0:T(8,128)(2,1)S(1)} %pad_maximum_fusion.4, bf16[1408,2048]{1,0:T(8,128)(2,1)S(1)} %bitcast.233), kind=kOutput, calls=%fused_computation.264 | convolution fusion | flops 5907677184 | bytes 21233664 | tf_op jit(solution)/shard_map/dot_general | solution.py:591
  382.7 14.9 %collective-permute-done.29 = bf16[256,2048]{1,0:T(8,128)(2,1)S(1)} collective-permute-done((bf16[256,2048]{1,0:T(8,128)(2,1)S(1)}, bf16[256,2048]{1,0:T(8,128)(2,1)S(1)}, u32[]{:S(2)}, u32[]{:S(2)}) %collective-permute-start.29) | collective-permute-done | bytes 1048608 | tf_op jit(solution)/shard_map/ppermute | solution.py:297
  398.5 3.7 fusion.114
  405.5 21.3 %collective-permute-done.31 = bf16[256,2048]{1,0:T(8,128)(2,1)} collective-permute-done((bf16[256,2048]{1,0:T(8,128)(2,1)S(1)}, bf16[256,2048]{1,0:T(8,128)(2,1)}, u32[]{:S(2)}, u32[]{:S(2)}) %collective-permute-start.31) | collective-permute-done | bytes 1048608 | tf_op jit(solution)/shard_map/ppermute | solution.py:297
  427.5 3.2 fusion.32
  432.9 5.5 convolution_convert_fusion.4
  447.8 5.4 fusion.3
  453.2 4.6 fusion.5
  458.7 2.5 fusion
  461.3 2.6 fusion.2
  469.6 9.8 %collective-permute-done.33 = bf16[256,2048]{1,0:T(8,128)(2,1)} collective-permute-done((bf16[256,2048]{1,0:T(8,128)(2,1)}, bf16[256,2048]{1,0:T(8,128)(2,1)}, u32[]{:S(2)}, u32[]{:S(2)}) %collective-permute-start.33) | collective-permute-done | bytes 1048608 | tf_op jit(solution)/shard_map/ppermute | solution.py:297
  479.4 4.6 all-to-all-start.3
  484.6 4.9 fusion.56
  491.6 4.0 fusion.35
  495.6 3.8 convolution_convert_fusion.3
  500.9 19.8 %all-to-all-done.3.refs_1_ = bf16[4,128,1536]{2,1,0:T(8,128)(2,1)} async-done(((bf16[4,128,1536]{2,1,0:T(8,128)(2,1)}), bf16[4,128,1536]{2,1,0:T(8,128)(2,1)}, u32[]{:S(2)}, u32[]{:S(2)}) %all-to-all-start.3) | async-done | bytes 1572896 | tf_op jit(solution)/shard_map/all_to_all | solution.py:312
  520.7 7.1 %fusion.128 = (bf16[1024,2048]{1,0:T(8,128)(2,1)S(1)}, f32[1024,2048]{1,0:T(8,128)}) fusion(bf16[1024,640]{0,1:T(8,128)(2,1)} %copy-done.41, bf16[2048,640]{1,0:T(8,128)(2,1)S(1)} %bitcast.193), kind=kOutput, calls=%fused_computation.266 | convolution fusion | flops 2686451712 | bytes 16515072 | tf_op jit(solution)/shard_map/dot_general | solution.py:688
  528.9 4.5 all-to-all-start.4
  533.5 2.4 collective-permute-start.41
  537.1 3.1 fusion.28
  542.1 5.3 multiply_add_fusion.1
  547.4 10.5 %collective-permute-done.41 = bf16[4,128,640]{2,1,0:T(8,128)(2,1)S(1)} collective-permute-done((bf16[4,128,640]{2,1,0:T(8,128)(2,1)}, bf16[4,128,640]{2,1,0:T(8,128)(2,1)S(1)}, u32[]{:S(2)}, u32[]{:S(2)}) %collective-permute-start.41) | collective-permute-done | bytes 655392 | tf_op jit(solution)/shard_map/ppermute | solution.py:320
  557.9 13.6 %collective-permute-done.40 = bf16[4,128,640]{2,1,0:T(8,128)(2,1)S(1)} collective-permute-done((bf16[4,128,640]{2,1,0:T(8,128)(2,1)}, bf16[4,128,640]{2,1,0:T(8,128)(2,1)S(1)}, u32[]{:S(2)}, u32[]{:S(2)}) %collective-permute-start.40) | collective-permute-done | bytes 655392 | tf_op jit(solution)/shard_map/ppermute | solution.py:320
  573.0 3.4 collective-permute-start.44
  579.4 13.8 %shard_map.471 = (f32[128,2,2816]{2,1,0:T(2,128)}, f32[128,2,2816]{2,1,0:T(2,128)}, f32[128,2,2816]{2,1,0:T(2,128)}, f32[128,2,2816]{2,1,0:T(2,128)}) custom-call(bf16[4,128,1280]{2,1,0:T(8,128)(2,1)} %all-to-all-done.4.refs_0_, bf16[4,128,1536]{2,1,0:T(8,128)(2,1)} %all-to-all-done.3.refs_1_, f32[128,2,2816]{2,1,0:T(2,128)S(1)} %copy-done.1, ...), custom_call_target="tpu_custom_call" | custom-call | tf_op jit(solution)/shard_map/pallas_call | solution.py:242
  595.9 2.9 shard_map.472
  598.8 3.3 fusion.23
  603.0 6.2 all-to-all-start.5
  609.3 5.2 fusion.25
  618.3 2.7 multiply_add_fusion.3
  (420 shorter events, 120.1 us)
Async XLA Ops:
  13.6 32.7 %collective-permute-start.24 = (bf16[128,1280]{1,0:T(8,128)(2,1)S(1)}, bf16[128,1280]{1,0:T(8,128)(2,1)S(1)}, u32[]{:S(2)}, u32[]{:S(2)}) collective-permute-start(bf16[128,1280]{1,0:T(8,128)(2,1)S(1)} %get-tuple-element.100), channel_id=1, source_target_pairs={{0,24},{2,26},{4,28},{6,30},{8,16},{10,18},{12,20},{14,22},{16,8},... | collective-permute-start | bytes 983048 | tf_op jit(solution)/shard_map/ppermute | solution.py:297
  18.7 27.7 %collective-permute-start.22 = (bf16[128,1280]{1,0:T(8,128)(2,1)S(1)}, bf16[128,1280]{1,0:T(8,128)(2,1)S(1)}, u32[]{:S(2)}, u32[]{:S(2)}) collective-permute-start(bf16[128,1280]{1,0:T(8,128)(2,1)S(1)} %get-tuple-element.100), channel_id=1, source_target_pairs={{0,8},{2,10},{4,12},{6,14},{8,0},{10,2},{12,4},{14,6},{16,24},{18,... | collective-permute-start | bytes 983048 | tf_op jit(solution)/shard_map/ppermute | solution.py:297
  22.5 21.7 %all-to-all-start = ((f32[32,1,646]{2,1,0:T(1,128)}), f32[32,1,646]{2,1,0:T(1,128)S(1)}, u32[]{:S(2)}, u32[]{:S(2)}) async-start(f32[32,1,646]{2,1,0:T(1,128)} %broadcast_in_dim.52), calls=%async_computation | async-start | bytes 196608 | tf_op jit(solution)/shard_map/all_to_all | solution.py:417
  26.7 246.6 %all-gather.4.cloned.1.call-start = ((), (), s32[]{:S(2)}) async-start(), calls=%async_computation.10 | async-start | bytes 6553600 | tf_op jit(solution)/shard_map/all_gather | solution.py:335
  26.8 21.9 %collective-permute-start.23 = (bf16[128,1280]{1,0:T(8,128)(2,1)S(1)}, bf16[128,1280]{1,0:T(8,128)(2,1)S(1)}, u32[]{:S(2)}, u32[]{:S(2)}) collective-permute-start(bf16[128,1280]{1,0:T(8,128)(2,1)S(1)} %get-tuple-element.101), channel_id=1, source_target_pairs={{0,16},{2,18},{4,20},{6,22},{8,24},{10,26},{12,28},{14,30},{16,0},... | collective-permute-start | bytes 983048 | tf_op jit(solution)/shard_map/ppermute | solution.py:297
  50.3 10.8 %collective-permute-start.7 = (bf16[64,2048]{1,0:T(8,128)(2,1)S(1)}, bf16[64,2048]{1,0:T(8,128)(2,1)S(1)}, u32[]{:S(2)}, u32[]{:S(2)}) collective-permute-start(bf16[64,2048]{1,0:T(8,128)(2,1)S(1)} %convert_element_type.222), channel_id=1, source_target_pairs={{0,16},{2,18},{4,20},{6,22},{8,0},{10,2},{12,4},{14,6},{16,24},{18... | collective-permute-start | bytes 786440 | tf_op jit(solution)/shard_map/ppermute | solution.py:297
  50.3 10.7 %collective-permute-start.6 = (bf16[64,2048]{1,0:T(8,128)(2,1)S(1)}, bf16[64,2048]{1,0:T(8,128)(2,1)S(1)}, u32[]{:S(2)}, u32[]{:S(2)}) collective-permute-start(bf16[64,2048]{1,0:T(8,128)(2,1)S(1)} %convert_element_type.222), channel_id=1, source_target_pairs={{8,16},{10,18},{12,20},{14,22},{16,8},{18,10},{20,12},{22,14},{9,1... | collective-permute-start | bytes 786440 | tf_op jit(solution)/shard_map/ppermute | solution.py:297
  52.1 46.8 %copy-start.92 = (f32[32]{0:T(128)}, f32[32]{0:T(128)S(1)}, u32[]{:S(2)}) copy-start(f32[32]{0:T(128)S(1)} %multiply_power_fusion) | copy-start | bytes 388
  52.1 43.0 %collective-permute-start.1 = (bf16[256,2048]{1,0:T(8,128)(2,1)}, bf16[256,2048]{1,0:T(8,128)(2,1)}, u32[]{:S(2)}, u32[]{:S(2)}) collective-permute-start(bf16[256,2048]{1,0:T(8,128)(2,1)} %fusion.22), channel_id=1, source_target_pairs={{0,8},{2,10},{4,12},{6,14},{8,0},{10,2},{12,4},{14,6},{16,24},{18,... | collective-permute-start | bytes 3145736 | tf_op jit(solution)/shard_map/ppermute | solution.py:297
  57.0 86.5 %collective-permute-start = (bf16[256,2048]{1,0:T(8,128)(2,1)}, bf16[256,2048]{1,0:T(8,128)(2,1)}, u32[]{:S(2)}, u32[]{:S(2)}) collective-permute-start(bf16[256,2048]{1,0:T(8,128)(2,1)} %fusion.22), channel_id=1, source_target_pairs={{0,1},{1,0},{2,3},{3,2},{4,5},{5,4},{6,7},{7,6},{8,9},{9,8},{10,11... | collective-permute-start | bytes 3145736 | tf_op jit(solution)/shard_map/ppermute | solution.py:326
  57.2 33.5 %all-to-all-start.1 = ((bf16[4,128,640]{2,1,0:T(8,128)(2,1)}), bf16[4,128,640]{2,1,0:T(8,128)(2,1)S(1)}, u32[]{:S(2)}, u32[]{:S(2)}) async-start(bf16[4,128,640]{2,1,0:T(8,128)(2,1)} %shard_map.467), calls=%async_computation.1 | async-start | bytes 1310720 | tf_op jit(solution)/shard_map/all_to_all | solution.py:312
  90.7 62.1 %all-to-all-start.2 = ((bf16[4,128,1536]{2,1,0:T(8,128)(2,1)}), bf16[4,128,1536]{2,1,0:T(8,128)(2,1)}, u32[]{:S(2)}, u32[]{:S(2)}) async-start(bf16[4,128,1536]{2,1,0:T(8,128)(2,1)} %copy-done.6), calls=%async_computation.2 | async-start | bytes 3145728 | tf_op jit(solution)/shard_map/all_to_all | solution.py:312
  95.0 191.7 %all-gather.6.cloned.1.call-start = ((), (), s32[]{:S(2)}) async-start(), calls=%async_computation.11 | async-start | bytes 7864320 | tf_op jit(solution)/shard_map/all_gather | solution.py:335
  95.1 48.4 %collective-permute-start.2 = (bf16[256,2048]{1,0:T(8,128)(2,1)}, bf16[256,2048]{1,0:T(8,128)(2,1)S(1)}, u32[]{:S(2)}, u32[]{:S(2)}) collective-permute-start(bf16[256,2048]{1,0:T(8,128)(2,1)} %collective-permute-done.1), channel_id=1, source_target_pairs={{0,1},{1,0},{2,3},{3,2},{4,5},{5,4},{6,7},{7,6},{8,9},{9,8},{10,11... | collective-permute-start | bytes 3145736 | tf_op jit(solution)/shard_map/ppermute | solution.py:326
  95.2 57.9 %copy-start.82 = (f32[1024]{0:T(1024)}, f32[1024]{0:T(1024)S(1)}, u32[]{:S(2)}) copy-start(f32[1024]{0:T(1024)S(1)} %add_convert_fusion.3) | copy-start | bytes 12292
  95.3 31.4 %collective-permute-start.5 = (bf16[4,128,640]{2,1,0:T(8,128)(2,1)S(1)}, bf16[4,128,640]{2,1,0:T(8,128)(2,1)S(1)}, u32[]{:S(2)}, u32[]{:S(2)}) collective-permute-start(bf16[4,128,640]{2,1,0:T(8,128)(2,1)S(1)} %all-to-all-done.1.refs_0_), channel_id=1, source_target_pairs={{0,6},{2,4},{4,2},{6,0},{8,14},{10,12},{12,10},{14,8},{16,22},{18,... | collective-permute-start | bytes 1966088 | tf_op jit(solution)/shard_map/ppermute | solution.py:320
  97.8 41.9 %collective-permute-start.4 = (bf16[4,128,640]{2,1,0:T(8,128)(2,1)S(1)}, bf16[4,128,640]{2,1,0:T(8,128)(2,1)S(1)}, u32[]{:S(2)}, u32[]{:S(2)}) collective-permute-start(bf16[4,128,640]{2,1,0:T(8,128)(2,1)S(1)} %all-to-all-done.1.refs_0_), channel_id=1, source_target_pairs={{0,4},{2,6},{4,0},{6,2},{8,12},{10,14},{12,8},{14,10},{16,20},{18,... | collective-permute-start | bytes 1966088 | tf_op jit(solution)/shard_map/ppermute | solution.py:320
  98.3 41.4 %collective-permute-start.3 = (bf16[4,128,640]{2,1,0:T(8,128)(2,1)S(1)}, bf16[4,128,640]{2,1,0:T(8,128)(2,1)S(1)}, u32[]{:S(2)}, u32[]{:S(2)}) collective-permute-start(bf16[4,128,640]{2,1,0:T(8,128)(2,1)S(1)} %all-to-all-done.1.refs_0_), channel_id=1, source_target_pairs={{0,2},{2,0},{4,6},{6,4},{8,10},{10,8},{12,14},{14,12},{16,18},{18,... | collective-permute-start | bytes 1966088 | tf_op jit(solution)/shard_map/ppermute | solution.py:320
  100.1 55.3 %copy-start.59 = (f32[1024,32]{0,1:T(8,128)}, f32[1024,32]{0,1:T(8,128)S(1)}, u32[]{:S(2)}) copy-start(f32[1024,32]{0,1:T(8,128)S(1)} %get-tuple-element.206) | copy-start | bytes 393220
  140.0 34.5 %collective-permute-start.13 = (bf16[2,64,2048]{2,1,0:T(8,128)(2,1)S(1)}, bf16[2,64,2048]{2,1,0:T(8,128)(2,1)S(1)}, u32[]{:S(2)}, u32[]{:S(2)}) collective-permute-start(bf16[2,64,2048]{2,1,0:T(8,128)(2,1)S(1)} %maximum_select_fusion.2.refs_0_), channel_id=1, source_target_pairs={{0,6},{2,4},{4,2},{6,0},{8,14},{10,12},{12,10},{14,8},{16,22},{18,... | collective-permute-start | bytes 1572872 | tf_op jit(solution)/shard_map/ppermute | solution.py:320
  141.5 33.0 %collective-permute-start.12 = (bf16[2,64,2048]{2,1,0:T(8,128)(2,1)S(1)}, bf16[2,64,2048]{2,1,0:T(8,128)(2,1)S(1)}, u32[]{:S(2)}, u32[]{:S(2)}) collective-permute-start(bf16[2,64,2048]{2,1,0:T(8,128)(2,1)S(1)} %maximum_select_fusion.2.refs_0_), channel_id=1, source_target_pairs={{0,4},{2,6},{4,0},{6,2},{8,12},{10,14},{12,8},{14,10},{16,20},{18,... | collective-permute-start | bytes 1572872 | tf_op jit(solution)/shard_map/ppermute | solution.py:320
  143.0 32.4 %collective-permute-start.11 = (bf16[2,64,2048]{2,1,0:T(8,128)(2,1)S(1)}, bf16[2,64,2048]{2,1,0:T(8,128)(2,1)S(1)}, u32[]{:S(2)}, u32[]{:S(2)}) collective-permute-start(bf16[2,64,2048]{2,1,0:T(8,128)(2,1)S(1)} %maximum_select_fusion.2.refs_0_), channel_id=1, source_target_pairs={{0,2},{2,0},{4,6},{6,4},{8,10},{10,8},{12,14},{14,12},{16,18},{18,... | collective-permute-start | bytes 1572872 | tf_op jit(solution)/shard_map/ppermute | solution.py:320
  145.7 24.6 %collective-permute-start.9 = (bf16[256,2048]{1,0:T(8,128)(2,1)}, bf16[256,2048]{1,0:T(8,128)(2,1)}, u32[]{:S(2)}, u32[]{:S(2)}) collective-permute-start(bf16[256,2048]{1,0:T(8,128)(2,1)} %param.29), channel_id=1, source_target_pairs={{0,8},{2,10},{4,12},{6,14},{8,0},{10,2},{12,4},{14,6},{16,24},{18,... | collective-permute-start | bytes 3145736 | tf_op jit(solution)/shard_map/ppermute | solution.py:297
  147.2 31.2 %collective-permute-start.8 = (bf16[256,2048]{1,0:T(8,128)(2,1)}, bf16[256,2048]{1,0:T(8,128)(2,1)}, u32[]{:S(2)}, u32[]{:S(2)}) collective-permute-start(bf16[256,2048]{1,0:T(8,128)(2,1)} %param.29), channel_id=1, source_target_pairs={{0,1},{1,0},{2,3},{3,2},{4,5},{5,4},{6,7},{7,6},{8,9},{9,8},{10,11... | collective-permute-start | bytes 3145736 | tf_op jit(solution)/shard_map/ppermute | solution.py:326
  152.8 156.9 %all-gather.8.cloned.1.call-start = ((), (), s32[]{:S(2)}) async-start(), calls=%async_computation.12 | async-start | bytes 7208960 | tf_op jit(solution)/shard_map/all_gather | solution.py:335
  170.2 10.8 %collective-permute-start.10 = (bf16[256,2048]{1,0:T(8,128)(2,1)}, bf16[256,2048]{1,0:T(8,128)(2,1)S(1)}, u32[]{:S(2)}, u32[]{:S(2)}) collective-permute-start(bf16[256,2048]{1,0:T(8,128)(2,1)} %collective-permute-done.9), channel_id=1, source_target_pairs={{0,1},{1,0},{2,3},{3,2},{4,5},{5,4},{6,7},{7,6},{8,9},{9,8},{10,11... | collective-permute-start | bytes 3145736 | tf_op jit(solution)/shard_map/ppermute | solution.py:326
  186.7 4.3 collective-permute-start.15
  189.5 7.0 %collective-permute-start.17 = (bf16[176,2048]{1,0:T(8,128)(2,1)}, bf16[176,2048]{1,0:T(8,128)(2,1)}, u32[]{:S(2)}, u32[]{:S(2)}) collective-permute-start(bf16[176,2048]{1,0:T(8,128)(2,1)} %convert_element_type.233), channel_id=1, source_target_pairs={{8,16},{10,18},{12,20},{14,22},{16,8},{18,10},{20,12},{22,14},{9,1... | collective-permute-start | bytes 2162696 | tf_op jit(solution)/shard_map/ppermute | solution.py:297
  192.3 45.4 %collective-permute-start.16 = (bf16[256,2048]{1,0:T(8,128)(2,1)}, bf16[256,2048]{1,0:T(8,128)(2,1)}, u32[]{:S(2)}, u32[]{:S(2)}) collective-permute-start(bf16[256,2048]{1,0:T(8,128)(2,1)} %fusion.36), channel_id=1, source_target_pairs={{0,8},{2,10},{4,12},{6,14},{8,0},{10,2},{12,4},{14,6},{16,24},{18,... | collective-permute-start | bytes 3145736 | tf_op jit(solution)/shard_map/ppermute | solution.py:297
  195.7 42.1 %collective-permute-start.14 = (bf16[256,2048]{1,0:T(8,128)(2,1)}, bf16[256,2048]{1,0:T(8,128)(2,1)}, u32[]{:S(2)}, u32[]{:S(2)}) collective-permute-start(bf16[256,2048]{1,0:T(8,128)(2,1)} %get-tuple-element.178), channel_id=1, source_target_pairs={{0,1},{1,0},{2,3},{3,2},{4,5},{5,4},{6,7},{7,6},{8,9},{9,8},{10,11... | collective-permute-start | bytes 3145736 | tf_op jit(solution)/shard_map/ppermute | solution.py:326
  195.7 39.3 %collective-permute-start.18 = (bf16[176,2048]{1,0:T(8,128)(2,1)}, bf16[176,2048]{1,0:T(8,128)(2,1)}, u32[]{:S(2)}, u32[]{:S(2)}) collective-permute-start(bf16[176,2048]{1,0:T(8,128)(2,1)} %convert_element_type.233), channel_id=1, source_target_pairs={{0,16},{2,18},{4,20},{6,22},{8,0},{10,2},{12,4},{14,6},{16,24},{18... | collective-permute-start | bytes 2162696 | tf_op jit(solution)/shard_map/ppermute | solution.py:297
  196.5 41.3 %copy-start.25 = (bf16[256,2048]{1,0:T(8,128)(2,1)S(1)}, bf16[256,2048]{1,0:T(8,128)(2,1)}, u32[]{:S(2)}) copy-start(bf16[256,2048]{1,0:T(8,128)(2,1)} %param.28) | copy-start | bytes 3145732
  237.7 204.7 %reduce-scatter.7.cloned.1.call-start = ((), (), s32[]{:S(2)}) async-start(), calls=%async_computation.14 | async-start | bytes 7208960 | tf_op jit(solution)/shard_map/reduce_scatter | solution.py:338
  242.2 24.9 %collective-permute-start.20 = (bf16[256,2048]{1,0:T(8,128)(2,1)S(1)}, bf16[256,2048]{1,0:T(8,128)(2,1)S(1)}, u32[]{:S(2)}, u32[]{:S(2)}) collective-permute-start(bf16[256,2048]{1,0:T(8,128)(2,1)S(1)} %multiply_convert_fusion.6), channel_id=1, source_target_pairs={{0,8},{2,10},{4,12},{6,14},{8,0},{10,2},{12,4},{14,6},{16,24},{18,... | collective-permute-start | bytes 3145736 | tf_op jit(solution)/shard_map/ppermute | solution.py:297
  244.0 23.1 %collective-permute-start.19 = (bf16[256,2048]{1,0:T(8,128)(2,1)S(1)}, bf16[256,2048]{1,0:T(8,128)(2,1)S(1)}, u32[]{:S(2)}, u32[]{:S(2)}) collective-permute-start(bf16[256,2048]{1,0:T(8,128)(2,1)S(1)} %multiply_convert_fusion.6), channel_id=1, source_target_pairs={{0,1},{1,0},{2,3},{3,2},{4,5},{5,4},{6,7},{7,6},{8,9},{9,8},{10,11... | collective-permute-start | bytes 3145736 | tf_op jit(solution)/shard_map/ppermute | solution.py:326
  267.1 2.7 collective-permute-start.21
  309.7 138.1 %reduce-scatter.5.cloned.1.call-start = ((), (), s32[]{:S(2)}) async-start(), calls=%async_computation.13 | async-start | bytes 7864320 | tf_op jit(solution)/shard_map/reduce_scatter | solution.py:338
  335.5 193.4 %reduce-scatter.9.cloned.1.call-start = ((), (), s32[]{:S(2)}) async-start(), calls=%async_computation.15 | async-start | bytes 6553600 | tf_op jit(solution)/shard_map/reduce_scatter | solution.py:338
  359.1 218.3 %reduce-scatter.11.cloned.1.call-start = ((), (), s32[]{:S(2)}) async-start(), calls=%async_computation.16 | async-start | bytes 2621440 | tf_op jit(solution)/shard_map/reduce_scatter | solution.py:338
  369.2 2.7 collective-permute-start.28
  370.6 27.0 %collective-permute-start.27 = (bf16[256,2048]{1,0:T(8,128)(2,1)S(1)}, bf16[256,2048]{1,0:T(8,128)(2,1)S(1)}, u32[]{:S(2)}, u32[]{:S(2)}) collective-permute-start(bf16[256,2048]{1,0:T(8,128)(2,1)S(1)} %get-tuple-element.176), channel_id=1, source_target_pairs={{0,1},{1,0},{2,3},{3,2},{4,5},{5,4},{6,7},{7,6},{8,9},{9,8},{10,11... | collective-permute-start | bytes 3145736 | tf_op jit(solution)/shard_map/ppermute | solution.py:326
  372.3 25.3 %collective-permute-start.29 = (bf16[256,2048]{1,0:T(8,128)(2,1)S(1)}, bf16[256,2048]{1,0:T(8,128)(2,1)S(1)}, u32[]{:S(2)}, u32[]{:S(2)}) collective-permute-start(bf16[256,2048]{1,0:T(8,128)(2,1)S(1)} %fusion.30), channel_id=1, source_target_pairs={{0,8},{2,10},{4,12},{6,14},{8,0},{10,2},{12,4},{14,6},{16,24},{18,... | collective-permute-start | bytes 3145736 | tf_op jit(solution)/shard_map/ppermute | solution.py:297
  402.2 24.7 %collective-permute-start.31 = (bf16[256,2048]{1,0:T(8,128)(2,1)S(1)}, bf16[256,2048]{1,0:T(8,128)(2,1)}, u32[]{:S(2)}, u32[]{:S(2)}) collective-permute-start(bf16[256,2048]{1,0:T(8,128)(2,1)S(1)} %get-tuple-element.164), channel_id=1, source_target_pairs={{0,8},{2,10},{4,12},{6,14},{8,0},{10,2},{12,4},{14,6},{16,24},{18,... | collective-permute-start | bytes 3145736 | tf_op jit(solution)/shard_map/ppermute | solution.py:297
  405.0 22.5 %collective-permute-start.26 = (bf16[256,2048]{1,0:T(8,128)(2,1)}, bf16[256,2048]{1,0:T(8,128)(2,1)}, u32[]{:S(2)}, u32[]{:S(2)}) collective-permute-start(bf16[256,2048]{1,0:T(8,128)(2,1)} %get-tuple-element.175), channel_id=1, source_target_pairs={{0,1},{1,0},{2,3},{3,2},{4,5},{5,4},{6,7},{7,6},{8,9},{9,8},{10,11... | collective-permute-start | bytes 3145736 | tf_op jit(solution)/shard_map/ppermute | solution.py:326
  405.0 25.7 %collective-permute-start.30 = (bf16[256,2048]{1,0:T(8,128)(2,1)S(1)}, bf16[256,2048]{1,0:T(8,128)(2,1)}, u32[]{:S(2)}, u32[]{:S(2)}) collective-permute-start(bf16[256,2048]{1,0:T(8,128)(2,1)S(1)} %get-tuple-element.164), channel_id=1, source_target_pairs={{0,1},{1,0},{2,3},{3,2},{4,5},{5,4},{6,7},{7,6},{8,9},{9,8},{10,11... | collective-permute-start | bytes 3145736 | tf_op jit(solution)/shard_map/ppermute | solution.py:326
  426.9 3.8 collective-permute-start.32
  426.9 62.7 %collective-permute-start.25 = (bf16[256,2048]{1,0:T(8,128)(2,1)}, bf16[256,2048]{1,0:T(8,128)(2,1)}, u32[]{:S(2)}, u32[]{:S(2)}) collective-permute-start(bf16[256,2048]{1,0:T(8,128)(2,1)} %get-tuple-element.174), channel_id=1, source_target_pairs={{0,1},{1,0},{2,3},{3,2},{4,5},{5,4},{6,7},{7,6},{8,9},{9,8},{10,11... | collective-permute-start | bytes 3145736 | tf_op jit(solution)/shard_map/ppermute | solution.py:326
  438.4 41.0 %collective-permute-start.33 = (bf16[256,2048]{1,0:T(8,128)(2,1)}, bf16[256,2048]{1,0:T(8,128)(2,1)}, u32[]{:S(2)}, u32[]{:S(2)}) collective-permute-start(bf16[256,2048]{1,0:T(8,128)(2,1)} %fusion.32), channel_id=1, source_target_pairs={{0,8},{2,10},{4,12},{6,14},{8,0},{10,2},{12,4},{14,6},{16,24},{18,... | collective-permute-start | bytes 3145736 | tf_op jit(solution)/shard_map/ppermute | solution.py:297
  444.7 50.8 %collective-permute-start.34 = (bf16[176,2048]{1,0:T(8,128)(2,1)}, bf16[176,2048]{1,0:T(8,128)(2,1)}, u32[]{:S(2)}, u32[]{:S(2)}) collective-permute-start(bf16[176,2048]{1,0:T(8,128)(2,1)} %get-tuple-element.189), channel_id=1, source_target_pairs={{0,8},{2,10},{4,12},{6,14},{8,24},{10,26},{12,28},{14,30},{16,0},{... | collective-permute-start | bytes 2162696 | tf_op jit(solution)/shard_map/ppermute | solution.py:297
  445.1 50.4 %collective-permute-start.35 = (bf16[176,2048]{1,0:T(8,128)(2,1)S(1)}, bf16[176,2048]{1,0:T(8,128)(2,1)}, u32[]{:S(2)}, u32[]{:S(2)}) collective-permute-start(bf16[176,2048]{1,0:T(8,128)(2,1)S(1)} %get-tuple-element.188), channel_id=1, source_target_pairs={{8,16},{10,18},{12,20},{14,22},{16,8},{18,10},{20,12},{22,14},{9,1... | collective-permute-start | bytes 2162696 | tf_op jit(solution)/shard_map/ppermute | solution.py:297
  479.4 41.3 %all-to-all-start.3 = ((bf16[4,128,1536]{2,1,0:T(8,128)(2,1)}), bf16[4,128,1536]{2,1,0:T(8,128)(2,1)}, u32[]{:S(2)}, u32[]{:S(2)}) async-start(bf16[4,128,1536]{2,1,0:T(8,128)(2,1)} %reduce-scatter.5.cloned.1.call-done), calls=%async_computation.5 | async-start | bytes 3145728 | tf_op jit(solution)/shard_map/all_to_all | solution.py:312
  528.9 8.2 %collective-permute-start.37 = (bf16[256,2048]{1,0:T(8,128)(2,1)S(1)}, bf16[256,2048]{1,0:T(8,128)(2,1)}, u32[]{:S(2)}, u32[]{:S(2)}) collective-permute-start(bf16[256,2048]{1,0:T(8,128)(2,1)S(1)} %get-tuple-element.173), channel_id=1, source_target_pairs={{0,1},{1,0},{2,3},{3,2},{4,5},{5,4},{6,7},{7,6},{8,9},{9,8},{10,11... | collective-permute-start | bytes 3145736 | tf_op jit(solution)/shard_map/ppermute | solution.py:326
  528.9 48.5 %all-to-all-start.4 = ((bf16[4,128,1280]{2,1,0:T(8,128)(2,1)}), bf16[4,128,1280]{2,1,0:T(8,128)(2,1)}, u32[]{:S(2)}, u32[]{:S(2)}) async-start(bf16[4,128,1280]{2,1,0:T(8,128)(2,1)} %reduce-scatter.9.cloned.1.call-done), calls=%async_computation.7 | async-start | bytes 2621440 | tf_op jit(solution)/shard_map/all_to_all | solution.py:312
  533.5 24.4 %collective-permute-start.41 = (bf16[4,128,640]{2,1,0:T(8,128)(2,1)}, bf16[4,128,640]{2,1,0:T(8,128)(2,1)S(1)}, u32[]{:S(2)}, u32[]{:S(2)}) collective-permute-start(bf16[4,128,640]{2,1,0:T(8,128)(2,1)} %get-tuple-element.180), channel_id=1, source_target_pairs={{0,6},{2,4},{4,2},{6,0},{8,14},{10,12},{12,10},{14,8},{16,22},{18,... | collective-permute-start | bytes 1966088 | tf_op jit(solution)/shard_map/ppermute | solution.py:320
  535.9 35.5 %collective-permute-start.40 = (bf16[4,128,640]{2,1,0:T(8,128)(2,1)}, bf16[4,128,640]{2,1,0:T(8,128)(2,1)S(1)}, u32[]{:S(2)}, u32[]{:S(2)}) collective-permute-start(bf16[4,128,640]{2,1,0:T(8,128)(2,1)} %get-tuple-element.181), channel_id=1, source_target_pairs={{0,4},{2,6},{4,0},{6,2},{8,12},{10,14},{12,8},{14,10},{16,20},{18,... | collective-permute-start | bytes 1966088 | tf_op jit(solution)/shard_map/ppermute | solution.py:320
  536.9 35.0 %collective-permute-start.39 = (bf16[4,128,640]{2,1,0:T(8,128)(2,1)}, bf16[4,128,640]{2,1,0:T(8,128)(2,1)S(1)}, u32[]{:S(2)}, u32[]{:S(2)}) collective-permute-start(bf16[4,128,640]{2,1,0:T(8,128)(2,1)} %get-tuple-element.182), channel_id=1, source_target_pairs={{0,2},{2,0},{4,6},{6,4},{8,10},{10,8},{12,14},{14,12},{16,18},{18,... | collective-permute-start | bytes 1966088 | tf_op jit(solution)/shard_map/ppermute | solution.py:320
  537.1 61.7 %collective-permute-start.36 = (bf16[256,2048]{1,0:T(8,128)(2,1)}, bf16[256,2048]{1,0:T(8,128)(2,1)}, u32[]{:S(2)}, u32[]{:S(2)}) collective-permute-start(bf16[256,2048]{1,0:T(8,128)(2,1)} %get-tuple-element.172), channel_id=1, source_target_pairs={{0,1},{1,0},{2,3},{3,2},{4,5},{5,4},{6,7},{7,6},{8,9},{9,8},{10,11... | collective-permute-start | bytes 3145736 | tf_op jit(solution)/shard_map/ppermute | solution.py:326
  540.2 58.5 %collective-permute-start.38 = (bf16[256,2048]{1,0:T(8,128)(2,1)}, bf16[256,2048]{1,0:T(8,128)(2,1)}, u32[]{:S(2)}, u32[]{:S(2)}) collective-permute-start(bf16[256,2048]{1,0:T(8,128)(2,1)} %fusion.28), channel_id=1, source_target_pairs={{0,8},{2,10},{4,12},{6,14},{8,0},{10,2},{12,4},{14,6},{16,24},{18,... | collective-permute-start | bytes 3145736 | tf_op jit(solution)/shard_map/ppermute | solution.py:297
  573.0 20.1 %collective-permute-start.44 = (bf16[128,640]{1,0:T(8,128)(2,1)}, bf16[128,640]{1,0:T(8,128)(2,1)S(1)}, u32[]{:S(2)}, u32[]{:S(2)}) collective-permute-start(bf16[128,640]{1,0:T(8,128)(2,1)} %get-tuple-element.190), channel_id=1, source_target_pairs={{0,24},{2,26},{4,28},{6,30},{8,16},{10,18},{12,20},{14,22},{16,8},... | collective-permute-start | bytes 491528 | tf_op jit(solution)/shard_map/ppermute | solution.py:297
  576.4 17.8 %collective-permute-start.43 = (bf16[128,640]{1,0:T(8,128)(2,1)}, bf16[128,640]{1,0:T(8,128)(2,1)S(1)}, u32[]{:S(2)}, u32[]{:S(2)}) collective-permute-start(bf16[128,640]{1,0:T(8,128)(2,1)} %get-tuple-element.191), channel_id=1, source_target_pairs={{0,8},{2,10},{4,12},{6,14},{8,0},{10,2},{12,4},{14,6},{16,24},{18,... | collective-permute-start | bytes 491528 | tf_op jit(solution)/shard_map/ppermute | solution.py:297
  576.4 19.4 %collective-permute-start.42 = (bf16[128,640]{1,0:T(8,128)(2,1)}, bf16[128,640]{1,0:T(8,128)(2,1)S(1)}, u32[]{:S(2)}, u32[]{:S(2)}) collective-permute-start(bf16[128,640]{1,0:T(8,128)(2,1)} %get-tuple-element.192), channel_id=1, source_target_pairs={{0,16},{2,18},{4,20},{6,22},{8,24},{10,26},{12,28},{14,30},{16,0},... | collective-permute-start | bytes 491528 | tf_op jit(solution)/shard_map/ppermute | solution.py:297
  593.2 25.1 %collective-permute-start.45 = (bf16[64,2048]{1,0:T(8,128)(2,1)}, bf16[64,2048]{1,0:T(8,128)(2,1)S(1)}, u32[]{:S(2)}, u32[]{:S(2)}) collective-permute-start(bf16[64,2048]{1,0:T(8,128)(2,1)} %get-tuple-element.198), channel_id=1, source_target_pairs={{0,8},{2,10},{4,12},{6,14},{8,24},{10,26},{12,28},{14,30},{16,0},{... | collective-permute-start | bytes 786440 | tf_op jit(solution)/shard_map/ppermute | solution.py:297
  594.3 24.0 %collective-permute-start.46 = (bf16[64,2048]{1,0:T(8,128)(2,1)}, bf16[64,2048]{1,0:T(8,128)(2,1)}, u32[]{:S(2)}, u32[]{:S(2)}) collective-permute-start(bf16[64,2048]{1,0:T(8,128)(2,1)} %get-tuple-element.199), channel_id=1, source_target_pairs={{8,16},{10,18},{12,20},{14,22},{16,8},{18,10},{20,12},{22,14},{9,1... | collective-permute-start | bytes 786440 | tf_op jit(solution)/shard_map/ppermute | solution.py:297
  603.0 13.3 %all-to-all-start.5 = ((f32[32,1,128]{2,1,0:T(1,128)}), f32[32,1,128]{2,1,0:T(1,128)S(1)}, u32[]{:S(2)}, u32[]{:S(2)}) async-start(f32[32,1,128]{2,1,0:T(1,128)} %reshape.724), calls=%async_computation.9 | async-start | bytes 32768 | tf_op jit(solution)/shard_map/all_to_all | solution.py:705
  (103 other events, 831.0 us)
Sparse Core Ops, SparseCore 0:
  50.3 87.2 all-gather.3
  152.9 71.5 all-gather.5
  237.8 65.0 all-gather.7
  309.8 64.8 reduce-scatter.6
  377.6 70.1 reduce-scatter.4
  450.6 61.4 reduce-scatter.8
  515.6 48.6 reduce-scatter.10
